TPU v7x, 128 devices: a whole 4x4x4 slice. The times are simulated.
128 devices in a mesh: dp: 16 (over z_lo, y, core), col: 8 (over x, z_hi).
Axes of the slice: x: 4, y: 4, z: 4 (z_hi: 2, z_lo: 2; z = z_hi * 2 + z_lo), core: 2. Of those that a mesh axis runs over, the one named last changes fastest.
Arguments:
- image_emb: bfloat16 [8192, 1024], P(('dp', 'col')), may hold values from -4 to 4
- text_emb: bfloat16 [8192, 1024], P(('col', 'dp')), may hold values from -4 to 4
- pairs: int32 [8192], P('dp'), may hold values from 0 to 8191, as said below
- logit_scale: float32 [1], replicated, may hold values from 10 to 400
- tokens: bfloat16 [128, 257, 1408], P(('dp', 'col')), may hold values from -6 to 6
- norm_gain: float32 [1408], replicated, may hold values from 0.1 to 1.9
- w_in: bfloat16 [1408, 6144], P('dp', 'col'), may hold values from -0.15625 to 0.15625
- w_out: bfloat16 [6144, 1408], P('col', 'dp'), may hold values from -0.078125 to 0.078125
- proj: bfloat16 [1408, 1024], P('dp'), may hold values from -0.15625 to 0.15625
Outputs:
- image_grad: float32 [8192, 1024], P(('dp', 'col'))
- text_grad: float32 [8192, 1024], P(('col', 'dp'))
- grad_w_in: float32 [1408, 6144], P('dp', 'col')
- grad_w_out: float32 [6144, 1408], P('col', 'dp')
- grad_proj: float32 [1408, 1024], P('dp')
Inputs may be any that keep to these rules, and one draw needn't show every extreme that they name: `pairs`: a permutation of 0 to 8191.
All inputs are finite; a program needn't handle non-finite values.
Results may differ from a plain program's by a relative error of at most 0.0075.
The roundings to bfloat16 on the way count: a program that leaves them out, or rounds other values in their place, can miss the bound.
Values may be sent and summed in bfloat16 or wider, within the bound.
No kernel may reach another device: no remote copies, remote signals or barrier semaphores. Data moves between devices by JAX's collectives and lax.ppermute only.
A program may use at most 128 MiB of HBM per device.

v0:
```python
import jax
import jax.numpy as jnp
from jax import lax
from jax.sharding import PartitionSpec as P

epsilon = 1e-06
inv_root_two_pi = 0.3989422804014327


def unit_rows(raw):
    values = raw.astype(jnp.float32)
    inverse = lax.rsqrt(jnp.sum(values * values, axis=1, keepdims=True) + epsilon)
    return (values * inverse, inverse)


def gelu_slope(pre_act):
    return (
        0.5 * (1.0 + jax.scipy.special.erf(pre_act * 0.7071067811865476))
        + pre_act * jnp.exp(-0.5 * pre_act * pre_act) * inv_root_two_pi
    )


def contract_rows(left, right):
    return lax.dot_general(
        left, right, (((0,), (0,)), ((), ())), preferred_element_type=jnp.float32
    )


def contract_cols(left, right):
    return lax.dot_general(
        left, right, (((1,), (1,)), ((), ())), preferred_element_type=jnp.float32
    )


def on_device(image_emb, text_emb, pairs, logit_scale, tokens, norm_gain, w_in, w_out, proj):
    img_unit, img_inv = unit_rows(image_emb)
    txt_unit, txt_inv = unit_rows(text_emb)
    all_img = lax.all_gather(img_unit.astype(jnp.bfloat16), "col", axis=0, tiled=True)
    all_txt = lax.all_gather(txt_unit.astype(jnp.bfloat16), "dp", axis=0, tiled=True)
    temper = logit_scale[0]
    logits = temper * contract_cols(all_img, all_txt)
    txt_count = all_txt.shape[0]
    col_base = lax.axis_index("col") * txt_count
    matches = (pairs[:, None] == col_base + jnp.arange(txt_count, dtype=jnp.int32)[None, :]).astype(
        jnp.float32
    )
    row_top = jnp.max(logits, axis=1)
    row_mass = jnp.sum(jnp.exp(logits - row_top[:, None]), axis=1)
    col_top = jnp.max(logits, axis=0)
    col_mass = jnp.sum(jnp.exp(logits - col_top[None, :]), axis=0)
    row_peak = lax.pmax(row_top, "col")
    row_total = lax.psum(row_mass * jnp.exp(row_top - row_peak), "col")
    col_peak = lax.pmax(col_top, "dp")
    col_total = lax.psum(col_mass * jnp.exp(col_top - col_peak), "dp")
    row_lse = row_peak + jnp.log(row_total)
    col_lse = col_peak + jnp.log(col_total)
    dlogit = (
        0.5 * (jnp.exp(logits - row_lse[:, None]) + jnp.exp(logits - col_lse[None, :])) - matches
    ).astype(jnp.bfloat16)
    img_dir = temper * lax.psum_scatter(
        jnp.dot(dlogit, all_txt, preferred_element_type=jnp.float32),
        "col",
        scatter_dimension=0,
        tiled=True,
    )
    txt_dir = temper * lax.psum_scatter(
        contract_rows(dlogit, all_img), "dp", scatter_dimension=0, tiled=True
    )
    image_grad = img_inv * (img_dir - img_unit * jnp.sum(img_unit * img_dir, axis=1, keepdims=True))
    text_grad = txt_inv * (txt_dir - txt_unit * jnp.sum(txt_unit * txt_dir, axis=1, keepdims=True))
    gathered = lax.all_gather(tokens, "col", axis=0, tiled=True)
    own_count, seq_len, width = tokens.shape
    img_count = gathered.shape[0]
    floats = gathered.astype(jnp.float32)
    center = jnp.mean(floats, axis=2, keepdims=True)
    spread = jnp.mean(jnp.square(floats - center), axis=2, keepdims=True)
    normed = (
        ((floats - center) * lax.rsqrt(spread + epsilon) * norm_gain)
        .astype(jnp.bfloat16)
        .reshape(img_count * seq_len, width)
    )
    hidden_cols = w_in.shape[1]
    piece_in = lax.all_gather(w_in, "dp", axis=0, tiled=True)
    piece_proj = lax.all_gather(proj, "dp", axis=0, tiled=True)
    acc_in = jnp.dot(normed, piece_in, preferred_element_type=jnp.float32)
    proj_full = piece_proj
    pre_act, proj_full = (acc_in, proj_full)
    act_mean = jnp.mean(
        jax.nn.gelu(pre_act, approximate=False).reshape(img_count, seq_len, hidden_cols), axis=1
    ).astype(jnp.bfloat16)
    out_full = lax.all_gather(w_out, "dp", axis=1, tiled=True)
    own_slot = lax.axis_index("col") * own_count
    token_mean = jnp.mean(tokens.astype(jnp.float32), axis=1)
    pool_part = jnp.dot(
        act_mean, out_full, preferred_element_type=jnp.float32
    ) + lax.dynamic_update_slice_in_dim(
        jnp.zeros((img_count, width), jnp.float32), token_mean, own_slot, 0
    )
    grad_part = lax.dynamic_update_slice_in_dim(
        jnp.zeros((img_count, image_grad.shape[1]), jnp.float32),
        image_grad[:own_count],
        own_slot,
        0,
    )
    pooled, cached = lax.psum((pool_part, grad_part), "col")
    pool_low = pooled.astype(jnp.bfloat16)
    grad_low = cached.astype(jnp.bfloat16)
    dpool_low = contract_cols(grad_low, proj_full).astype(jnp.bfloat16)
    act_grad = contract_cols(dpool_low, out_full) / seq_len
    pre_grad = (
        (gelu_slope(pre_act).reshape(img_count, seq_len, hidden_cols) * act_grad[:, None, :])
        .astype(jnp.bfloat16)
        .reshape(img_count * seq_len, hidden_cols)
    )
    in_term = contract_rows(normed, pre_grad)
    out_term = contract_rows(dpool_low, act_mean)
    proj_term = contract_rows(pool_low, grad_low)
    stacked = lax.psum_scatter(
        jnp.concatenate((in_term, out_term, proj_term), axis=1),
        "dp",
        scatter_dimension=0,
        tiled=True,
    )
    grad_w_in = stacked[:, :hidden_cols]
    grad_w_out = stacked[:, hidden_cols : 2 * hidden_cols].T
    grad_proj = stacked[:, 2 * hidden_cols :]
    return (image_grad, text_grad, grad_w_in, grad_w_out, grad_proj)


def solution(mesh):
    in_specs = (
        P(("dp", "col"), None),
        P(("col", "dp"), None),
        P("dp"),
        P(),
        P(("dp", "col"), None, None),
        P(),
        P("dp", "col"),
        P("col", "dp"),
        P("dp", None),
    )
    out_specs = (
        P(("dp", "col"), None),
        P(("col", "dp"), None),
        P("dp", "col"),
        P("col", "dp"),
        P("dp", None),
    )
    return jax.shard_map(
        on_device, mesh=mesh, in_specs=in_specs, out_specs=out_specs, check_vma=False
    )
```

profile of v0, /device:TPU:8, one launch (start us, length us, event | category | flops | bytes accessed | tf_op | source)
XLA Modules:
  0.0 634.4 jit_solution(15778677272781189664)
XLA Ops:
  7.2 1.0 fusion.28
  8.3 1.7 fusion.24
  10.0 1.0 fusion.32
  11.0 1.7 fusion.21
  13.4 47.2 %all-gather.7.cloned.1.call-done = bf16[512,1024]{1,0:T(8,128)(2,1)} async-done(((bf16[64,1024]{1,0:T(8,128)(2,1)}), bf16[512,1024]{1,0:T(8,128)(2,1)}) %all-gather.7.cloned.1.call-update) | async-done | bytes 1048592 | tf_op jit(solution)/shard_map/all_gather | solution.py:38
  60.6 34.8 %all-gather.9.cloned.1.call-done = bf16[1024,1024]{1,0:T(8,128)(2,1)} async-done(((bf16[64,1024]{1,0:T(8,128)(2,1)}), bf16[1024,1024]{1,0:T(8,128)(2,1)}) %all-gather.9.cloned.1.call-update) | async-done | bytes 2097168 | tf_op jit(solution)/shard_map/all_gather | solution.py:39
  95.4 3.3 fusion.43
  98.7 25.3 %pmax.15 = f32[1024]{0:T(1024)S(1)} all-reduce(f32[1024]{0:T(1024)S(1)} %get-tuple-element.23), channel_id=1, replica_groups=mesh['dp'=16,'col'=8] {'dp'}, use_global_device_ids=true, to_apply=%region_7.0 | all-reduce | flops 1024 | bytes 8192 | tf_op jit(solution)/shard_map/pmax | solution.py:53
  123.9 24.1 %pmax.14 = f32[512]{0:T(512)S(1)} all-reduce(f32[512]{0:T(512)S(1)} %get-tuple-element.22), channel_id=1, replica_groups=mesh['dp'=16,'col'=8] {'col'}, use_global_device_ids=true, to_apply=%region_3.0 | all-reduce | flops 512 | bytes 4096 | tf_op jit(solution)/shard_map/pmax | solution.py:51
  148.0 0.7 exponential_reduce_fusion.1
  148.8 27.1 %psum.29 = f32[1024]{0:T(1024)S(1)} all-reduce(f32[1024]{0:T(1024)S(1)} %exponential_multiply_fusion), channel_id=1, replica_groups=mesh['dp'=16,'col'=8] {'dp'}, use_global_device_ids=true, to_apply=%region_9.0 | all-reduce | flops 1024 | bytes 8192 | tf_op jit(solution)/shard_map/psum | solution.py:54
  175.9 19.0 %psum.28 = f32[512]{0:T(512)S(1)} all-reduce(f32[512]{0:T(512)S(1)} %exponential_multiply_fusion.1), channel_id=1, replica_groups=mesh['dp'=16,'col'=8] {'col'}, use_global_device_ids=true, to_apply=%region_5.0 | all-reduce | flops 512 | bytes 4096 | tf_op jit(solution)/shard_map/psum | solution.py:52
  194.9 4.6 fusion.42
  199.6 0.5 all-gather.11.cloned.1.call-update
  200.2 0.5 all-gather.13.cloned.1.call-update
  201.3 0.7 all-gather.15.cloned.1.call-update
  202.2 5.0 fusion.41
  207.3 68.5 %reduce-scatter.6.cloned.1.call-done = f32[64,1024]{1,0:T(8,128)} async-done(((f32[512,1024]{1,0:T(8,128)}), f32[64,1024]{1,0:T(8,128)}) %reduce-scatter.6.cloned.1.call-update) | async-done | bytes 262160 | tf_op jit(solution)/shard_map/reduce_scatter | solution.py:60
  275.7 1.2 fusion.25
  276.9 1.1 fusion.27
  278.3 84.9 %all-gather.11.cloned.1.call-done = bf16[8,257,1408]{2,1,0:T(8,128)(2,1)} async-done(((bf16[1,257,1408]{2,1,0:T(8,128)(2,1)}), bf16[8,257,1408]{2,1,0:T(8,128)(2,1)}) %all-gather.11.cloned.1.call-update) | async-done | bytes 5789712 | tf_op jit(solution)/shard_map/all_gather | solution.py:71
  363.2 3.7 convert_reduce_fusion
  367.0 0.7 copy-done
  367.7 1.7 fusion.2
  369.4 4.0 fusion.4
  373.4 6.9 %reshape.69 = bf16[2056,1408]{1,0:T(8,128)(2,1)} reshape(bf16[8,257,1408]{2,1,0:T(8,128)(2,1)} %fusion.4) | data formatting | bytes 11579392 | tf_op jit(solution)/shard_map/reshape | solution.py:80
  380.3 16.3 %all-gather.13.cloned.1.call-done = bf16[1408,768]{1,0:T(8,128)(2,1)} async-done(((bf16[88,768]{1,0:T(8,128)(2,1)}), bf16[1408,768]{1,0:T(8,128)(2,1)}) %all-gather.13.cloned.1.call-update) | async-done | bytes 2162704 | tf_op jit(solution)/shard_map/all_gather | solution.py:83
  396.6 23.7 %fusion.8 = (f32[2056,768]{1,0:T(8,128)}, f32[2056,768]{1,0:T(8,128)}) fusion(bf16[2056,1408]{1,0:T(8,128)(2,1)} %reshape.69, bf16[1408,768]{1,0:T(8,128)(2,1)} %all-gather.13.cloned.1.call-done), kind=kOutput, calls=%fused_computation.14 | convolution fusion | flops 4560175104 | bytes 20584448 | tf_op jit(solution)/shard_map/dot_general | solution.py:85
  420.3 6.3 reshape.71
  426.6 3.3 reduce_sum.98
  429.9 2.6 all-gather.17.cloned.1.call-done
  432.4 2.3 fusion.37
  434.9 6.5 %reshape.70 = f32[8,257,768]{2,1,0:T(8,128)} reshape(f32[2056,768]{1,0:T(8,128)} %get-tuple-element.26) | data formatting | bytes 12632064 | tf_op jit(solution)/shard_map/reshape | solution.py:111
  441.4 42.5 %all-reduce = (bf16[8,1408]{1,0:T(8,128)(2,1)S(1)}, bf16[8,1024]{1,0:T(8,128)(2,1)S(1)}) all-reduce(f32[8,1408]{1,0:T(8,128)S(1)} %add.87, f32[8,1024]{1,0:T(8,128)S(1)} %dynamic_update_slice.6), channel_id=1, replica_groups=mesh['dp'=16,'col'=8] {'col'}, use_global_device_ids=true, to_apply=%region_19.0 | all-reduce | flops 19456 | bytes 116736 | tf_op jit(solution)/shard_map/psum | solution.py:105
  483.9 2.8 convolution_convert_fusion
  487.1 0.8 fusion.38
  487.9 1.0 fusion.44
  489.4 0.7 slice-done.1
  490.1 0.7 slice-done.3
  490.8 6.3 convolution_bitcast_fusion
  497.1 6.0 pad_maximum_fusion
  503.1 15.0 %copy.23 = f32[1408,2560]{1,0:T(8,128)} copy(f32[1408,2560]{0,1:T(8,128)} %pad_maximum_fusion) | data formatting | bytes 28835840
  518.1 17.7 %reduce-scatter.8.cloned.1.call-done = f32[64,1024]{1,0:T(8,128)} async-done(((f32[1024,1024]{1,0:T(8,128)}), f32[64,1024]{1,0:T(8,128)}) %reduce-scatter.8.cloned.1.call-update) | async-done | bytes 262160 | tf_op jit(solution)/shard_map/reduce_scatter | solution.py:66
  535.9 1.2 fusion.29
  537.0 1.8 fusion.31
  538.8 85.5 %reduce-scatter.10.cloned.1.call-done = f32[88,2560]{1,0:T(8,128)} async-done(((f32[1408,2560]{1,0:T(8,128)}), f32[88,2560]{1,0:T(8,128)}) %reduce-scatter.10.cloned.1.call-update) | async-done | bytes 901136
  624.3 1.9 slice_bitcast_fusion
  626.1 1.7 slice.19
  (56 shorter events, 2.6 us)
Async XLA Ops:
  7.2 53.4 %all-gather.7.cloned.1.call-start = ((), (), s32[]{:S(2)}) async-start(), calls=%async_computation.3 | async-start | bytes 1179648 | tf_op jit(solution)/shard_map/all_gather | solution.py:38
  9.9 85.4 %all-gather.9.cloned.1.call-start = ((), (), s32[]{:S(2)}) async-start(), calls=%async_computation.4 | async-start | bytes 2228224 | tf_op jit(solution)/shard_map/all_gather | solution.py:39
  12.7 182.2 %copy-start.7 = (s32[512]{0:T(512)S(1)}, s32[512]{0:T(512)}, u32[]{:S(2)}) copy-start(s32[512]{0:T(512)} %param.11) | copy-start | bytes 6148
  12.7 263.0 %reduce-scatter.6.cloned.1.call-start = ((), (), s32[]{:S(2)}) async-start(), calls=%async_computation.5 | async-start | bytes 2359296 | tf_op jit(solution)/shard_map/reduce_scatter | solution.py:60
  194.9 7.2 %copy-start.2 = (bf16[1,257,1408]{2,1,0:T(8,128)(2,1)S(1)}, bf16[1,257,1408]{2,1,0:T(8,128)(2,1)}, u32[]{:S(2)}) copy-start(bf16[1,257,1408]{2,1,0:T(8,128)(2,1)} %param.13) | copy-start | bytes 2171140
  199.5 163.7 %all-gather.11.cloned.1.call-start = ((), (), s32[]{:S(2)}) async-start(), calls=%async_computation.7 | async-start | bytes 6690816 | tf_op jit(solution)/shard_map/all_gather | solution.py:71
  200.1 196.5 %all-gather.13.cloned.1.call-start = ((), (), s32[]{:S(2)}) async-start(), calls=%async_computation.8 | async-start | bytes 2297856 | tf_op jit(solution)/shard_map/all_gather | solution.py:83
  200.7 231.7 %all-gather.17.cloned.1.call-start = ((), (), s32[]{:S(2)}) async-start(), calls=%async_computation.10 | async-start | bytes 2297856 | tf_op jit(solution)/shard_map/all_gather | solution.py:91
  201.3 282.6 %all-gather.15.cloned.1.call-start = ((), (), s32[]{:S(2)}) async-start(), calls=%async_computation.9 | async-start | bytes 3063808 | tf_op jit(solution)/shard_map/all_gather | solution.py:84
  202.0 333.8 %reduce-scatter.8.cloned.1.call-start = ((), (), s32[]{:S(2)}) async-start(), calls=%async_computation.6 | async-start | bytes 4456448 | tf_op jit(solution)/shard_map/reduce_scatter | solution.py:66
  202.2 73.5 %copy-start.3 = (bf16[64,1024]{1,0:T(8,128)(2,1)S(1)}, bf16[64,1024]{1,0:T(8,128)(2,1)}, u32[]{:S(2)}) copy-start(bf16[64,1024]{1,0:T(8,128)(2,1)} %param.9) | copy-start | bytes 393220
  207.2 417.0 %reduce-scatter.10.cloned.1.call-start = ((), (), s32[]{:S(2)}) async-start(), calls=%async_computation.11 | async-start | bytes 15319040
  276.9 92.5 %copy-start.6 = (f32[1408]{0:T(1024)S(1)}, f32[1408]{0:T(1024)}, u32[]{:S(2)}) copy-start(f32[1408]{0:T(1024)} %param.14) | copy-start | bytes 16900
  278.0 95.4 %copy-start.5 = (f32[64,1024]{1,0:T(8,128)}, f32[64,1024]{1,0:T(8,128)S(1)}, u32[]{:S(2)}) copy-start(f32[64,1024]{1,0:T(8,128)S(1)} %fusion.27) | copy-start | bytes 786436
  363.2 4.4 copy-start
  434.9 51.8 %copy-start.1 = (bf16[768,1408]{0,1:T(8,128)(2,1)S(1)}, bf16[768,1408]{0,1:T(8,128)(2,1)}, u32[]{:S(2)}) copy-start(bf16[768,1408]{0,1:T(8,128)(2,1)} %all-gather.17.cloned.1.call-done) | copy-start | bytes 6488068
  483.9 5.0 slice-start.2
  487.1 2.3 slice-start
  487.9 2.2 slice-start.1
  487.9 2.9 slice-start.3
  518.1 17.7 %copy-start.4 = (bf16[64,1024]{1,0:T(8,128)(2,1)S(1)}, bf16[64,1024]{1,0:T(8,128)(2,1)}, u32[]{:S(2)}) copy-start(bf16[64,1024]{1,0:T(8,128)(2,1)} %param.10) | copy-start | bytes 393220
Sparse Core Ops, SparseCore 0:
  10.9 49.6 all-gather.6
  62.9 32.4 all-gather.8
  199.7 76.0 reduce-scatter.5
  278.3 84.9 all-gather.10
  364.9 31.6 all-gather.12
  398.3 34.1 all-gather.16
  434.3 35.7 all-gather.14
  472.6 63.2 reduce-scatter.7
  538.4 85.7 reduce-scatter.9
where the time goes:
time: 639 us; the launch traced here: 634 us
  waiting for transfers between devices  360 us (56%)
  blocking collectives  138 us (22%)
  matrix products  50 us (8%)
  local copies, waits for them, and re-layouts  41.4 us (6%)
  other arithmetic  30.3 us (5%)
  between operations  14.7 us (2%)
    unnamed x10, waiting for transfers between devices  87.8 us
    all_gather x1, waiting for transfers between devices, on_device(): gathered = lax.all_gather(tokens, 'col', axis=0, tiled=True)  84.9 us
    reduce_scatter x1, waiting for transfers between devices, on_device(): lax.psum_scatter(jnp.dot(dlogit, all_txt, preferred_element_type=jnp.floa...  68.5 us
    all_gather x1, waiting for transfers between devices, on_device(): lax.all_gather(img_unit.astype(jnp.bfloat16), 'col', axis=0, tiled=True)  47.2 us
    psum x1, blocking collectives, on_device(): pooled, cached = lax.psum((pool_part, grad_part), 'col')  42.5 us
    all_gather x1, waiting for transfers between devices, on_device(): lax.all_gather(txt_unit.astype(jnp.bfloat16), 'dp', axis=0, tiled=True)  34.8 us
    psum x1, blocking collectives, on_device(): col_total = lax.psum(col_mass * jnp.exp(col_top - col_peak), 'dp')  27.1 us
    pmax x1, blocking collectives, on_device(): col_peak = lax.pmax(col_top, 'dp')  25.3 us
  transfers between devices with their start and end apart: 9, of which 8 were waited for; matrix products, arithmetic and copies ran while one was open for 16% of the time, Pallas kernels for 0%

commit v1 on v0

v1 whole, which is shorter than its diff:
```python
import functools

import jax
import jax.numpy as jnp
from jax import lax
from jax.experimental import pallas as pl
from jax.experimental.pallas import tpu as pltpu
from jax.sharding import PartitionSpec as P

epsilon = 1e-06
inv_root_two_pi = 0.3989422804014327
root_half = 0.7071067811865476
bf16 = jnp.bfloat16
f32 = jnp.float32


def unit_rows(raw):
    values = raw.astype(f32)
    inverse = lax.rsqrt(jnp.sum(values * values, axis=-1, keepdims=True) + epsilon)
    return (values * inverse, inverse)


def contract_rows(left, right):
    return lax.dot_general(left, right, (((0,), (0,)), ((), ())), preferred_element_type=f32)


def contract_cols(left, right):
    return lax.dot_general(left, right, (((1,), (1,)), ((), ())), preferred_element_type=f32)


def share(piece, axis):
    count = lax.axis_size(axis)
    return lax.all_to_all(
        jnp.broadcast_to(piece[None], (count,) + piece.shape), axis, 0, 0, tiled=True
    )


def forward_kernel(tok_ref, gain_ref, win_ref, normed_ref, slope_ref, act_ref, mean_ref):
    floats = tok_ref[0].astype(f32)
    seq = floats.shape[0]
    center = jnp.mean(floats, axis=1, keepdims=True)
    shifted = floats - center
    spread = jnp.mean(shifted * shifted, axis=1, keepdims=True)
    normed = (shifted * lax.rsqrt(spread + epsilon) * gain_ref[...]).astype(bf16)
    normed_ref[0] = normed
    mean_ref[0] = jnp.sum(floats, axis=0, keepdims=True) * (1.0 / seq)
    pre = jnp.dot(normed, win_ref[...], preferred_element_type=f32)
    half = 0.5 * (1.0 + lax.erf(pre * root_half))
    act_ref[0] = jnp.sum(pre * half, axis=0, keepdims=True) * (1.0 / seq)
    slope_ref[0] = half + pre * jnp.exp(-0.5 * pre * pre) * inv_root_two_pi


def encode(tokens, gain, weights, hidden):
    images, seq, width = tokens.shape
    return pl.pallas_call(
        forward_kernel,
        grid=(images,),
        in_specs=[
            pl.BlockSpec((1, seq, width), lambda i: (i, 0, 0)),
            pl.BlockSpec((1, width), lambda i: (0, 0)),
            pl.BlockSpec((width, hidden), lambda i: (0, 0)),
        ],
        out_specs=[
            pl.BlockSpec((1, seq, width), lambda i: (i, 0, 0)),
            pl.BlockSpec((1, seq, hidden), lambda i: (i, 0, 0)),
            pl.BlockSpec((1, 1, hidden), lambda i: (i, 0, 0)),
            pl.BlockSpec((1, 1, width), lambda i: (i, 0, 0)),
        ],
        out_shape=[
            jax.ShapeDtypeStruct((images, seq, width), bf16),
            jax.ShapeDtypeStruct((images, seq, hidden), f32),
            jax.ShapeDtypeStruct((images, 1, hidden), f32),
            jax.ShapeDtypeStruct((images, 1, width), f32),
        ],
        compiler_params=pltpu.CompilerParams(vmem_limit_bytes=48 * 2**20),
        cost_estimate=pl.CostEstimate(
            flops=2 * images * seq * width * hidden,
            bytes_accessed=images * seq * (4 * width + 4 * hidden),
            transcendentals=images * seq * hidden * 2,
        ),
        name="encode",
    )(tokens, gain, weights)


def backward_kernel(core_ref, normed_ref, slope_ref, grad_ref, keep_ref, send_ref, total):
    step = pl.program_id(0)
    pre_grad = (slope_ref[0] * grad_ref[0]).astype(bf16)
    term = contract_rows(normed_ref[0], pre_grad)

    @pl.when(step == 0)
    def _():
        total[...] = term

    @pl.when(step > 0)
    def _():
        total[...] += term

    @pl.when(step == pl.num_programs(0) - 1)
    def _():
        core = core_ref[0]
        pairs, rows, _ = keep_ref.shape
        for pair in range(pairs):
            mine = pl.multiple_of((2 * pair + core) * rows, 8)
            other = pl.multiple_of((2 * pair + 1 - core) * rows, 8)
            keep_ref[pair] = total[pl.ds(mine, rows), :]
            send_ref[pair] = total[pl.ds(other, rows), :].astype(bf16)


def weigh(core, normed, slope, act_grad, rows):
    images, seq, width = normed.shape
    hidden = slope.shape[2]
    pairs = width // rows // 2
    return pl.pallas_call(
        backward_kernel,
        grid=(images,),
        in_specs=[
            pl.BlockSpec(memory_space=pltpu.SMEM),
            pl.BlockSpec((1, seq, width), lambda i: (i, 0, 0)),
            pl.BlockSpec((1, seq, hidden), lambda i: (i, 0, 0)),
            pl.BlockSpec((1, 1, hidden), lambda i: (i, 0, 0)),
        ],
        out_specs=[
            pl.BlockSpec((pairs, rows, hidden), lambda i: (0, 0, 0)),
            pl.BlockSpec((pairs, rows, hidden), lambda i: (0, 0, 0)),
        ],
        out_shape=[
            jax.ShapeDtypeStruct((pairs, rows, hidden), f32),
            jax.ShapeDtypeStruct((pairs, rows, hidden), bf16),
        ],
        scratch_shapes=[pltpu.VMEM((width, hidden), f32)],
        compiler_params=pltpu.CompilerParams(vmem_limit_bytes=48 * 2**20),
        cost_estimate=pl.CostEstimate(
            flops=2 * images * seq * width * hidden,
            bytes_accessed=images * seq * (2 * width + 4 * hidden),
            transcendentals=0,
        ),
        name="weigh",
    )(core, normed, slope, act_grad)


def project(partial, unit):
    return partial - unit * jnp.sum(unit * partial, axis=1, keepdims=True)


def on_device(image_emb, text_emb, pairs, logit_scale, tokens, norm_gain, w_in, w_out, proj):
    dp_size = lax.axis_size("dp")
    hidden = w_in.shape[1]
    rows_d = w_in.shape[0]
    _, seq, width = tokens.shape
    temper = logit_scale[0]

    all_img = share(image_emb, "col")
    all_txt = share(text_emb, "dp")
    all_tok = share(tokens[0], "col")
    weights = lax.all_gather(
        jnp.concatenate((w_in, w_out.T, proj), axis=1), "dp", axis=0, tiled=True
    )

    own_rows = image_emb.shape[0]
    groups = all_img.shape[0]
    img_unit, img_inv = unit_rows(all_img.reshape(-1, image_emb.shape[1]))
    txt_unit, txt_inv = unit_rows(all_txt.reshape(-1, image_emb.shape[1]))
    img_low = img_unit.astype(bf16)
    txt_low = txt_unit.astype(bf16)
    logits = temper * contract_cols(img_low, txt_low)
    txt_count = txt_low.shape[0]
    col_base = lax.axis_index("col") * txt_count
    matches = (
        pairs[:, None] == col_base + jnp.arange(txt_count, dtype=jnp.int32)[None, :]
    ).astype(f32)
    row_top = jnp.max(logits, axis=1)
    row_mass = jnp.sum(jnp.exp(logits - row_top[:, None]), axis=1)
    col_top = jnp.max(logits, axis=0)
    col_mass = jnp.sum(jnp.exp(logits - col_top[None, :]), axis=0)
    row_stats = share(jnp.stack((row_top, row_mass)), "col")
    col_stats = share(jnp.stack((col_top, col_mass)), "dp")

    def lse(stats):
        peak = jnp.max(stats[:, 0], axis=0)
        return peak + jnp.log(jnp.sum(stats[:, 1] * jnp.exp(stats[:, 0] - peak), axis=0))

    row_lse = lse(row_stats)
    col_lse = lse(col_stats)
    dlogit = (
        0.5 * (jnp.exp(logits - row_lse[:, None]) + jnp.exp(logits - col_lse[None, :])) - matches
    ).astype(bf16)

    cached_part = jnp.dot(
        dlogit.reshape(groups, own_rows, txt_count)[:, 0], txt_low, preferred_element_type=f32
    )
    cached_dir = temper * jnp.sum(share(cached_part, "col"), axis=0)
    cached_unit, cached_inv = unit_rows(all_img[:, 0])
    grad_low = (cached_inv * project(cached_dir, cached_unit)).astype(bf16)

    img_part = project(jnp.dot(dlogit, txt_low, preferred_element_type=f32), img_unit)
    img_sum = lax.all_to_all(
        img_part.astype(bf16).reshape(groups, own_rows, -1), "col", 0, 0, tiled=True
    )
    txt_part = project(contract_rows(dlogit, img_low), txt_unit)
    txt_sum = lax.all_to_all(
        txt_part.astype(bf16).reshape(dp_size, own_rows, -1), "dp", 0, 0, tiled=True
    )
    _, own_img_inv = unit_rows(image_emb)
    _, own_txt_inv = unit_rows(text_emb)
    image_grad = own_img_inv * temper * jnp.sum(img_sum.astype(f32), axis=0)
    text_grad = own_txt_inv * temper * jnp.sum(txt_sum.astype(f32), axis=0)

    normed, slope, act_mean, token_mean = encode(all_tok, norm_gain[None, :], weights, hidden)
    act_low = act_mean[:, 0].astype(bf16)
    out_t = weights[:, hidden : 2 * hidden]
    pool_part = contract_cols(act_low, out_t)
    pooled = token_mean[:, 0] + jnp.sum(share(pool_part, "col"), axis=0)
    pool_low = pooled.astype(bf16)
    dpool_low = contract_cols(grad_low, weights[:, 2 * hidden :]).astype(bf16)
    act_grad = jnp.dot(dpool_low, out_t, preferred_element_type=f32) / seq
    core = lax.rem(lax.axis_index("dp"), 2).astype(jnp.int32)[None]
    keep, send = weigh(core, normed, slope, act_grad[:, None, :], rows_d)
    swap = [(i, i ^ 1) for i in range(dp_size)]
    chip_sum = (keep + lax.ppermute(send, "dp", swap).astype(f32)).astype(bf16)
    chips = [list(range(0, dp_size, 2)), list(range(1, dp_size, 2))]
    in_sum = lax.all_to_all(chip_sum, "dp", 0, 0, axis_index_groups=chips, tiled=True)
    grad_w_in = jnp.sum(in_sum.astype(f32), axis=0)

    def slices(array):
        return array.reshape(-1, dp_size, rows_d).transpose(1, 0, 2)

    mixed = jnp.concatenate(
        (
            jnp.broadcast_to(act_low[None], (dp_size,) + act_low.shape),
            jnp.broadcast_to(grad_low[None], (dp_size,) + grad_low.shape),
            slices(dpool_low),
            slices(pool_low),
        ),
        axis=2,
    )
    mixed = lax.all_to_all(mixed, "dp", 0, 0, tiled=True)
    mixed = mixed.reshape(-1, mixed.shape[2])
    emb = grad_low.shape[1]
    act_all = mixed[:, :hidden]
    low_all = mixed[:, hidden : hidden + emb]
    dpool_all = mixed[:, hidden + emb : hidden + emb + rows_d]
    pool_all = mixed[:, hidden + emb + rows_d :]
    grad_w_out = contract_rows(act_all, dpool_all)
    grad_proj = contract_rows(pool_all, low_all)
    return (image_grad, text_grad, grad_w_in, grad_w_out, grad_proj)


def solution(mesh):
    in_specs = (
        P(("dp", "col"), None),
        P(("col", "dp"), None),
        P("dp"),
        P(),
        P(("dp", "col"), None, None),
        P(),
        P("dp", "col"),
        P("col", "dp"),
        P("dp", None),
    )
    out_specs = (
        P(("dp", "col"), None),
        P(("col", "dp"), None),
        P("dp", "col"),
        P("col", "dp"),
        P("dp", None),
    )
    return jax.shard_map(
        on_device, mesh=mesh, in_specs=in_specs, out_specs=out_specs, check_vma=False
    )
```

time: 639 us -> 337 us (0.53)
  waiting for transfers between devices: 360 us -> 141 us
  blocking collectives: 138 us -> 36.1 us
  starting transfers between devices: 0.36 us -> 52.7 us
  matrix products: 50 us -> 17.1 us
  Pallas kernels: 0 us -> 29.6 us
  local copies, waits for them, and re-layouts: 41.4 us -> 18.9 us
    all_gather x6 -> x1, waiting for transfers between devices: 186 us -> 0.01 us  [on_device(): lax.all_gather(jnp.concatenate((w_in, w_out.T, proj), axis=1), 'dp', axis...]
    all_to_all x0 -> x9, waiting for transfers between devices: none -> 141 us  [the longest x5 128 us: share(): lax.all_to_all(jnp.broadcast_to(piece[None], (count,) + piece.shape), axi...]
    psum x3 -> x0, blocking collectives: 88.6 us -> none  [the longest x1 42.5 us: on_device(): pooled, cached = lax.psum((pool_part, grad_part), 'col')]
    unnamed x10 -> x1, waiting for transfers between devices: 87.8 us -> 0.02 us
    reduce_scatter x2 -> x0, waiting for transfers between devices: 86.2 us -> none  [the longest x1 68.5 us: on_device(): lax.psum_scatter(jnp.dot(dlogit, all_txt, preferred_element_type=jnp.floa...]
    all_to_all x0 -> x9, starting transfers between devices: none -> 52.4 us  [the longest x5 31.1 us: share(): lax.all_to_all(jnp.broadcast_to(piece[None], (count,) + piece.shape), axi...]
    pmax x2 -> x0, blocking collectives: 49.3 us -> none  [the longest x1 25.3 us: on_device(): col_peak = lax.pmax(col_top, 'dp')]
    all_to_all x0 -> x2, blocking collectives: none -> 36.1 us  [share(): lax.all_to_all(jnp.broadcast_to(piece[None], (count,) + piece.shape), axi...]
  transfers between devices with their start and end apart: 9 -> 11, of which waited for: 8 -> 8; matrix products, arithmetic and copies ran while one was open for 16% -> 15% of each run, Pallas kernels for 0% -> 9%
where the time goes in v1:
time: 337 us; the launch traced here: 334 us
  waiting for transfers between devices  141 us (42%)
  starting transfers between devices  52.7 us (16%)
  blocking collectives  36.1 us (11%)
  Pallas kernels  29.6 us (9%)
  other arithmetic  24 us (7%)
  local copies, waits for them, and re-layouts  18.9 us (6%)
  matrix products  17.1 us (5%)
  between operations  15 us (4%)
    all_to_all x5, waiting for transfers between devices, share(): lax.all_to_all(jnp.broadcast_to(piece[None], (count,) + piece.shape), axi...  128 us
    all_to_all x2, blocking collectives, share(): lax.all_to_all(jnp.broadcast_to(piece[None], (count,) + piece.shape), axi...  36.1 us
    all_to_all x5, starting transfers between devices, share(): lax.all_to_all(jnp.broadcast_to(piece[None], (count,) + piece.shape), axi...  31.1 us
    pallas_call x1, Pallas kernels, weigh(): pl.pallas_call(backward_kernel, grid=(images,), in_specs=[pl.BlockSpec(me...  15.7 us
    pallas_call x1, Pallas kernels, encode(): pl.pallas_call(forward_kernel, grid=(images,), in_specs=[pl.BlockSpec((1,...  14 us
    broadcast_in_dim x7, local copies, waits for them, and re-layouts, share(): jnp.broadcast_to(piece[None], (count,) + piece.shape)  7.78 us
    all_to_all x1, waiting for transfers between devices, on_device(): lax.all_to_all(chip_sum, 'dp', 0, 0, axis_index_groups=chips, tiled=True)  7.32 us
    dot_general x3, matrix products, contract_rows(): lax.dot_general(left, right, (((0,), (0,)), ((), ())), preferred_element_...  7.02 us
  transfers between devices with their start and end apart: 11, of which 8 were waited for; matrix products, arithmetic and copies ran while one was open for 15% of the time, Pallas kernels for 9%

profile of v1, /device:TPU:8, one launch (start us, length us, event | category | flops | bytes accessed | tf_op | source)
XLA Modules:
  0.0 334.1 jit_solution(13140079887211619211)
XLA Ops:
  7.2 1.9 pad_maximum_fusion
  9.2 1.0 broadcast_in_dim.26
  10.2 24.3 %all_to_all.55 = bf16[8,64,1024]{2,1,0:T(8,128)(2,1)S(1)} all-to-all(bf16[8,64,1024]{2,1,0:T(8,128)(2,1)S(1)} %broadcast_in_dim.26), channel_id=1, replica_groups=mesh['dp'=16,'col'=8] {'col'}, dimensions={0} | all-to-all | bytes 2097152 | tf_op jit(solution)/shard_map/all_to_all | solution.py:33
  34.5 1.6 broadcast_in_dim.27
  36.1 5.4 %all-to-all-start.1 = ((bf16[16,64,1024]{2,1,0:T(8,128)(2,1)}), bf16[16,64,1024]{2,1,0:T(8,128)(2,1)S(1)}, u32[]{:S(2)}, u32[]{:S(2)}) async-start(bf16[16,64,1024]{2,1,0:T(8,128)(2,1)} %broadcast_in_dim.27), calls=%async_computation.1 | async-start | bytes 4194304 | tf_op jit(solution)/shard_map/all_to_all | solution.py:33
  42.5 1.2 multiply_convert_fusion.1
  43.7 35.2 %all-to-all-done.1 = bf16[16,64,1024]{2,1,0:T(8,128)(2,1)S(1)} async-done(((bf16[16,64,1024]{2,1,0:T(8,128)(2,1)}), bf16[16,64,1024]{2,1,0:T(8,128)(2,1)S(1)}, u32[]{:S(2)}, u32[]{:S(2)}) %all-to-all-start.1) | async-done | bytes 2097184 | tf_op jit(solution)/shard_map/all_to_all | solution.py:33
  80.5 1.4 fusion.37
  81.9 1.3 copy-done.3
  84.6 6.4 %all-to-all-start.2 = ((f32[8,2,512]{2,1,0:T(2,128)}), f32[8,2,512]{2,1,0:T(2,128)S(1)}, u32[]{:S(2)}, u32[]{:S(2)}) async-start(f32[8,2,512]{2,1,0:T(2,128)} %broadcast_in_dim.28), calls=%async_computation.2 | async-start | bytes 65536 | tf_op jit(solution)/shard_map/all_to_all | solution.py:33
  91.0 7.7 %all-to-all-done.2 = f32[8,2,512]{2,1,0:T(2,128)S(1)} async-done(((f32[8,2,512]{2,1,0:T(2,128)}), f32[8,2,512]{2,1,0:T(2,128)S(1)}, u32[]{:S(2)}, u32[]{:S(2)}) %all-to-all-start.2) | async-done | bytes 32800 | tf_op jit(solution)/shard_map/all_to_all | solution.py:33
  99.4 7.4 %all-to-all-start.3 = ((f32[16,2,1024]{2,1,0:T(2,128)}), f32[16,2,1024]{2,1,0:T(2,128)S(1)}, u32[]{:S(2)}, u32[]{:S(2)}) async-start(f32[16,2,1024]{2,1,0:T(2,128)} %broadcast_in_dim.29), calls=%async_computation.3 | async-start | bytes 262144 | tf_op jit(solution)/shard_map/all_to_all | solution.py:33
  107.5 4.2 %all-to-all-done.3 = f32[16,2,1024]{2,1,0:T(2,128)S(1)} async-done(((f32[16,2,1024]{2,1,0:T(2,128)}), f32[16,2,1024]{2,1,0:T(2,128)S(1)}, u32[]{:S(2)}, u32[]{:S(2)}) %all-to-all-start.3) | async-done | bytes 131104 | tf_op jit(solution)/shard_map/all_to_all | solution.py:33
  111.8 2.6 subtract_convert_fusion.2
  115.5 11.9 %all_to_all.56 = f32[8,8,1024]{2,1,0:T(8,128)S(1)} all-to-all(f32[8,8,1024]{2,1,0:T(8,128)S(1)} %broadcast_in_dim.34), channel_id=1, replica_groups=mesh['dp'=16,'col'=8] {'col'}, dimensions={0} | all-to-all | bytes 524288 | tf_op jit(solution)/shard_map/all_to_all | solution.py:33
  127.4 2.9 broadcast_in_dim.32
  130.3 4.7 %all-to-all-start.6 = ((bf16[8,257,1408]{2,1,0:T(8,128)(2,1)}), bf16[8,257,1408]{2,1,0:T(8,128)(2,1)}, u32[]{:S(2)}, u32[]{:S(2)}) async-start(bf16[8,257,1408]{2,1,0:T(8,128)(2,1)} %broadcast_in_dim.32), calls=%async_computation.6 | async-start | bytes 11894784 | tf_op jit(solution)/shard_map/all_to_all | solution.py:33
  135.1 1.2 fusion.10
  136.4 3.1 multiply_reduce_fusion
  139.6 2.1 subtract_convert_fusion
  141.7 1.4 multiply_reduce_fusion.2
  143.0 1.4 subtract_convert_fusion.1
  144.5 72.7 %all-to-all-done.6.tok_ref = bf16[8,257,1408]{2,1,0:T(8,128)(2,1)} async-done(((bf16[8,257,1408]{2,1,0:T(8,128)(2,1)}), bf16[8,257,1408]{2,1,0:T(8,128)(2,1)}, u32[]{:S(2)}, u32[]{:S(2)}) %all-to-all-start.6) | async-done | bytes 5789728 | tf_op jit(solution)/shard_map/all_to_all | solution.py:33
  217.2 4.6 %all-to-all-start.4 = ((bf16[8,64,1024]{2,1,0:T(8,128)(2,1)}), bf16[8,64,1024]{2,1,0:T(8,128)(2,1)S(1)}, u32[]{:S(2)}, u32[]{:S(2)}) async-start(bf16[8,64,1024]{2,1,0:T(8,128)(2,1)} %bitcast.11), calls=%async_computation.4 | async-start | bytes 2097152 | tf_op jit(solution)/shard_map/all_to_all | solution.py:196
  222.0 14.0 %encode.1 = (bf16[8,257,1408]{2,1,0:T(8,128)(2,1)S(1)}, f32[8,257,768]{2,1,0:T(8,128)}, f32[8,1,768]{2,1,0:T(1,128)S(1)}, f32[8,1,1408]{2,1,0:T(1,128)S(1)}) custom-call(bf16[8,257,1408]{2,1,0:T(8,128)(2,1)} %all-to-all-done.6.tok_ref, f32[1,1408]{1,0:T(1,128)S(1)} %broadcast_in_dim.33.gain_ref, bf16[1408,2560]{1,0:T(8,128)(2,1)} %all-gather.2.cloned.1.call-done.win_ref), custom_call_target="tpu_custom_call" | custom-call | flops 4446486528 | bytes 17895424 | tf_op jit(solution)/shard_map/encode/pallas_call | solution.py:55
  235.9 2.5 copy-done
  238.5 2.3 fusion.6
  240.8 0.8 broadcast_in_dim.38
  241.6 7.2 %all-to-all-start.9 = ((f32[8,8,1408]{2,1,0:T(8,128)}), f32[8,8,1408]{2,1,0:T(8,128)S(1)}, u32[]{:S(2)}, u32[]{:S(2)}) async-start(f32[8,8,1408]{2,1,0:T(8,128)} %broadcast_in_dim.38), calls=%async_computation.9 | async-start | bytes 720896 | tf_op jit(solution)/shard_map/all_to_all | solution.py:33
  249.0 8.6 %all-to-all-done.9 = f32[8,8,1408]{2,1,0:T(8,128)S(1)} async-done(((f32[8,8,1408]{2,1,0:T(8,128)}), f32[8,8,1408]{2,1,0:T(8,128)S(1)}, u32[]{:S(2)}, u32[]{:S(2)}) %all-to-all-start.9) | async-done | bytes 360480 | tf_op jit(solution)/shard_map/all_to_all | solution.py:33
  258.4 5.4 %all-to-all-start.5 = ((bf16[16,64,1024]{2,1,0:T(8,128)(2,1)}), bf16[16,64,1024]{2,1,0:T(8,128)(2,1)}, u32[]{:S(2)}, u32[]{:S(2)}) async-start(bf16[16,64,1024]{2,1,0:T(8,128)(2,1)} %bitcast.12), calls=%async_computation.5 | async-start | bytes 4194304 | tf_op jit(solution)/shard_map/all_to_all | solution.py:200
  263.8 2.7 fusion.3
  266.5 2.0 fusion.11
  268.6 15.7 %weigh.1 = (f32[8,88,768]{2,1,0:T(8,128)S(1)}, bf16[8,88,768]{2,1,0:T(8,128)(2,1)S(1)}) custom-call(s32[1]{0:T(128)} %bitcast.13.core_ref, bf16[8,257,1408]{2,1,0:T(8,128)(2,1)} %copy-done, f32[8,257,768]{2,1,0:T(8,128)} %get-tuple-element.12.slope_ref, f32[8,1,768]{2,1,0:T(1,128)S(1)} %broadcast_in_dim.35.grad_ref), custom_call_target="tpu_custom_call" | custom-call | flops 4446486528 | bytes 12105728 | tf_op jit(solution)/shard_map/weigh/pallas_call | solution.py:113
  286.2 1.0 reduce_sum.171
  288.1 1.4 broadcast_in_dim.36
  289.5 1.8 concatenate.7
  291.3 1.2 all-to-all-done.5
  292.5 4.6 %all-to-all-start.10 = ((bf16[16,8,1968]{2,1,0:T(8,128)(2,1)}), bf16[16,8,1968]{2,1,0:T(8,128)(2,1)}, u32[]{:S(2)}, u32[]{:S(2)}) async-start(bf16[16,8,1968]{2,1,0:T(8,128)(2,1)} %concatenate.7), calls=%async_computation.10 | async-start | bytes 1048576 | tf_op jit(solution)/shard_map/all_to_all | solution.py:236
  297.1 1.4 convert_reduce_fusion.2
  298.6 2.5 add_convert_fusion
  301.1 3.8 %all-to-all-done.10 = bf16[16,8,1968]{2,1,0:T(8,128)(2,1)} async-done(((bf16[16,8,1968]{2,1,0:T(8,128)(2,1)}), bf16[16,8,1968]{2,1,0:T(8,128)(2,1)}, u32[]{:S(2)}, u32[]{:S(2)}) %all-to-all-start.10) | async-done | bytes 503840 | tf_op jit(solution)/shard_map/all_to_all | solution.py:236
  304.9 6.7 %all-to-all-start.8 = ((bf16[8,88,768]{2,1,0:T(8,128)(2,1)}), bf16[8,88,768]{2,1,0:T(8,128)(2,1)S(1)}, u32[]{:S(2)}, u32[]{:S(2)}) async-start(bf16[8,88,768]{2,1,0:T(8,128)(2,1)} %add_convert_fusion), calls=%async_computation.8 | async-start | bytes 2162688 | tf_op jit(solution)/shard_map/all_to_all | solution.py:221
  312.4 2.0 convert_reduce_fusion
  315.2 1.9 fusion.16
  317.1 2.0 fusion.14
  319.1 7.3 %all-to-all-done.8 = bf16[8,88,768]{2,1,0:T(8,128)(2,1)S(1)} async-done(((bf16[8,88,768]{2,1,0:T(8,128)(2,1)}), bf16[8,88,768]{2,1,0:T(8,128)(2,1)S(1)}, u32[]{:S(2)}, u32[]{:S(2)}) %all-to-all-start.8) | async-done | bytes 1081376 | tf_op jit(solution)/shard_map/all_to_all | solution.py:221
  326.4 0.8 convert_reduce_fusion.1
  (82 shorter events, 11.7 us)
Async XLA Ops:
  7.2 214.8 %all-gather.2.cloned.1.call-start = ((), (), s32[]{:S(2)}) async-start(), calls=%async_computation.11 | async-start | bytes 7659520 | tf_op jit(solution)/shard_map/all_gather | solution.py:155
  7.2 27.3 %copy-start.11 = (bf16[64,1024]{1,0:T(8,128)(2,1)S(1)}, bf16[64,1024]{1,0:T(8,128)(2,1)}, u32[]{:S(2)}) copy-start(bf16[64,1024]{1,0:T(8,128)(2,1)} %param.10) | copy-start | bytes 393220
  36.1 42.7 %all-to-all-start.1 = ((bf16[16,64,1024]{2,1,0:T(8,128)(2,1)}), bf16[16,64,1024]{2,1,0:T(8,128)(2,1)S(1)}, u32[]{:S(2)}, u32[]{:S(2)}) async-start(bf16[16,64,1024]{2,1,0:T(8,128)(2,1)} %broadcast_in_dim.27), calls=%async_computation.1 | async-start | bytes 4194304 | tf_op jit(solution)/shard_map/all_to_all | solution.py:33
  79.3 1.2 copy-start.8
  79.7 2.2 copy-start.1
  81.9 1.3 copy-start.3
  84.6 14.1 %all-to-all-start.2 = ((f32[8,2,512]{2,1,0:T(2,128)}), f32[8,2,512]{2,1,0:T(2,128)S(1)}, u32[]{:S(2)}, u32[]{:S(2)}) async-start(f32[8,2,512]{2,1,0:T(2,128)} %broadcast_in_dim.28), calls=%async_computation.2 | async-start | bytes 65536 | tf_op jit(solution)/shard_map/all_to_all | solution.py:33
  99.4 12.2 %all-to-all-start.3 = ((f32[16,2,1024]{2,1,0:T(2,128)}), f32[16,2,1024]{2,1,0:T(2,128)S(1)}, u32[]{:S(2)}, u32[]{:S(2)}) async-start(f32[16,2,1024]{2,1,0:T(2,128)} %broadcast_in_dim.29), calls=%async_computation.3 | async-start | bytes 262144 | tf_op jit(solution)/shard_map/all_to_all | solution.py:33
  111.6 2.9 copy-start.2
  114.5 1.0 copy-start.6
  114.5 12.9 %copy-start.9 = (bf16[1,257,1408]{2,1,0:T(8,128)(2,1)S(1)}, bf16[1,257,1408]{2,1,0:T(8,128)(2,1)}, u32[]{:S(2)}) copy-start(bf16[1,257,1408]{2,1,0:T(8,128)(2,1)} %param.13) | copy-start | bytes 2171140
  130.3 86.9 %all-to-all-start.6 = ((bf16[8,257,1408]{2,1,0:T(8,128)(2,1)}), bf16[8,257,1408]{2,1,0:T(8,128)(2,1)}, u32[]{:S(2)}, u32[]{:S(2)}) async-start(bf16[8,257,1408]{2,1,0:T(8,128)(2,1)} %broadcast_in_dim.32), calls=%async_computation.6 | async-start | bytes 11894784 | tf_op jit(solution)/shard_map/all_to_all | solution.py:33
  139.5 2.1 copy-start.7
  144.5 77.3 %copy-start.14 = (f32[1408]{0:T(1024)S(1)}, f32[1408]{0:T(1024)}, u32[]{:S(2)}) copy-start(f32[1408]{0:T(1024)} %param.14) | copy-start | bytes 16900
  217.2 23.5 %all-to-all-start.4 = ((bf16[8,64,1024]{2,1,0:T(8,128)(2,1)}), bf16[8,64,1024]{2,1,0:T(8,128)(2,1)S(1)}, u32[]{:S(2)}, u32[]{:S(2)}) async-start(bf16[8,64,1024]{2,1,0:T(8,128)(2,1)} %bitcast.11), calls=%async_computation.4 | async-start | bytes 2097152 | tf_op jit(solution)/shard_map/all_to_all | solution.py:196
  235.9 2.5 copy-start
  238.5 19.2 %copy-start.13 = (bf16[8,1,768]{2,0,1:T(8,128)(2,1)}, bf16[8,1,768]{2,0,1:T(8,128)(2,1)S(1)}, u32[]{:S(2)}) copy-start(bf16[8,1,768]{2,0,1:T(8,128)(2,1)S(1)} %copy.90) | copy-start | bytes 36868
  240.7 16.9 %copy-start.4 = (bf16[8,64,1024]{2,1,0:T(8,128)(2,1)}, bf16[8,64,1024]{2,1,0:T(8,128)(2,1)S(1)}, u32[]{:S(2)}) copy-start(bf16[8,64,1024]{2,1,0:T(8,128)(2,1)S(1)} %all-to-all-done.4) | copy-start | bytes 3145732
  241.6 16.0 %all-to-all-start.9 = ((f32[8,8,1408]{2,1,0:T(8,128)}), f32[8,8,1408]{2,1,0:T(8,128)S(1)}, u32[]{:S(2)}, u32[]{:S(2)}) async-start(f32[8,8,1408]{2,1,0:T(8,128)} %broadcast_in_dim.38), calls=%async_computation.9 | async-start | bytes 720896 | tf_op jit(solution)/shard_map/all_to_all | solution.py:33
  257.6 0.7 copy-start.5
  258.4 34.1 %all-to-all-start.5 = ((bf16[16,64,1024]{2,1,0:T(8,128)(2,1)}), bf16[16,64,1024]{2,1,0:T(8,128)(2,1)}, u32[]{:S(2)}, u32[]{:S(2)}) async-start(bf16[16,64,1024]{2,1,0:T(8,128)(2,1)} %bitcast.12), calls=%async_computation.5 | async-start | bytes 4194304 | tf_op jit(solution)/shard_map/all_to_all | solution.py:200
  263.8 4.7 %copy-start.12 = (bf16[8,1024]{1,0:T(8,128)(2,1)}, bf16[8,1024]{1,0:T(8,128)(2,1)S(1)}, u32[]{:S(2)}) copy-start(bf16[8,1024]{1,0:T(8,128)(2,1)S(1)} %fusion.27) | copy-start | bytes 49156
  268.6 15.9 %copy-start.10 = (bf16[64,1024]{1,0:T(8,128)(2,1)S(1)}, bf16[64,1024]{1,0:T(8,128)(2,1)}, u32[]{:S(2)}) copy-start(bf16[64,1024]{1,0:T(8,128)(2,1)} %param.9) | copy-start | bytes 393220
  284.2 14.3 %collective-permute-start = (bf16[8,88,768]{2,1,0:T(8,128)(2,1)S(1)}, bf16[8,88,768]{2,1,0:T(8,128)(2,1)}, u32[]{:S(2)}, u32[]{:S(2)}) collective-permute-start(bf16[8,88,768]{2,1,0:T(8,128)(2,1)S(1)} %get-tuple-element.14), channel_id=1, source_target_pairs={{0,8},{8,0},{16,24},{24,16},{32,40},{40,32},{48,56},{56,48},{64,72... | collective-permute-start | bytes 3244040 | tf_op jit(solution)/shard_map/ppermute | solution.py:219
  292.5 12.5 %all-to-all-start.10 = ((bf16[16,8,1968]{2,1,0:T(8,128)(2,1)}), bf16[16,8,1968]{2,1,0:T(8,128)(2,1)}, u32[]{:S(2)}, u32[]{:S(2)}) async-start(bf16[16,8,1968]{2,1,0:T(8,128)(2,1)} %concatenate.7), calls=%async_computation.10 | async-start | bytes 1048576 | tf_op jit(solution)/shard_map/all_to_all | solution.py:236
  301.1 10.5 %copy-start.15 = (f32[64]{0:T(128)S(1)}, f32[64]{0:T(128)}, u32[]{:S(2)}) copy-start(f32[64]{0:T(128)} %rsqrt_multiply_fusion.1) | copy-start | bytes 772
  304.9 21.5 %all-to-all-start.8 = ((bf16[8,88,768]{2,1,0:T(8,128)(2,1)}), bf16[8,88,768]{2,1,0:T(8,128)(2,1)S(1)}, u32[]{:S(2)}, u32[]{:S(2)}) async-start(bf16[8,88,768]{2,1,0:T(8,128)(2,1)} %add_convert_fusion), calls=%async_computation.8 | async-start | bytes 2162688 | tf_op jit(solution)/shard_map/all_to_all | solution.py:221
Sparse Core Ops, SparseCore 0:
  9.7 77.2 all-gather.1

commit v2 on v1

v2 whole, which is shorter than its diff:
```python
import functools

import jax
import jax.numpy as jnp
from jax import lax
from jax.experimental import pallas as pl
from jax.experimental.pallas import tpu as pltpu
from jax.sharding import PartitionSpec as P

epsilon = 1e-06
inv_root_two_pi = 0.3989422804014327
root_half = 0.7071067811865476
bf16 = jnp.bfloat16
f32 = jnp.float32


def unit_rows(raw):
    values = raw.astype(f32)
    inverse = lax.rsqrt(jnp.sum(values * values, axis=-1, keepdims=True) + epsilon)
    return (values * inverse, inverse)


def contract_rows(left, right):
    return lax.dot_general(left, right, (((0,), (0,)), ((), ())), preferred_element_type=f32)


def contract_cols(left, right):
    return lax.dot_general(left, right, (((1,), (1,)), ((), ())), preferred_element_type=f32)


def share(piece, axis, groups=None):
    count = len(groups[0]) if groups else lax.axis_size(axis)
    copies = jnp.broadcast_to(piece[None], (count,) + piece.shape)
    return lax.all_to_all(copies, axis, 0, 0, axis_index_groups=groups, tiled=True)


def encode_kernel(cuts, *refs):
    images = len(cuts)
    pieces = 1 + max(cut[0] for image in cuts for cut in image)
    toks, refs = refs[:pieces], refs[pieces:]
    gain_ref, win_ref, main_ref, last_ref, slope_ref, slope_last_ref, act_ref, slots, sems = refs
    step = pl.program_id(0)

    def copies(index):
        slot = index % 2
        return [
            pltpu.make_async_copy(
                toks[piece], slots.at[slot, :, pl.ds(start, size)], sems.at[slot, k]
            )
            for k, (piece, start, size) in enumerate(cuts[index])
        ]

    def each(index, act):
        for k in range(images):

            @pl.when(index == k)
            def _():
                for copy in copies(k):
                    act(copy)

    @pl.when(step == 0)
    def _():
        each(step, lambda copy: copy.start())

    @pl.when(step + 1 < images)
    def _():
        each(step + 1, lambda copy: copy.start())

    each(step, lambda copy: copy.wait())
    slot = lax.rem(step, 2)
    floats = slots[slot].astype(f32)
    seq = floats.shape[0]
    center = jnp.mean(floats, axis=1, keepdims=True)
    shifted = floats - center
    spread = jnp.mean(shifted * shifted, axis=1, keepdims=True)
    wide = shifted * lax.rsqrt(spread + epsilon) * gain_ref[...]
    normed = wide.astype(bf16)
    main_ref[...] = normed[: seq - 1].T
    last_ref[0] = normed[seq - 1 :]
    pre = jnp.dot(normed, win_ref[...], preferred_element_type=f32)
    half = 0.5 * (1.0 + lax.erf(pre * root_half))
    act_ref[0] = jnp.sum(pre * half, axis=0, keepdims=True) * (1.0 / seq)
    slope = half + pre * jnp.exp(-0.5 * pre * pre) * inv_root_two_pi
    slope_ref[0] = slope[: seq - 1]
    slope_last_ref[0] = slope[seq - 1 :]


def encode(tokens, gain, weights, hidden):
    seq, width = tokens[0][0].shape[0], sum(piece.shape[1] for piece in tokens[0])
    images = len(tokens)
    pieces, cuts = [], []
    for image in tokens:
        ends = [sum(piece.shape[1] for piece in image[:k]) for k in range(len(image))]
        cuts.append(
            [(len(pieces) + k, end, piece.shape[1]) for k, (end, piece) in enumerate(zip(ends, image))]
        )
        pieces += image
    return pl.pallas_call(
        functools.partial(encode_kernel, cuts),
        grid=(images,),
        in_specs=[pl.BlockSpec(memory_space=pltpu.HBM)] * len(pieces)
        + [
            pl.BlockSpec((1, width), lambda i: (0, 0)),
            pl.BlockSpec((width, hidden), lambda i: (0, 0)),
        ],
        out_specs=[
            pl.BlockSpec((width, seq - 1), lambda i: (0, i)),
            pl.BlockSpec((1, 1, width), lambda i: (i, 0, 0)),
            pl.BlockSpec((1, seq - 1, hidden), lambda i: (i, 0, 0)),
            pl.BlockSpec((1, 1, hidden), lambda i: (i, 0, 0)),
            pl.BlockSpec((1, 1, hidden), lambda i: (i, 0, 0)),
        ],
        out_shape=[
            jax.ShapeDtypeStruct((width, images * (seq - 1)), bf16),
            jax.ShapeDtypeStruct((images, 1, width), bf16),
            jax.ShapeDtypeStruct((images, seq - 1, hidden), f32),
            jax.ShapeDtypeStruct((images, 1, hidden), f32),
            jax.ShapeDtypeStruct((images, 1, hidden), f32),
        ],
        scratch_shapes=[
            pltpu.VMEM((2, seq, width), bf16),
            pltpu.SemaphoreType.DMA((2, 2)),
        ],
        compiler_params=pltpu.CompilerParams(vmem_limit_bytes=60 * 2**20),
        cost_estimate=pl.CostEstimate(
            flops=2 * images * seq * width * hidden,
            bytes_accessed=images * seq * (4 * width + 4 * hidden),
            transcendentals=images * seq * hidden * 2,
        ),
        name="encode",
    )(*pieces, gain, weights)


def weigh_kernel(core_ref, order_ref, *refs):
    grad_ref, keep_ref, send_ref, pre_grad, pre_last, last_rows, last_term, total = refs[-8:]
    sets = (refs[0:4], refs[4:8])
    images, tokens, _ = sets[0][2].shape

    @pl.when(pl.program_id(0) == 0)
    def _():
        for k, (_, last_ref, slope_ref, slope_last_ref) in enumerate(sets):
            for i in range(images):
                row = grad_ref[order_ref[k * images + i]]
                pre_grad[k, pl.ds(i * tokens, tokens), :] = (slope_ref[i] * row).astype(bf16)
                pre_last[pl.ds(k * images + i, 1), :] = slope_last_ref[i] * row
                last_rows[pl.ds(k * images + i, 1), :] = last_ref[i].astype(f32)
        last_term[...] = contract_rows(last_rows[...].astype(bf16), pre_last[...].astype(bf16))

    chunk = total.shape[0]
    value = last_term[pl.ds(pl.multiple_of(pl.program_id(0) * chunk, 8), chunk), :]
    for k, (main_ref, _, _, _) in enumerate(sets):
        value += jnp.dot(main_ref[...], pre_grad[k], preferred_element_type=f32)
    total[...] = value
    core = core_ref[0]
    pairs, rows, _ = keep_ref.shape
    for pair in range(pairs):
        mine = pl.multiple_of((2 * pair + core) * rows, 8)
        other = pl.multiple_of((2 * pair + 1 - core) * rows, 8)
        keep_ref[pair] = total[pl.ds(mine, rows), :]
        send_ref[pair] = total[pl.ds(other, rows), :].astype(bf16)


def weigh(core, order, sets, act_grad, rows):
    main, _, slope, _ = sets[0]
    images, tokens, hidden = slope.shape
    width = main.shape[0]
    chunk = 4 * rows
    steps = width // chunk
    set_specs = [
        pl.BlockSpec((chunk, images * tokens), lambda i: (i, 0)),
        pl.BlockSpec((images, 1, width), lambda i: (0, 0, 0)),
        pl.BlockSpec((images, tokens, hidden), lambda i: (0, 0, 0)),
        pl.BlockSpec((images, 1, hidden), lambda i: (0, 0, 0)),
    ]
    operands = []
    for main, last, slope, slope_last in sets:
        operands += [main, last, slope, slope_last]
    return pl.pallas_call(
        weigh_kernel,
        grid=(steps,),
        in_specs=[pl.BlockSpec(memory_space=pltpu.SMEM)] * 2
        + set_specs * len(sets)
        + [pl.BlockSpec(act_grad.shape, lambda i: (0, 0, 0))],
        out_specs=[
            pl.BlockSpec((2, rows, hidden), lambda i: (i, 0, 0)),
            pl.BlockSpec((2, rows, hidden), lambda i: (i, 0, 0)),
        ],
        out_shape=[
            jax.ShapeDtypeStruct((2 * steps, rows, hidden), f32),
            jax.ShapeDtypeStruct((2 * steps, rows, hidden), bf16),
        ],
        scratch_shapes=[
            pltpu.VMEM((len(sets), images * tokens, hidden), bf16),
            pltpu.VMEM((len(sets) * images, hidden), f32),
            pltpu.VMEM((len(sets) * images, width), f32),
            pltpu.VMEM((width, hidden), f32),
            pltpu.VMEM((chunk, hidden), f32),
        ],
        compiler_params=pltpu.CompilerParams(vmem_limit_bytes=60 * 2**20),
        cost_estimate=pl.CostEstimate(
            flops=4 * images * tokens * width * hidden,
            bytes_accessed=2 * images * tokens * (2 * width + 4 * hidden),
            transcendentals=0,
        ),
        name="weigh",
    )(core, order, *operands, act_grad)


def unit_kernel(where_ref, *refs):
    pieces = refs[:-10]
    txt_hbm, raw_img, low_img, low_txt, inv_img, inv_txt, first_rows, halves, raw_txt, sems = refs[-10:]
    blocks = raw_txt.shape[0]
    part = blocks // len(pieces)
    img_loads, txt_loads = [], []
    for hop, piece in enumerate(pieces):
        chunk = pl.ds(hop * part, part)
        img_loads.append(pltpu.make_async_copy(piece, halves.at[hop], sems.at[0, hop]))
        txt_loads.append(
            pltpu.make_async_copy(txt_hbm.at[chunk], raw_txt.at[chunk], sems.at[1, hop])
        )
    for load in img_loads + txt_loads:
        load.start()
    for hop, load in enumerate(img_loads):
        load.wait()
        for flag in range(2):
            spot = where_ref[2 * hop + flag]
            values = halves[hop, flag]
            unit, inverse = unit_rows(values)
            raw_img[spot] = values
            first_rows[pl.ds(spot, 1), :] = values[0:1].astype(f32)
            low_img[spot] = unit.astype(bf16)
            inv_img[spot] = inverse
    for hop, load in enumerate(txt_loads):
        load.wait()
        for k in range(hop * part, hop * part + part):
            unit, inverse = unit_rows(raw_txt[k])
            low_txt[k] = unit.astype(bf16)
            inv_txt[k] = inverse


def gather_units(where, ring_img, raw_txt):
    texts, rows, width = raw_txt.shape
    images = 2 * len(ring_img)
    vmem = pl.BlockSpec(memory_space=pltpu.VMEM)
    return pl.pallas_call(
        unit_kernel,
        in_specs=[pl.BlockSpec(memory_space=pltpu.SMEM)]
        + [pl.BlockSpec(memory_space=pl.ANY)] * len(ring_img)
        + [pl.BlockSpec(memory_space=pltpu.HBM)],
        out_specs=[vmem] * 6,
        out_shape=[
            jax.ShapeDtypeStruct((images, rows, width), bf16),
            jax.ShapeDtypeStruct((images, rows, width), bf16),
            jax.ShapeDtypeStruct((texts, rows, width), bf16),
            jax.ShapeDtypeStruct((images, rows, 1), f32),
            jax.ShapeDtypeStruct((texts, rows, 1), f32),
            jax.ShapeDtypeStruct((images, width), f32),
        ],
        scratch_shapes=[
            pltpu.VMEM((len(ring_img), 2, rows, width), bf16),
            pltpu.VMEM((texts, rows, width), bf16),
            pltpu.SemaphoreType.DMA((2, len(ring_img))),
        ],
        compiler_params=pltpu.CompilerParams(vmem_limit_bytes=24 * 2**20),
        cost_estimate=pl.CostEstimate(
            flops=4 * (images + texts) * rows * width,
            bytes_accessed=6 * (images + texts) * rows * width,
            transcendentals=0,
        ),
        name="gather_units",
    )(where, *ring_img, raw_txt)


def direction_kernel(turn, left_ref, inv_ref, low_hbm, raw_hbm, out_hbm, low, raw, out, *rest):
    in_sems, out_sems = rest[-2:]
    blocks, rows, _ = raw.shape
    part = blocks // 4
    loads = [
        pltpu.make_async_copy(low_hbm, low, in_sems.at[0]),
        pltpu.make_async_copy(raw_hbm, raw, in_sems.at[1]),
    ]
    for load in loads:
        load.start()
    left = left_ref
    if turn:
        left = rest[0]
        left[...] = left_ref[...].T
    for load in loads:
        load.wait()
    stores = []
    for k in range(4):
        total = jnp.dot(
            left[pl.ds(k * part * rows, part * rows), :], low[...], preferred_element_type=f32
        )
        for m in range(part):
            unit = raw[k * part + m].astype(f32) * inv_ref[k * part + m]
            piece = project(total[m * rows : (m + 1) * rows], unit)
            out[k * part + m] = piece.astype(out.dtype)
        piece = pl.ds(k * part, part)
        stores.append(pltpu.make_async_copy(out.at[piece], out_hbm.at[piece], out_sems.at[k]))
        stores[-1].start()
    for store in stores:
        store.wait()


def directions(turn, dlogit, low, raw, inv, kind):
    vmem = pl.BlockSpec(memory_space=pltpu.VMEM)
    hbm = pl.BlockSpec(memory_space=pltpu.HBM)
    turned = [pltpu.VMEM(dlogit.shape[::-1], bf16)] if turn else []
    return pl.pallas_call(
        functools.partial(direction_kernel, turn),
        in_specs=[vmem] * 2 + [pl.BlockSpec(memory_space=pl.ANY)] * 2,
        out_specs=hbm,
        out_shape=jax.ShapeDtypeStruct(raw.shape, kind),
        scratch_shapes=[
            pltpu.VMEM(low.shape, bf16),
            pltpu.VMEM(raw.shape, bf16),
            pltpu.VMEM(raw.shape, kind),
        ]
        + turned
        + [pltpu.SemaphoreType.DMA((2,)), pltpu.SemaphoreType.DMA((4,))],
        compiler_params=pltpu.CompilerParams(vmem_limit_bytes=60 * 2**20),
        cost_estimate=pl.CostEstimate(
            flops=2 * dlogit.size * low.shape[1], bytes_accessed=4 * raw.size, transcendentals=0
        ),
        name="directions",
    )(dlogit, inv, low, raw)


def project(partial, unit):
    return partial - unit * jnp.sum(unit * partial, axis=1, keepdims=True)


def head_kernel(
    seq, spots_ref, temper_ref, cached_ref, raw_ref, mean_ref, act_a, act_b, weights_hbm,
    mixed_ref, grad_ref, out_t, proj, act_rows, sems,
):
    hidden, emb = out_t.shape[1], proj.shape[1]
    loads = [
        pltpu.make_async_copy(weights_hbm.at[:, pl.ds(2 * hidden, emb)], proj, sems.at[0]),
        pltpu.make_async_copy(weights_hbm.at[:, pl.ds(hidden, hidden)], out_t, sems.at[1]),
    ]
    for load in loads:
        load.start()
    images = cached_ref.shape[0]
    half = images // 2
    for k in range(images):
        row = act_a[k] if k < half else act_b[k - half]
        act_rows[pl.ds(spots_ref[k], 1), :] = row
    act_low = act_rows[...].astype(bf16)
    cached_dir = temper_ref[0] * jnp.sum(cached_ref[...], axis=0)
    unit, inverse = unit_rows(raw_ref[...])
    grad_low = (inverse * project(cached_dir, unit)).astype(bf16)
    loads[0].wait()
    dpool_low = contract_cols(grad_low, proj[...]).astype(bf16)
    loads[1].wait()
    act_grad = jnp.dot(dpool_low, out_t[...], preferred_element_type=f32) / seq
    for k in range(images):
        grad_ref[k] = act_grad[k : k + 1]
    own = lax.broadcasted_iota(jnp.int32, (images, 1), 0) == spots_ref[images]
    pool_part = contract_cols(act_low, out_t[...]) + jnp.where(own, mean_ref[...], 0.0)
    pool_high = pool_part.astype(bf16).astype(f32)
    pool_rest = pool_part - pool_high
    dpool = dpool_low.astype(f32)
    chips = mixed_ref.shape[0]
    rows = pool_part.shape[1] // chips
    first = hidden + emb
    for k in range(chips):
        mixed_ref[k, :, 0:hidden] = act_low
        mixed_ref[k, :, hidden:first] = grad_low
        for m, array in enumerate((dpool, pool_high, pool_rest)):
            start = first + 128 * m
            mixed_ref[k, :, start : start + rows] = array[:, k * rows : (k + 1) * rows].astype(bf16)


def head(seq, spots, temper, cached, raw, mean, act_a, act_b, weights, chips):
    images, _, emb = cached.shape
    hidden = act_a.shape[2]
    width = weights.shape[0]
    smem = pl.BlockSpec(memory_space=pltpu.SMEM)
    vmem = pl.BlockSpec(memory_space=pltpu.VMEM)
    return pl.pallas_call(
        functools.partial(head_kernel, seq),
        in_specs=[smem] * 2 + [vmem] * 5 + [pl.BlockSpec(memory_space=pltpu.HBM)],
        out_specs=[vmem] * 2,
        out_shape=[
            jax.ShapeDtypeStruct((chips, images, hidden + emb + 3 * 128), bf16),
            jax.ShapeDtypeStruct((images, 1, hidden), f32),
        ],
        scratch_shapes=[
            pltpu.VMEM((width, hidden), bf16),
            pltpu.VMEM((width, emb), bf16),
            pltpu.VMEM((images, hidden), f32),
            pltpu.SemaphoreType.DMA((2,)),
        ],
        compiler_params=pltpu.CompilerParams(vmem_limit_bytes=60 * 2**20),
        cost_estimate=pl.CostEstimate(
            flops=4 * images * width * (hidden + emb),
            bytes_accessed=2 * width * (hidden + emb),
            transcendentals=0,
        ),
        name="head",
    )(spots, temper, cached, raw, mean, act_a, act_b, weights)


def on_device(image_emb, text_emb, pairs, logit_scale, tokens, norm_gain, w_in, w_out, proj):
    dp_size = lax.axis_size("dp")
    cols = lax.axis_size("col")
    ring = cols // 2
    hidden = w_in.shape[1]
    rows_d = w_in.shape[0]
    _, seq, width = tokens.shape
    temper = logit_scale[0]
    own_col = lax.axis_index("col")
    place, side = own_col // 2, own_col % 2
    core = lax.axis_index("dp") % 2
    swap = [(i, i ^ 1) for i in range(dp_size)]
    chips = [list(range(0, dp_size, 2)), list(range(1, dp_size, 2))]

    far_dp = dp_size // 2
    both = ("dp", "col")
    twin = [((d + far_dp) % dp_size) * cols + (c ^ 1) for d in range(dp_size) for c in range(cols)]
    row_groups = [
        [((d + far_dp * (c % 2)) % dp_size) * cols + c for c in range(cols)] for d in range(dp_size)
    ]

    def across(piece):
        return lax.ppermute(piece, both, list(enumerate(twin)))

    def share_rows(piece):
        return share(piece, both, row_groups)

    def along(piece, hop):
        return lax.ppermute(piece, "col", [(i, (i - 2 * hop) % cols) for i in range(cols)])

    hops = (0, 1, 3, 2)
    shard = jnp.concatenate((w_in, w_out.T, proj), axis=1)
    own_tok = tokens[0]
    raw_txt = lax.all_gather(text_emb, "dp", axis=0, tiled=True)
    weights = lax.all_gather(shard, "dp", axis=0, tiled=True)
    other_img = across(image_emb)
    other_pairs = across(pairs)
    near = [along(own_tok, hop) for hop in (1, 3)]
    own_tok, other_img, other_pairs, near = lax.optimization_barrier(
        (own_tok, other_img, other_pairs, near)
    )
    pair_img = jnp.stack((image_emb, other_img))
    ring_img = [pair_img] + [along(pair_img, hop) for hop in hops[1:]]
    other_tok = across(own_tok)
    ring_img, raw_txt, own_tok = lax.optimization_barrier((ring_img, raw_txt, own_tok))
    facing = along(own_tok, 2)
    own_rows, emb = image_emb.shape
    raw_txt = raw_txt.reshape(dp_size, own_rows, emb)
    where = [((place + hop) % ring) * 2 + flag for hop in hops for flag in (side, 1 - side)]
    order = jnp.stack([where[k] for k in (0, 2, 4, 1, 6, 3, 5, 7)]).astype(jnp.int32)
    where = jnp.stack(where + [core]).astype(jnp.int32)
    raw_img, img_low, txt_low, img_inv, txt_inv, cached_raw = gather_units(where, ring_img, raw_txt)
    img_low = img_low.reshape(-1, emb)
    txt_low = txt_low.reshape(-1, emb)
    logits = temper * contract_cols(img_low, txt_low)
    txt_count = txt_low.shape[0]
    col_base = own_col * txt_count
    group_pairs = jnp.where(
        (jnp.arange(cols, dtype=jnp.int32) % 2 == side)[:, None],
        pairs.reshape(cols, own_rows),
        other_pairs.reshape(cols, own_rows),
    ).reshape(-1)
    matches = (
        group_pairs[:, None] == col_base + jnp.arange(txt_count, dtype=jnp.int32)[None, :]
    ).astype(f32)
    row_top = jnp.max(logits, axis=1)
    row_mass = jnp.sum(jnp.exp(logits - row_top[:, None]), axis=1)
    col_top = jnp.max(logits, axis=0)
    col_mass = jnp.sum(jnp.exp(logits - col_top[None, :]), axis=0)
    row_top, row_mass, facing = lax.optimization_barrier((row_top, row_mass, facing))
    row_stats = share_rows(jnp.stack((row_top, row_mass)))
    row_stats, other_tok = lax.optimization_barrier((row_stats, other_tok))
    far = [along(other_tok, hop) for hop in (1, 3)]
    col_stats = share(jnp.stack((col_top, col_mass)), "dp")
    gain = norm_gain[None, :]
    first = encode([[own_tok], [near[0]], [near[1]], [other_tok]], gain, weights, hidden)

    def lse(stats):
        peak = jnp.max(stats[:, 0], axis=0)
        return peak + jnp.log(jnp.sum(stats[:, 1] * jnp.exp(stats[:, 0] - peak), axis=0))

    row_stats, col_stats, far, other_tok = lax.optimization_barrier(
        (row_stats, col_stats, far, other_tok)
    )
    far_facing = along(other_tok, 2)
    row_lse = lse(row_stats)
    col_lse = lse(col_stats)
    dlogit = (
        0.5 * (jnp.exp(logits - row_lse[:, None]) + jnp.exp(logits - col_lse[None, :])) - matches
    ).astype(bf16)

    cached_part = jnp.dot(
        dlogit.reshape(cols, own_rows, txt_count)[:, 0], txt_low, preferred_element_type=f32
    )
    txt_part = directions(True, dlogit, img_low, raw_txt, txt_inv, f32)
    txt_sum = lax.psum_scatter(txt_part.reshape(-1, emb), "dp", scatter_dimension=0, tiled=True)
    second = encode([[facing], [far[0]], [far[1]], [far_facing]], gain, weights, hidden)
    own_mean = jnp.mean(own_tok.astype(f32), axis=0, keepdims=True)
    spots = jnp.concatenate((order, own_col[None]))
    cached_all = share_rows(cached_part)
    img_part = directions(False, dlogit, txt_low, raw_img, img_inv, bf16)
    cached_all, first, second, own_mean, img_part = lax.optimization_barrier(
        (cached_all, first, second, own_mean, img_part)
    )
    img_pairs = img_part.reshape(ring, 2, own_rows, emb)

    def to_place(hop):
        return lax.dynamic_index_in_dim(img_pairs, (place + hop) % ring, 0, keepdims=False)

    img_terms = [along(to_place(ring - hop), hop) for hop in hops[1:]]
    _, own_img_inv = unit_rows(image_emb)
    _, own_txt_inv = unit_rows(text_emb)

    mixed, act_grad = head(
        seq, spots, logit_scale, cached_all, cached_raw, own_mean, first[4], second[4], weights, dp_size
    )
    keep, send = weigh(
        core.astype(jnp.int32)[None],
        order,
        (first[:4], second[:4]),
        act_grad,
        rows_d,
    )
    mixed = lax.all_to_all(mixed, "dp", 0, 0, tiled=True)
    send, mixed, img_terms = lax.optimization_barrier((send, mixed, img_terms))
    received = lax.ppermute(send, "dp", swap)
    mixed = mixed.reshape(-1, mixed.shape[2])
    act_all, low_all = mixed[:, :hidden], mixed[:, hidden : hidden + emb]
    dpool_all, pool_high, pool_rest = (
        mixed[:, hidden + emb + 128 * k : hidden + emb + 128 * k + rows_d] for k in range(3)
    )
    grad_w_out = contract_rows(act_all, dpool_all)
    pool_all = pool_high.astype(f32) + pool_rest.astype(f32)
    pair_sum = to_place(0).astype(f32) + sum(term.astype(f32) for term in img_terms)
    received, pair_sum, pool_all, grad_w_out = lax.optimization_barrier(
        (received, pair_sum, pool_all, grad_w_out)
    )
    for partner in (lambda x: x ^ 1, lambda x: ring - 1 - x):
        hop = [(c, partner(c // 2) * 2 + c % 2) for c in range(cols)]
        pool_all += lax.ppermute(pool_all, "col", hop)
    half = pool_all.shape[0] // 2
    turned = jnp.concatenate((pool_all[half:], pool_all[:half]))
    pool_all += lax.ppermute(turned, "col", [(c, c ^ 1) for c in range(cols)])
    pool_all = pool_all.astype(bf16)
    grad_proj = contract_rows(pool_all, low_all)
    chip_sum = (keep + received.astype(f32)).astype(bf16)
    in_sum = lax.all_to_all(chip_sum, "dp", 0, 0, axis_index_groups=chips, tiled=True)
    kept = jnp.where(side == 0, pair_sum[0], pair_sum[1])
    away = jnp.where(side == 0, pair_sum[1], pair_sum[0])
    img_sum = kept + across(away.astype(bf16)).astype(f32)
    image_grad = own_img_inv * temper * img_sum
    in_sum, txt_sum = lax.optimization_barrier((in_sum, txt_sum))
    text_grad = own_txt_inv * temper * txt_sum
    grad_w_in = jnp.sum(in_sum.astype(f32), axis=0)
    return (image_grad, text_grad, grad_w_in, grad_w_out, grad_proj)


def solution(mesh):
    in_specs = (
        P(("dp", "col"), None),
        P(("col", "dp"), None),
        P("dp"),
        P(),
        P(("dp", "col"), None, None),
        P(),
        P("dp", "col"),
        P("col", "dp"),
        P("dp", None),
    )
    out_specs = (
        P(("dp", "col"), None),
        P(("col", "dp"), None),
        P("dp", "col"),
        P("col", "dp"),
        P("dp", None),
    )
    return jax.shard_map(
        on_device, mesh=mesh, in_specs=in_specs, out_specs=out_specs, check_vma=False
    )
```

time: 337 us -> 214 us (0.64)
  waiting for transfers between devices: 141 us -> 49.2 us
  blocking collectives: 36.1 us -> 0 us
  Pallas kernels: 29.6 us -> 49.3 us
  matrix products: 17.1 us -> 3.65 us
  starting transfers between devices: 52.7 us -> 64.5 us
  other arithmetic: 24 us -> 13.6 us
    all_to_all x7 -> x3, waiting for transfers between devices: 130 us -> 12 us  [share(): lax.all_to_all(copies, axis, 0, 0, axis_index_groups=groups, tiled=True)]
    ppermute x1 -> x20, starting transfers between devices: 0.23 us -> 38.9 us  [the longest x12 22.9 us: along(): lax.ppermute(piece, 'col', [(i, (i - 2 * hop) % cols) for i in range(cols)])]
    ppermute x1 -> x20, waiting for transfers between devices: 0.01 us -> 36.4 us  [the longest x12 21.8 us: along(): lax.ppermute(piece, 'col', [(i, (i - 2 * hop) % cols) for i in range(cols)])]
    all_to_all x2 -> x0, blocking collectives: 36.1 us -> none  [share(): lax.all_to_all(jnp.broadcast_to(piece[None], (count,) + piece.shape), axi...]
    all_to_all x7 -> x3, starting transfers between devices: 41.1 us -> 15 us  [share(): lax.all_to_all(copies, axis, 0, 0, axis_index_groups=groups, tiled=True)]
    pallas_call x2 -> x7, Pallas kernels: 29.6 us -> 49.3 us  [the longest x2 18.3 us: encode(): pl.pallas_call(functools.partial(encode_kernel, cuts), grid=(images,), in...]
    convert_element_type x8 -> x2, other arithmetic: 9.01 us -> 1.34 us  [the longest x1 1.31 us: on_device(): chip_sum = (keep + received.astype(f32)).astype(bf16)]
    all_to_all x1, waiting for transfers between devices: 7.32 us -> 0.01 us  [on_device(): lax.all_to_all(chip_sum, 'dp', 0, 0, axis_index_groups=chips, tiled=True)]
  transfers between devices with their start and end apart: 11 -> 28, of which waited for: 8 -> 11; matrix products, arithmetic and copies ran while one was open for 15% -> 10% of each run, Pallas kernels for 9% -> 23%
where the time goes in v2:
time: 214 us; the launch traced here: 213 us
  starting transfers between devices  64.5 us (30%)
  Pallas kernels  49.3 us (23%)
  waiting for transfers between devices  49.2 us (23%)
  local copies, waits for them, and re-layouts  17.6 us (8%)
  between operations  14.8 us (7%)
  other arithmetic  13.6 us (6%)
  matrix products  3.65 us (2%)
    ppermute x12, starting transfers between devices, along(): lax.ppermute(piece, 'col', [(i, (i - 2 * hop) % cols) for i in range(cols)])  22.9 us
    ppermute x12, waiting for transfers between devices, along(): lax.ppermute(piece, 'col', [(i, (i - 2 * hop) % cols) for i in range(cols)])  21.8 us
    pallas_call x2, Pallas kernels, encode(): pl.pallas_call(functools.partial(encode_kernel, cuts), grid=(images,), in...  18.3 us
    all_to_all x3, starting transfers between devices, share(): lax.all_to_all(copies, axis, 0, 0, axis_index_groups=groups, tiled=True)  15 us
    all_to_all x3, waiting for transfers between devices, share(): lax.all_to_all(copies, axis, 0, 0, axis_index_groups=groups, tiled=True)  12 us
    ppermute x4, starting transfers between devices, across(): return lax.ppermute(piece, both, list(enumerate(twin)))  11.9 us
    unnamed x52, local copies, waits for them, and re-layouts  11.6 us
    pallas_call x1, Pallas kernels, weigh(): pl.pallas_call(weigh_kernel, grid=(steps,), in_specs=[pl.BlockSpec(memory...  11.5 us
  transfers between devices with their start and end apart: 28, of which 11 were waited for; matrix products, arithmetic and copies ran while one was open for 10% of the time, Pallas kernels for 23%

profile of v2, /device:TPU:8, one launch (start us, length us, event | category | flops | bytes accessed | tf_op | source)
XLA Modules:
  0.0 212.7 jit_solution(11330006458486979947)
XLA Ops:
  8.0 1.9 pad_maximum_fusion
  9.8 1.6 collective-permute-start.3
  11.4 1.7 collective-permute-start.2
  13.1 4.0 %collective-permute-start = (bf16[64,1024]{1,0:T(8,128)(2,1)}, bf16[64,1024]{1,0:T(8,128)(2,1)S(1)}, u32[]{:S(2)}, u32[]{:S(2)}) collective-permute-start(bf16[64,1024]{1,0:T(8,128)(2,1)} %param.9), channel_id=1, source_target_pairs={{0,65},{1,64},{2,67},{3,66},{4,69},{5,68},{6,71},{7,70},{8,73},{9,... | collective-permute-start | bytes 393224 | tf_op jit(solution)/shard_map/ppermute | solution.py:428
  17.2 5.0 %collective-permute-done.1 = s32[512]{0:T(512)S(1)} collective-permute-done((s32[512]{0:T(512)}, s32[512]{0:T(512)S(1)}, u32[]{:S(2)}, u32[]{:S(2)}) %collective-permute-start.1) | collective-permute-done | bytes 2080 | tf_op jit(solution)/shard_map/ppermute | solution.py:428
  22.2 7.5 %collective-permute-done.3.refs_2_ = bf16[257,1408]{1,0:T(8,128)(2,1)S(1)} collective-permute-done((bf16[257,1408]{1,0:T(8,128)(2,1)}, bf16[257,1408]{1,0:T(8,128)(2,1)S(1)}, u32[]{:S(2)}, u32[]{:S(2)}) %collective-permute-start.3) | collective-permute-done | bytes 723744 | tf_op jit(solution)/shard_map/ppermute | solution.py:434
  31.7 2.6 %collective-permute-start.6 = (bf16[2,64,1024]{2,1,0:T(8,128)(2,1)S(1)}, bf16[2,64,1024]{2,1,0:T(8,128)(2,1)S(1)}, u32[]{:S(2)}, u32[]{:S(2)}) collective-permute-start(bf16[2,64,1024]{2,1,0:T(8,128)(2,1)S(1)} %pad_maximum_fusion.1.refs_0_), channel_id=1, source_target_pairs={{0,4},{1,5},{2,6},{3,7},{4,0},{5,1},{6,2},{7,3},{8,12},{9,13},{10,... | collective-permute-start | bytes 786440 | tf_op jit(solution)/shard_map/ppermute | solution.py:434
  34.3 1.1 collective-permute-start.5
  35.4 2.2 %collective-permute-start.4 = (bf16[2,64,1024]{2,1,0:T(8,128)(2,1)S(1)}, bf16[2,64,1024]{2,1,0:T(8,128)(2,1)S(1)}, u32[]{:S(2)}, u32[]{:S(2)}) collective-permute-start(bf16[2,64,1024]{2,1,0:T(8,128)(2,1)S(1)} %pad_maximum_fusion.1.refs_0_), channel_id=1, source_target_pairs={{0,6},{1,7},{2,0},{3,1},{4,2},{5,3},{6,4},{7,5},{8,14},{9,15},{10,... | collective-permute-start | bytes 786440 | tf_op jit(solution)/shard_map/ppermute | solution.py:434
  37.6 5.0 %collective-permute-done.6.refs_3_ = bf16[2,64,1024]{2,1,0:T(8,128)(2,1)S(1)} collective-permute-done((bf16[2,64,1024]{2,1,0:T(8,128)(2,1)S(1)}, bf16[2,64,1024]{2,1,0:T(8,128)(2,1)S(1)}, u32[]{:S(2)}, u32[]{:S(2)}) %collective-permute-start.6) | collective-permute-done | bytes 262176 | tf_op jit(solution)/shard_map/ppermute | solution.py:434
  43.3 2.8 %collective-permute-done.5.refs_2_ = bf16[2,64,1024]{2,1,0:T(8,128)(2,1)S(1)} collective-permute-done((bf16[2,64,1024]{2,1,0:T(8,128)(2,1)S(1)}, bf16[2,64,1024]{2,1,0:T(8,128)(2,1)S(1)}, u32[]{:S(2)}, u32[]{:S(2)}) %collective-permute-start.5) | collective-permute-done | bytes 262176 | tf_op jit(solution)/shard_map/ppermute | solution.py:434
  47.5 1.8 collective-permute-start.7
  50.1 4.1 %collective-permute-start.8 = (bf16[257,1408]{1,0:T(8,128)(2,1)S(1)}, bf16[257,1408]{1,0:T(8,128)(2,1)}, u32[]{:S(2)}, u32[]{:S(2)}) collective-permute-start(bf16[257,1408]{1,0:T(8,128)(2,1)S(1)} %bitcast.85), channel_id=1, source_target_pairs={{0,65},{1,64},{2,67},{3,66},{4,69},{5,68},{6,71},{7,70},{8,73},{9,... | collective-permute-start | bytes 2171144 | tf_op jit(solution)/shard_map/ppermute | solution.py:428
  54.2 1.6 copy-done
  55.8 0.9 copy-done.6
  56.7 1.0 copy-done.8
  57.7 0.9 copy-done.10
  58.7 2.2 %gather_units.1 = (bf16[8,64,1024]{2,1,0:T(8,128)(2,1)S(1)}, bf16[8,64,1024]{2,1,0:T(8,128)(2,1)S(1)}, bf16[16,64,1024]{2,1,0:T(8,128)(2,1)S(1)}, f32[8,64,1]{2,...) custom-call(s32[9]{0:T(128)S(1)} %stack.75.where_ref, ...), custom_call_target="tpu_custom_call" | custom-call | flops 6291456 | bytes 9437184 | tf_op jit(solution)/shard_map/gather_units/pallas_call | solution.py:245
  60.9 1.4 fusion.13
  62.5 1.5 copy-done.13
  64.7 2.8 %collective-permute-done.7.refs_0_ = bf16[257,1408]{1,0:T(8,128)(2,1)} collective-permute-done((bf16[257,1408]{1,0:T(8,128)(2,1)}, bf16[257,1408]{1,0:T(8,128)(2,1)}, u32[]{:S(2)}, u32[]{:S(2)}) %collective-permute-start.7) | collective-permute-done | bytes 723744 | tf_op jit(solution)/shard_map/ppermute | solution.py:434
  68.2 6.4 %all-to-all-start = ((f32[8,2,512]{2,1,0:T(2,128)}), f32[8,2,512]{2,1,0:T(2,128)S(1)}, u32[]{:S(2)}, u32[]{:S(2)}) async-start(f32[8,2,512]{2,1,0:T(2,128)} %broadcast_in_dim.23), calls=%async_computation | async-start | bytes 65536 | tf_op jit(solution)/shard_map/all_to_all | solution.py:34
  74.6 7.4 %all-to-all-done = f32[8,2,512]{2,1,0:T(2,128)S(1)} async-done(((f32[8,2,512]{2,1,0:T(2,128)}), f32[8,2,512]{2,1,0:T(2,128)S(1)}, u32[]{:S(2)}, u32[]{:S(2)}) %all-to-all-start) | async-done | bytes 32800 | tf_op jit(solution)/shard_map/all_to_all | solution.py:34
  82.6 2.7 %collective-permute-start.9 = (bf16[257,1408]{1,0:T(8,128)(2,1)}, bf16[257,1408]{1,0:T(8,128)(2,1)}, u32[]{:S(2)}, u32[]{:S(2)}) collective-permute-start(bf16[257,1408]{1,0:T(8,128)(2,1)} %collective-permute-done.8.refs_3_), channel_id=1, source_target_pairs={{0,6},{1,7},{2,0},{3,1},{4,2},{5,3},{6,4},{7,5},{8,14},{9,15},{10,... | collective-permute-start | bytes 2171144 | tf_op jit(solution)/shard_map/ppermute | solution.py:434
  86.0 4.9 %all-to-all-start.1 = ((f32[16,2,1024]{2,1,0:T(2,128)}), f32[16,2,1024]{2,1,0:T(2,128)S(1)}, u32[]{:S(2)}, u32[]{:S(2)}) async-start(f32[16,2,1024]{2,1,0:T(2,128)} %broadcast_in_dim.24), calls=%async_computation.1 | async-start | bytes 262144 | tf_op jit(solution)/shard_map/all_to_all | solution.py:34
  91.1 4.6 %all-to-all-done.1 = f32[16,2,1024]{2,1,0:T(2,128)S(1)} async-done(((f32[16,2,1024]{2,1,0:T(2,128)}), f32[16,2,1024]{2,1,0:T(2,128)S(1)}, u32[]{:S(2)}, u32[]{:S(2)}) %all-to-all-start.1) | async-done | bytes 131104 | tf_op jit(solution)/shard_map/all_to_all | solution.py:34
  95.7 3.6 %collective-permute-done.10.refs_2_ = bf16[257,1408]{1,0:T(8,128)(2,1)} collective-permute-done((bf16[257,1408]{1,0:T(8,128)(2,1)}, bf16[257,1408]{1,0:T(8,128)(2,1)}, u32[]{:S(2)}, u32[]{:S(2)}) %collective-permute-start.10) | collective-permute-done | bytes 723744 | tf_op jit(solution)/shard_map/ppermute | solution.py:434
  99.6 3.5 %subtract_convert_fusion.left_ref = bf16[512,1024]{1,0:T(8,128)(2,1)} fusion(f32[512,1024]{1,0:T(8,128)} %copy-done.13, s32[1024]{0:T(1024)S(1)} %iota_add_fusion, f32[1024]{0:T(1024)S(1)} %log_add_fusion, f32[512]{0:T(512)S(1)} %log_add_fusion.1, s32[512]{0:T(512)S(1)} %select_n.101), kind=kLoop, calls=%fused_computation.2 | loop fusion | flops 4194304 | bytes 3158016 | tf_op jit(solution)/shard_map/convert_element_type | solution.py:495
  103.2 6.0 %directions.3 = f32[16,64,1024]{2,1,0:T(8,128)} custom-call(bf16[512,1024]{1,0:T(8,128)(2,1)} %subtract_convert_fusion.left_ref, f32[16,64,1]{2,1,0:T(8,128)} %copy-done.4, bf16[512,1024]{1,0:T(8,128)(2,1)} %bitcast.76, bf16[16,64,1024]{2,1,0:T(8,128)(2,1)} %bitcast.70), custom_call_target="tpu_custom_call" | custom-call | flops 1073741824 | bytes 4194304 | tf_op jit(solution)/shard_map/directions/pallas_call | solution.py:310
  111.4 1.8 collective-permute-start.11
  115.8 3.7 %all-to-all-start.2 = ((f32[8,8,1024]{2,1,0:T(8,128)}), f32[8,8,1024]{2,1,0:T(8,128)S(1)}, u32[]{:S(2)}, u32[]{:S(2)}) async-start(f32[8,8,1024]{2,1,0:T(8,128)} %broadcast_in_dim.27), calls=%async_computation.2 | async-start | bytes 524288 | tf_op jit(solution)/shard_map/all_to_all | solution.py:34
  119.5 5.4 %directions.2 = bf16[8,64,1024]{2,1,0:T(8,128)(2,1)} custom-call(bf16[512,1024]{1,0:T(8,128)(2,1)} %subtract_convert_fusion.left_ref, f32[8,64,1]{2,1,0:T(8,128)} %copy-done.11, bf16[1024,1024]{1,0:T(8,128)(2,1)} %bitcast.74, bf16[8,64,1024]{2,1,0:T(8,128)(2,1)} %copy-done.3), custom_call_target="tpu_custom_call" | custom-call | flops 1073741824 | bytes 2097152 | tf_op jit(solution)/shard_map/directions/pallas_call | solution.py:310
  125.0 9.2 %encode.2 = (bf16[1408,1024]{1,0:T(8,128)(2,1)}, bf16[4,1,1408]{2,1,0:T(2,128)(2,1)}, f32[4,256,768]{2,1,0:T(8,128)}, f32[4,1,768]{2,1,0:T(1,128)}, f32[4,1,768]{2,1,0:T(1,128)}) custom-call(bf16[257,1408]{1,0:T(8,128)(2,1)} %bitcast.84, bf16[257,1408]{1,0:T(8,128)(2,1)} %copy-done.19, bf16[257,1408]{1,0:T(8,128)(2,1)} %copy-done.18, ...), custom_call_target="tpu_custom_call" | custom-call | flops 2223243264 | bytes 8947712 | tf_op jit(solution)/shard_map/encode/pallas_call | solution.py:98
  135.0 9.1 %encode.3 = (bf16[1408,1024]{1,0:T(8,128)(2,1)}, bf16[4,1,1408]{2,1,0:T(2,128)(2,1)}, f32[4,256,768]{2,1,0:T(8,128)}, f32[4,1,768]{2,1,0:T(1,128)}, f32[4,1,768]{2,1,0:T(1,128)}) custom-call(bf16[257,1408]{1,0:T(8,128)(2,1)} %collective-permute-done.7.refs_0_, bf16[257,1408]{1,0:T(8,128)(2,1)} %collective-permute-done.9.refs_1_, ...), custom_call_target="tpu_custom_call" | custom-call | flops 2223243264 | bytes 8947712 | tf_op jit(solution)/shard_map/encode/pallas_call | solution.py:98
  144.9 5.9 %head.1 = (bf16[16,8,2176]{2,1,0:T(8,128)(2,1)}, f32[8,1,768]{2,1,0:T(1,128)}) custom-call(s32[9]{0:T(128)} %concatenate.11.spots_ref, f32[1]{0:T(128)} %copy.30.temper_ref, f32[8,8,1024]{2,1,0:T(8,128)} %copy-done.17, f32[8,1024]{1,0:T(8,128)} %copy-done.12, f32[1,1408]{1,0:T(1,128)} %div.21.mean_ref, f32[4,1,768]{2,1,0:T(1,128)} %get-tuple-element.116.act_a, ...), custom_call_target="tpu_custom_call" | custom-call | flops 80740352 | bytes 5046272 | tf_op jit(solution)/shard_map/head/pallas_call | solution.py:382
  150.8 4.8 %all-to-all-start.3 = ((bf16[16,8,2176]{2,1,0:T(8,128)(2,1)}), bf16[16,8,2176]{2,1,0:T(8,128)(2,1)S(1)}, u32[]{:S(2)}, u32[]{:S(2)}) async-start(bf16[16,8,2176]{2,1,0:T(8,128)(2,1)} %get-tuple-element.120), calls=%async_computation.3 | async-start | bytes 1114112 | tf_op jit(solution)/shard_map/all_to_all | solution.py:529
  155.7 3.7 %collective-permute-start.14 = (bf16[2,64,1024]{2,1,0:T(8,128)(2,1)S(1)}, bf16[2,64,1024]{2,1,0:T(8,128)(2,1)}, u32[]{:S(2)}, u32[]{:S(2)}) collective-permute-start(bf16[2,64,1024]{2,1,0:T(8,128)(2,1)S(1)} %get-tuple-element.139), channel_id=1, source_target_pairs={{0,4},{1,5},{2,6},{3,7},{4,0},{5,1},{6,2},{7,3},{8,12},{9,13},{10,... | collective-permute-start | bytes 786440 | tf_op jit(solution)/shard_map/ppermute | solution.py:434
  159.9 2.7 %collective-permute-start.12 = (bf16[2,64,1024]{2,1,0:T(8,128)(2,1)S(1)}, bf16[2,64,1024]{2,1,0:T(8,128)(2,1)S(1)}, u32[]{:S(2)}, u32[]{:S(2)}) collective-permute-start(bf16[2,64,1024]{2,1,0:T(8,128)(2,1)S(1)} %get-tuple-element.141), channel_id=1, source_target_pairs={{0,6},{1,7},{2,0},{3,1},{4,2},{5,3},{6,4},{7,5},{8,14},{9,15},{10,... | collective-permute-start | bytes 786440 | tf_op jit(solution)/shard_map/ppermute | solution.py:434
  162.6 11.5 %weigh.1 = (f32[8,88,768]{2,1,0:T(8,128)}, bf16[8,88,768]{2,1,0:T(8,128)(2,1)}) custom-call(s32[1]{0:T(128)} %bitcast.1.core_ref, s32[8]{0:T(128)} %stack.74.order_ref, bf16[1408,1024]{1,0:T(8,128)(2,1)} %get-tuple-element.105.refs_0_, bf16[4,1,1408]{2,1,0:T(2,128)(2,1)} %get-tuple-element.106.refs_1_, f32[4,256,768]{2,1,0:T(8,128)} %get-tuple-element.107.refs_2_, ...), custom_call_target="tpu_custom_call" | custom-call | flops 4429185024 | bytes 12058624 | tf_op jit(solution)/shard_map/weigh/pallas_call | solution.py:178
  176.0 1.3 convert_add_fusion
  177.8 1.3 add_convert_fusion
  179.1 5.7 %all-to-all-start.4 = ((bf16[8,88,768]{2,1,0:T(8,128)(2,1)}), bf16[8,88,768]{2,1,0:T(8,128)(2,1)S(1)}, u32[]{:S(2)}, u32[]{:S(2)}) async-start(bf16[8,88,768]{2,1,0:T(8,128)(2,1)} %add_convert_fusion), calls=%async_computation.4 | async-start | bytes 2162688 | tf_op jit(solution)/shard_map/all_to_all | solution.py:552
  185.4 3.7 %collective-permute-start.16 = (bf16[64,1024]{1,0:T(8,128)(2,1)S(1)}, bf16[64,1024]{1,0:T(8,128)(2,1)S(1)}, u32[]{:S(2)}, u32[]{:S(2)}) collective-permute-start(bf16[64,1024]{1,0:T(8,128)(2,1)S(1)} %fusion.5), channel_id=1, source_target_pairs={{0,65},{1,64},{2,67},{3,66},{4,69},{5,68},{6,71},{7,70},{8,73},{9,... | collective-permute-start | bytes 393224 | tf_op jit(solution)/shard_map/ppermute | solution.py:428
  189.0 1.3 collective-permute-done.18
  190.4 3.6 %collective-permute-start.19 = (f32[128,88]{1,0:T(8,128)S(1)}, f32[128,88]{1,0:T(8,128)S(1)}, u32[]{:S(2)}, u32[]{:S(2)}) collective-permute-start(f32[128,88]{1,0:T(8,128)S(1)} %pad_maximum_fusion.2), channel_id=1, source_target_pairs={{0,1},{1,0},{2,3},{3,2},{4,5},{5,4},{6,7},{7,6},{8,9},{9,8},{10,11... | collective-permute-start | bytes 135176 | tf_op jit(solution)/shard_map/ppermute | solution.py:548
  194.8 7.7 %collective-permute-done.19 = f32[128,88]{1,0:T(8,128)S(1)} collective-permute-done((f32[128,88]{1,0:T(8,128)S(1)}, f32[128,88]{1,0:T(8,128)S(1)}, u32[]{:S(2)}, u32[]{:S(2)}) %collective-permute-start.19) | collective-permute-done | bytes 45088 | tf_op jit(solution)/shard_map/ppermute | solution.py:548
  202.6 1.0 fusion
  204.4 1.7 broadcast_multiply_fusion
  (122 shorter events, 19.9 us)
Async XLA Ops:
  7.2 42.9 %copy-start.15 = (bf16[1,257,1408]{2,1,0:T(8,128)(2,1)S(1)}, bf16[1,257,1408]{2,1,0:T(8,128)(2,1)}, u32[]{:S(2)}) copy-start(bf16[1,257,1408]{2,1,0:T(8,128)(2,1)} %param.13) | copy-start | bytes 2171140
  7.2 40.3 %all-gather.3.cloned.1.call-start = ((), (), s32[]{:S(2)}) async-start(), calls=%async_computation.6 | async-start | bytes 2228224 | tf_op jit(solution)/shard_map/all_gather | solution.py:439
  7.9 117.0 %all-gather.5.cloned.1.call-start = ((), (), s32[]{:S(2)}) async-start(), calls=%async_computation.7 | async-start | bytes 7659520 | tf_op jit(solution)/shard_map/all_gather | solution.py:440
  9.8 19.8 %collective-permute-start.3 = (bf16[257,1408]{1,0:T(8,128)(2,1)}, bf16[257,1408]{1,0:T(8,128)(2,1)S(1)}, u32[]{:S(2)}, u32[]{:S(2)}) collective-permute-start(bf16[257,1408]{1,0:T(8,128)(2,1)} %bitcast.81), channel_id=1, source_target_pairs={{0,2},{1,3},{2,4},{3,5},{4,6},{5,7},{6,0},{7,1},{8,10},{9,11},{10,... | collective-permute-start | bytes 2171144 | tf_op jit(solution)/shard_map/ppermute | solution.py:434
  11.4 18.3 %collective-permute-start.2 = (bf16[257,1408]{1,0:T(8,128)(2,1)}, bf16[257,1408]{1,0:T(8,128)(2,1)S(1)}, u32[]{:S(2)}, u32[]{:S(2)}) collective-permute-start(bf16[257,1408]{1,0:T(8,128)(2,1)} %bitcast.82), channel_id=1, source_target_pairs={{0,6},{1,7},{2,0},{3,1},{4,2},{5,3},{6,4},{7,5},{8,14},{9,15},{10,... | collective-permute-start | bytes 2171144 | tf_op jit(solution)/shard_map/ppermute | solution.py:434
  13.1 9.0 %collective-permute-start = (bf16[64,1024]{1,0:T(8,128)(2,1)}, bf16[64,1024]{1,0:T(8,128)(2,1)S(1)}, u32[]{:S(2)}, u32[]{:S(2)}) collective-permute-start(bf16[64,1024]{1,0:T(8,128)(2,1)} %param.9), channel_id=1, source_target_pairs={{0,65},{1,64},{2,67},{3,66},{4,69},{5,68},{6,71},{7,70},{8,73},{9,... | collective-permute-start | bytes 393224 | tf_op jit(solution)/shard_map/ppermute | solution.py:428
  17.2 5.0 %collective-permute-start.1 = (s32[512]{0:T(512)}, s32[512]{0:T(512)S(1)}, u32[]{:S(2)}, u32[]{:S(2)}) collective-permute-start(s32[512]{0:T(512)} %param.11), channel_id=1, source_target_pairs={{0,65},{1,64},{2,67},{3,66},{4,69},{5,68},{6,71},{7,70},{8,73},{9,... | collective-permute-start | bytes 6152 | tf_op jit(solution)/shard_map/ppermute | solution.py:428
  29.7 0.9 copy-start.18
  29.7 1.1 copy-start.19
  31.7 10.9 %collective-permute-start.6 = (bf16[2,64,1024]{2,1,0:T(8,128)(2,1)S(1)}, bf16[2,64,1024]{2,1,0:T(8,128)(2,1)S(1)}, u32[]{:S(2)}, u32[]{:S(2)}) collective-permute-start(bf16[2,64,1024]{2,1,0:T(8,128)(2,1)S(1)} %pad_maximum_fusion.1.refs_0_), channel_id=1, source_target_pairs={{0,4},{1,5},{2,6},{3,7},{4,0},{5,1},{6,2},{7,3},{8,12},{9,13},{10,... | collective-permute-start | bytes 786440 | tf_op jit(solution)/shard_map/ppermute | solution.py:434
  34.3 11.8 %collective-permute-start.5 = (bf16[2,64,1024]{2,1,0:T(8,128)(2,1)S(1)}, bf16[2,64,1024]{2,1,0:T(8,128)(2,1)S(1)}, u32[]{:S(2)}, u32[]{:S(2)}) collective-permute-start(bf16[2,64,1024]{2,1,0:T(8,128)(2,1)S(1)} %pad_maximum_fusion.1.refs_0_), channel_id=1, source_target_pairs={{0,2},{1,3},{2,4},{3,5},{4,6},{5,7},{6,0},{7,1},{8,10},{9,11},{10,... | collective-permute-start | bytes 786440 | tf_op jit(solution)/shard_map/ppermute | solution.py:434
  35.4 11.4 %collective-permute-start.4 = (bf16[2,64,1024]{2,1,0:T(8,128)(2,1)S(1)}, bf16[2,64,1024]{2,1,0:T(8,128)(2,1)S(1)}, u32[]{:S(2)}, u32[]{:S(2)}) collective-permute-start(bf16[2,64,1024]{2,1,0:T(8,128)(2,1)S(1)} %pad_maximum_fusion.1.refs_0_), channel_id=1, source_target_pairs={{0,6},{1,7},{2,0},{3,1},{4,2},{5,3},{6,4},{7,5},{8,14},{9,15},{10,... | collective-permute-start | bytes 786440 | tf_op jit(solution)/shard_map/ppermute | solution.py:434
  47.5 20.0 %collective-permute-start.7 = (bf16[257,1408]{1,0:T(8,128)(2,1)}, bf16[257,1408]{1,0:T(8,128)(2,1)}, u32[]{:S(2)}, u32[]{:S(2)}) collective-permute-start(bf16[257,1408]{1,0:T(8,128)(2,1)} %bitcast.83), channel_id=1, source_target_pairs={{0,4},{1,5},{2,6},{3,7},{4,0},{5,1},{6,2},{7,3},{8,12},{9,13},{10,... | collective-permute-start | bytes 2171144 | tf_op jit(solution)/shard_map/ppermute | solution.py:434
  50.1 24.6 %collective-permute-start.8 = (bf16[257,1408]{1,0:T(8,128)(2,1)S(1)}, bf16[257,1408]{1,0:T(8,128)(2,1)}, u32[]{:S(2)}, u32[]{:S(2)}) collective-permute-start(bf16[257,1408]{1,0:T(8,128)(2,1)S(1)} %bitcast.85), channel_id=1, source_target_pairs={{0,65},{1,64},{2,67},{3,66},{4,69},{5,68},{6,71},{7,70},{8,73},{9,... | collective-permute-start | bytes 2171144 | tf_op jit(solution)/shard_map/ppermute | solution.py:428
  54.2 1.6 copy-start
  55.8 0.9 copy-start.6
  56.7 1.0 copy-start.8
  57.7 0.9 copy-start.10
  60.9 1.4 copy-start.2
  60.9 1.4 copy-start.3
  60.9 1.5 copy-start.4
  60.9 1.5 copy-start.11
  60.9 1.5 copy-start.12
  60.9 53.8 %copy-start.1 = (bf16[16,64,1024]{2,1,0:T(8,128)(2,1)}, bf16[16,64,1024]{2,1,0:T(8,128)(2,1)S(1)}, u32[]{:S(2)}) copy-start(bf16[16,64,1024]{2,1,0:T(8,128)(2,1)S(1)} %get-tuple-element.78) | copy-start | bytes 6291460
  62.5 1.5 copy-start.13
  62.5 28.6 %copy-start.25 = (s32[512]{0:T(512)S(1)}, s32[512]{0:T(512)}, u32[]{:S(2)}) copy-start(s32[512]{0:T(512)} %param.11) | copy-start | bytes 6148
  68.2 13.9 %all-to-all-start = ((f32[8,2,512]{2,1,0:T(2,128)}), f32[8,2,512]{2,1,0:T(2,128)S(1)}, u32[]{:S(2)}, u32[]{:S(2)}) async-start(f32[8,2,512]{2,1,0:T(2,128)} %broadcast_in_dim.23), calls=%async_computation | async-start | bytes 65536 | tf_op jit(solution)/shard_map/all_to_all | solution.py:34
  82.1 17.3 %collective-permute-start.10 = (bf16[257,1408]{1,0:T(8,128)(2,1)}, bf16[257,1408]{1,0:T(8,128)(2,1)}, u32[]{:S(2)}, u32[]{:S(2)}) collective-permute-start(bf16[257,1408]{1,0:T(8,128)(2,1)} %collective-permute-done.8.refs_3_), channel_id=1, source_target_pairs={{0,2},{1,3},{2,4},{3,5},{4,6},{5,7},{6,0},{7,1},{8,10},{9,11},{10,... | collective-permute-start | bytes 2171144 | tf_op jit(solution)/shard_map/ppermute | solution.py:434
  82.6 16.7 %collective-permute-start.9 = (bf16[257,1408]{1,0:T(8,128)(2,1)}, bf16[257,1408]{1,0:T(8,128)(2,1)}, u32[]{:S(2)}, u32[]{:S(2)}) collective-permute-start(bf16[257,1408]{1,0:T(8,128)(2,1)} %collective-permute-done.8.refs_3_), channel_id=1, source_target_pairs={{0,6},{1,7},{2,0},{3,1},{4,2},{5,3},{6,4},{7,5},{8,14},{9,15},{10,... | collective-permute-start | bytes 2171144 | tf_op jit(solution)/shard_map/ppermute | solution.py:434
  86.0 9.7 %all-to-all-start.1 = ((f32[16,2,1024]{2,1,0:T(2,128)}), f32[16,2,1024]{2,1,0:T(2,128)S(1)}, u32[]{:S(2)}, u32[]{:S(2)}) async-start(f32[16,2,1024]{2,1,0:T(2,128)} %broadcast_in_dim.24), calls=%async_computation.1 | async-start | bytes 262144 | tf_op jit(solution)/shard_map/all_to_all | solution.py:34
  90.9 112.7 %reduce-scatter.2.cloned.1.call-start = ((), (), s32[]{:S(2)}) async-start(), calls=%async_computation.8 | async-start | bytes 4456448 | tf_op jit(solution)/shard_map/reduce_scatter | solution.py:501
  109.1 1.4 copy-start.24
  109.2 2.0 copy-start.21
  111.4 22.7 %collective-permute-start.11 = (bf16[257,1408]{1,0:T(8,128)(2,1)}, bf16[257,1408]{1,0:T(8,128)(2,1)S(1)}, u32[]{:S(2)}, u32[]{:S(2)}) collective-permute-start(bf16[257,1408]{1,0:T(8,128)(2,1)} %collective-permute-done.8.refs_3_), channel_id=1, source_target_pairs={{0,4},{1,5},{2,6},{3,7},{4,0},{5,1},{6,2},{7,3},{8,12},{9,13},{10,... | collective-permute-start | bytes 2171144 | tf_op jit(solution)/shard_map/ppermute | solution.py:434
  115.8 28.3 %all-to-all-start.2 = ((f32[8,8,1024]{2,1,0:T(8,128)}), f32[8,8,1024]{2,1,0:T(8,128)S(1)}, u32[]{:S(2)}, u32[]{:S(2)}) async-start(f32[8,8,1024]{2,1,0:T(8,128)} %broadcast_in_dim.27), calls=%async_computation.2 | async-start | bytes 524288 | tf_op jit(solution)/shard_map/all_to_all | solution.py:34
  144.9 10.7 %copy-start.14 = (bf16[8,64,1024]{2,1,0:T(8,128)(2,1)S(1)}, bf16[8,64,1024]{2,1,0:T(8,128)(2,1)}, u32[]{:S(2)}) copy-start(bf16[8,64,1024]{2,1,0:T(8,128)(2,1)} %directions.2) | copy-start | bytes 3145732
  150.8 23.3 %all-to-all-start.3 = ((bf16[16,8,2176]{2,1,0:T(8,128)(2,1)}), bf16[16,8,2176]{2,1,0:T(8,128)(2,1)S(1)}, u32[]{:S(2)}, u32[]{:S(2)}) async-start(bf16[16,8,2176]{2,1,0:T(8,128)(2,1)} %get-tuple-element.120), calls=%async_computation.3 | async-start | bytes 1114112 | tf_op jit(solution)/shard_map/all_to_all | solution.py:529
  155.7 18.4 %collective-permute-start.14 = (bf16[2,64,1024]{2,1,0:T(8,128)(2,1)S(1)}, bf16[2,64,1024]{2,1,0:T(8,128)(2,1)}, u32[]{:S(2)}, u32[]{:S(2)}) collective-permute-start(bf16[2,64,1024]{2,1,0:T(8,128)(2,1)S(1)} %get-tuple-element.139), channel_id=1, source_target_pairs={{0,4},{1,5},{2,6},{3,7},{4,0},{5,1},{6,2},{7,3},{8,12},{9,13},{10,... | collective-permute-start | bytes 786440 | tf_op jit(solution)/shard_map/ppermute | solution.py:434
  159.4 14.8 %collective-permute-start.13 = (bf16[2,64,1024]{2,1,0:T(8,128)(2,1)S(1)}, bf16[2,64,1024]{2,1,0:T(8,128)(2,1)}, u32[]{:S(2)}, u32[]{:S(2)}) collective-permute-start(bf16[2,64,1024]{2,1,0:T(8,128)(2,1)S(1)} %get-tuple-element.140), channel_id=1, source_target_pairs={{0,2},{1,3},{2,4},{3,5},{4,6},{5,7},{6,0},{7,1},{8,10},{9,11},{10,... | collective-permute-start | bytes 786440 | tf_op jit(solution)/shard_map/ppermute | solution.py:434
  159.9 14.2 %collective-permute-start.12 = (bf16[2,64,1024]{2,1,0:T(8,128)(2,1)S(1)}, bf16[2,64,1024]{2,1,0:T(8,128)(2,1)S(1)}, u32[]{:S(2)}, u32[]{:S(2)}) collective-permute-start(bf16[2,64,1024]{2,1,0:T(8,128)(2,1)S(1)} %get-tuple-element.141), channel_id=1, source_target_pairs={{0,6},{1,7},{2,0},{3,1},{4,2},{5,3},{6,4},{7,5},{8,14},{9,15},{10,... | collective-permute-start | bytes 786440 | tf_op jit(solution)/shard_map/ppermute | solution.py:434
  162.6 12.3 %copy-start.22 = (bf16[64,1024]{1,0:T(8,128)(2,1)S(1)}, bf16[64,1024]{1,0:T(8,128)(2,1)}, u32[]{:S(2)}) copy-start(bf16[64,1024]{1,0:T(8,128)(2,1)} %param.9) | copy-start | bytes 393220
  174.8 2.9 %collective-permute-start.15 = (bf16[8,88,768]{2,1,0:T(8,128)(2,1)}, bf16[8,88,768]{2,1,0:T(8,128)(2,1)S(1)}, u32[]{:S(2)}, u32[]{:S(2)}) collective-permute-start(bf16[8,88,768]{2,1,0:T(8,128)(2,1)} %get-tuple-element.122), channel_id=1, source_target_pairs={{0,8},{8,0},{16,24},{24,16},{32,40},{40,32},{48,56},{56,48},{64,72... | collective-permute-start | bytes 3244040 | tf_op jit(solution)/shard_map/ppermute | solution.py:531
  174.9 2.9 %copy-start.16 = (f32[8,88,768]{2,1,0:T(8,128)S(1)}, f32[8,88,768]{2,1,0:T(8,128)}, u32[]{:S(2)}) copy-start(f32[8,88,768]{2,1,0:T(8,128)} %get-tuple-element.128) | copy-start | bytes 6488068
  177.8 7.0 %collective-permute-start.17 = (f32[128,88]{1,0:T(8,128)S(1)}, f32[128,88]{1,0:T(8,128)S(1)}, u32[]{:S(2)}, u32[]{:S(2)}) collective-permute-start(f32[128,88]{1,0:T(8,128)S(1)} %convert_add_fusion.1), channel_id=1, source_target_pairs={{0,2},{1,3},{2,0},{3,1},{4,6},{5,7},{6,4},{7,5},{8,10},{9,11},{10,... | collective-permute-start | bytes 135176 | tf_op jit(solution)/shard_map/ppermute | solution.py:545
  179.1 24.5 %all-to-all-start.4 = ((bf16[8,88,768]{2,1,0:T(8,128)(2,1)}), bf16[8,88,768]{2,1,0:T(8,128)(2,1)S(1)}, u32[]{:S(2)}, u32[]{:S(2)}) async-start(bf16[8,88,768]{2,1,0:T(8,128)(2,1)} %add_convert_fusion), calls=%async_computation.4 | async-start | bytes 2162688 | tf_op jit(solution)/shard_map/all_to_all | solution.py:552
  184.8 5.6 %collective-permute-start.18 = (f32[128,88]{1,0:T(8,128)S(1)}, f32[128,88]{1,0:T(8,128)S(1)}, u32[]{:S(2)}, u32[]{:S(2)}) collective-permute-start(f32[128,88]{1,0:T(8,128)S(1)} %add.198), channel_id=1, source_target_pairs={{0,6},{1,7},{2,4},{3,5},{4,2},{5,3},{6,0},{7,1},{8,14},{9,15},{10,... | collective-permute-start | bytes 135176 | tf_op jit(solution)/shard_map/ppermute | solution.py:545
  185.4 8.7 %collective-permute-start.16 = (bf16[64,1024]{1,0:T(8,128)(2,1)S(1)}, bf16[64,1024]{1,0:T(8,128)(2,1)S(1)}, u32[]{:S(2)}, u32[]{:S(2)}) collective-permute-start(bf16[64,1024]{1,0:T(8,128)(2,1)S(1)} %fusion.5), channel_id=1, source_target_pairs={{0,65},{1,64},{2,67},{3,66},{4,69},{5,68},{6,71},{7,70},{8,73},{9,... | collective-permute-start | bytes 393224 | tf_op jit(solution)/shard_map/ppermute | solution.py:428
  190.4 12.2 %collective-permute-start.19 = (f32[128,88]{1,0:T(8,128)S(1)}, f32[128,88]{1,0:T(8,128)S(1)}, u32[]{:S(2)}, u32[]{:S(2)}) collective-permute-start(f32[128,88]{1,0:T(8,128)S(1)} %pad_maximum_fusion.2), channel_id=1, source_target_pairs={{0,1},{1,0},{2,3},{3,2},{4,5},{5,4},{6,7},{7,6},{8,9},{9,8},{10,11... | collective-permute-start | bytes 135176 | tf_op jit(solution)/shard_map/ppermute | solution.py:548
  (6 other events, 4.4 us)
Sparse Core Ops, SparseCore 0:
  9.7 36.0 all-gather.2
  47.5 46.6 all-gather.4
  109.3 63.7 reduce-scatter.1

commit v3 on v2

--- a/solution.py
+++ b/solution.py
@@ -245,7 +245,7 @@
     return pl.pallas_call(
         unit_kernel,
         in_specs=[pl.BlockSpec(memory_space=pltpu.SMEM)]
-        + [pl.BlockSpec(memory_space=pl.ANY)] * len(ring_img)
+        + [pl.BlockSpec(memory_space=pltpu.HBM)] * len(ring_img)
         + [pl.BlockSpec(memory_space=pltpu.HBM)],
         out_specs=[vmem] * 6,
         out_shape=[
@@ -309,7 +309,7 @@
     turned = [pltpu.VMEM(dlogit.shape[::-1], bf16)] if turn else []
     return pl.pallas_call(
         functools.partial(direction_kernel, turn),
-        in_specs=[vmem] * 2 + [pl.BlockSpec(memory_space=pl.ANY)] * 2,
+        in_specs=[vmem] * 2 + [hbm] * 2,
         out_specs=hbm,
         out_shape=jax.ShapeDtypeStruct(raw.shape, kind),
         scratch_shapes=[
@@ -454,6 +454,8 @@
     where = [((place + hop) % ring) * 2 + flag for hop in hops for flag in (side, 1 - side)]
     order = jnp.stack([where[k] for k in (0, 2, 4, 1, 6, 3, 5, 7)]).astype(jnp.int32)
     where = jnp.stack(where + [core]).astype(jnp.int32)
+    spots = jnp.concatenate((order, own_col[None]))
+    own_mean = jnp.mean(own_tok.astype(f32), axis=0, keepdims=True)
     raw_img, img_low, txt_low, img_inv, txt_inv, cached_raw = gather_units(where, ring_img, raw_txt)
     img_low = img_low.reshape(-1, emb)
     txt_low = txt_low.reshape(-1, emb)
@@ -472,10 +474,13 @@
     row_mass = jnp.sum(jnp.exp(logits - row_top[:, None]), axis=1)
     col_top = jnp.max(logits, axis=0)
     col_mass = jnp.sum(jnp.exp(logits - col_top[None, :]), axis=0)
-    row_top, row_mass, facing = lax.optimization_barrier((row_top, row_mass, facing))
+    row_top, row_mass, facing, order, spots, own_mean = lax.optimization_barrier(
+        (row_top, row_mass, facing, order, spots, own_mean)
+    )
     row_stats = share_rows(jnp.stack((row_top, row_mass)))
-    row_stats, other_tok = lax.optimization_barrier((row_stats, other_tok))
+    row_stats, other_tok, facing = lax.optimization_barrier((row_stats, other_tok, facing))
     far = [along(other_tok, hop) for hop in (1, 3)]
+    far_facing = across(facing)
     col_stats = share(jnp.stack((col_top, col_mass)), "dp")
     gain = norm_gain[None, :]
     first = encode([[own_tok], [near[0]], [near[1]], [other_tok]], gain, weights, hidden)
@@ -484,10 +489,9 @@
         peak = jnp.max(stats[:, 0], axis=0)
         return peak + jnp.log(jnp.sum(stats[:, 1] * jnp.exp(stats[:, 0] - peak), axis=0))
 
-    row_stats, col_stats, far, other_tok = lax.optimization_barrier(
-        (row_stats, col_stats, far, other_tok)
-    )
-    far_facing = along(other_tok, 2)
+    row_stats, col_stats, far, far_facing, first = lax.optimization_barrier(
+        (row_stats, col_stats, far, far_facing, first)
+    )
     row_lse = lse(row_stats)
     col_lse = lse(col_stats)
     dlogit = (
@@ -500,13 +504,9 @@
     txt_part = directions(True, dlogit, img_low, raw_txt, txt_inv, f32)
     txt_sum = lax.psum_scatter(txt_part.reshape(-1, emb), "dp", scatter_dimension=0, tiled=True)
     second = encode([[facing], [far[0]], [far[1]], [far_facing]], gain, weights, hidden)
-    own_mean = jnp.mean(own_tok.astype(f32), axis=0, keepdims=True)
-    spots = jnp.concatenate((order, own_col[None]))
     cached_all = share_rows(cached_part)
     img_part = directions(False, dlogit, txt_low, raw_img, img_inv, bf16)
-    cached_all, first, second, own_mean, img_part = lax.optimization_barrier(
-        (cached_all, first, second, own_mean, img_part)
-    )
+    cached_all, second, img_part = lax.optimization_barrier((cached_all, second, img_part))
     img_pairs = img_part.reshape(ring, 2, own_rows, emb)
 
     def to_place(hop):

time: 214 us -> 208 us (0.972)
  waiting for transfers between devices: 49.2 us -> 41.2 us
    ppermute x12 -> x11, waiting for transfers between devices: 21.8 us -> 16.9 us  [along(): lax.ppermute(piece, 'col', [(i, (i - 2 * hop) % cols) for i in range(cols)])]
    all_to_all x3, waiting for transfers between devices: 12 us -> 7.43 us  [share(): lax.all_to_all(copies, axis, 0, 0, axis_index_groups=groups, tiled=True)]
    all_to_all x3, starting transfers between devices: 15 us -> 18.2 us  [share(): lax.all_to_all(copies, axis, 0, 0, axis_index_groups=groups, tiled=True)]
    ppermute x12 -> x11, starting transfers between devices: 22.9 us -> 21 us  [along(): lax.ppermute(piece, 'col', [(i, (i - 2 * hop) % cols) for i in range(cols)])]
    ppermute x4 -> x5, starting transfers between devices: 11.9 us -> 12.5 us  [across(): return lax.ppermute(piece, both, list(enumerate(twin)))]
    unnamed x52 -> x58, local copies, waits for them, and re-layouts: 11.6 us -> 11.2 us
    ppermute x4 -> x5, waiting for transfers between devices: 4.98 us -> 4.98 us  [across(): return lax.ppermute(piece, both, list(enumerate(twin)))]
  transfers between devices with their start and end apart: 28 -> 28, of which waited for: 11 -> 9; matrix products, arithmetic and copies ran while one was open for 10% -> 8% of each run, Pallas kernels for 23% -> 21%
where the time goes in v3:
time: 208 us; the launch traced here: 206 us
  starting transfers between devices  66.3 us (32%)
  Pallas kernels  49.4 us (24%)
  waiting for transfers between devices  41.2 us (20%)
  local copies, waits for them, and re-layouts  17 us (8%)
  between operations  14.9 us (7%)
  other arithmetic  13.6 us (7%)
  matrix products  3.65 us (2%)
    ppermute x11, starting transfers between devices, along(): lax.ppermute(piece, 'col', [(i, (i - 2 * hop) % cols) for i in range(cols)])  21 us
    pallas_call x2, Pallas kernels, encode(): pl.pallas_call(functools.partial(encode_kernel, cuts), grid=(images,), in...  18.3 us
    all_to_all x3, starting transfers between devices, share(): lax.all_to_all(copies, axis, 0, 0, axis_index_groups=groups, tiled=True)  18.2 us
    ppermute x11, waiting for transfers between devices, along(): lax.ppermute(piece, 'col', [(i, (i - 2 * hop) % cols) for i in range(cols)])  16.9 us
    ppermute x5, starting transfers between devices, across(): return lax.ppermute(piece, both, list(enumerate(twin)))  12.5 us
    pallas_call x1, Pallas kernels, weigh(): pl.pallas_call(weigh_kernel, grid=(steps,), in_specs=[pl.BlockSpec(memory...  11.5 us
    pallas_call x2, Pallas kernels, directions(): pl.pallas_call(functools.partial(direction_kernel, turn), in_specs=[vmem]...  11.4 us
    unnamed x58, local copies, waits for them, and re-layouts  11.2 us
  transfers between devices with their start and end apart: 28, of which 9 were waited for; matrix products, arithmetic and copies ran while one was open for 8% of the time, Pallas kernels for 21%

profile of v3, /device:TPU:8, one launch (start us, length us, event | category | flops | bytes accessed | tf_op | source)
XLA Modules:
  0.0 206.0 jit_solution(2542711275449660417)
XLA Ops:
  8.0 1.9 pad_maximum_fusion
  9.8 1.6 collective-permute-start.3
  11.4 1.7 collective-permute-start.2
  13.2 4.0 %collective-permute-start = (bf16[64,1024]{1,0:T(8,128)(2,1)}, bf16[64,1024]{1,0:T(8,128)(2,1)S(1)}, u32[]{:S(2)}, u32[]{:S(2)}) collective-permute-start(bf16[64,1024]{1,0:T(8,128)(2,1)} %param.9), channel_id=1, source_target_pairs={{0,65},{1,64},{2,67},{3,66},{4,69},{5,68},{6,71},{7,70},{8,73},{9,... | collective-permute-start | bytes 393224 | tf_op jit(solution)/shard_map/ppermute | solution.py:428
  17.2 5.0 %collective-permute-done.1 = s32[512]{0:T(512)S(1)} collective-permute-done((s32[512]{0:T(512)}, s32[512]{0:T(512)S(1)}, u32[]{:S(2)}, u32[]{:S(2)}) %collective-permute-start.1) | collective-permute-done | bytes 2080 | tf_op jit(solution)/shard_map/ppermute | solution.py:428
  22.2 7.5 %collective-permute-done.3.refs_2_ = bf16[257,1408]{1,0:T(8,128)(2,1)S(1)} collective-permute-done((bf16[257,1408]{1,0:T(8,128)(2,1)}, bf16[257,1408]{1,0:T(8,128)(2,1)S(1)}, u32[]{:S(2)}, u32[]{:S(2)}) %collective-permute-start.3) | collective-permute-done | bytes 723744 | tf_op jit(solution)/shard_map/ppermute | solution.py:434
  29.7 1.0 copy-done.18
  30.9 0.9 pad_maximum_fusion.1.refs_0_
  31.8 2.6 %collective-permute-start.6 = (bf16[2,64,1024]{2,1,0:T(8,128)(2,1)S(1)}, bf16[2,64,1024]{2,1,0:T(8,128)(2,1)S(1)}, u32[]{:S(2)}, u32[]{:S(2)}) collective-permute-start(bf16[2,64,1024]{2,1,0:T(8,128)(2,1)S(1)} %pad_maximum_fusion.1.refs_0_), channel_id=1, source_target_pairs={{0,4},{1,5},{2,6},{3,7},{4,0},{5,1},{6,2},{7,3},{8,12},{9,13},{10,... | collective-permute-start | bytes 786440 | tf_op jit(solution)/shard_map/ppermute | solution.py:434
  34.4 1.1 collective-permute-start.5
  35.5 2.2 %collective-permute-start.4 = (bf16[2,64,1024]{2,1,0:T(8,128)(2,1)S(1)}, bf16[2,64,1024]{2,1,0:T(8,128)(2,1)S(1)}, u32[]{:S(2)}, u32[]{:S(2)}) collective-permute-start(bf16[2,64,1024]{2,1,0:T(8,128)(2,1)S(1)} %pad_maximum_fusion.1.refs_0_), channel_id=1, source_target_pairs={{0,6},{1,7},{2,0},{3,1},{4,2},{5,3},{6,4},{7,5},{8,14},{9,15},{10,... | collective-permute-start | bytes 786440 | tf_op jit(solution)/shard_map/ppermute | solution.py:434
  39.6 4.1 %collective-permute-start.8 = (bf16[257,1408]{1,0:T(8,128)(2,1)S(1)}, bf16[257,1408]{1,0:T(8,128)(2,1)}, u32[]{:S(2)}, u32[]{:S(2)}) collective-permute-start(bf16[257,1408]{1,0:T(8,128)(2,1)S(1)} %bitcast.84), channel_id=1, source_target_pairs={{0,65},{1,64},{2,67},{3,66},{4,69},{5,68},{6,71},{7,70},{8,73},{9,... | collective-permute-start | bytes 2171144 | tf_op jit(solution)/shard_map/ppermute | solution.py:428
  43.7 2.5 %collective-permute-done.5.refs_2_ = bf16[2,64,1024]{2,1,0:T(8,128)(2,1)S(1)} collective-permute-done((bf16[2,64,1024]{2,1,0:T(8,128)(2,1)S(1)}, bf16[2,64,1024]{2,1,0:T(8,128)(2,1)S(1)}, u32[]{:S(2)}, u32[]{:S(2)}) %collective-permute-start.5) | collective-permute-done | bytes 262176 | tf_op jit(solution)/shard_map/ppermute | solution.py:434
  46.9 1.8 collective-permute-start.7
  49.5 1.6 copy-done
  51.1 0.9 copy-done.6
  52.1 0.9 copy-done.8
  53.0 0.9 copy-done.10
  54.0 2.2 %gather_units.1 = (bf16[8,64,1024]{2,1,0:T(8,128)(2,1)S(1)}, bf16[8,64,1024]{2,1,0:T(8,128)(2,1)S(1)}, bf16[16,64,1024]{2,1,0:T(8,128)(2,1)S(1)}, f32[8,64,1]{2,...) custom-call(s32[9]{0:T(128)S(1)} %stack.74.where_ref, ...), custom_call_target="tpu_custom_call" | custom-call | flops 6291456 | bytes 9437184 | tf_op jit(solution)/shard_map/gather_units/pallas_call | solution.py:245
  56.2 1.4 fusion.13
  57.8 1.4 copy-done.13
  59.9 6.9 %collective-permute-done.7.refs_0_ = bf16[257,1408]{1,0:T(8,128)(2,1)S(1)} collective-permute-done((bf16[257,1408]{1,0:T(8,128)(2,1)S(1)}, bf16[257,1408]{1,0:T(8,128)(2,1)S(1)}, u32[]{:S(2)}, u32[]{:S(2)}) %collective-permute-start.7) | collective-permute-done | bytes 723744 | tf_op jit(solution)/shard_map/ppermute | solution.py:434
  68.3 6.5 %all-to-all-start = ((f32[8,2,512]{2,1,0:T(2,128)}), f32[8,2,512]{2,1,0:T(2,128)S(1)}, u32[]{:S(2)}, u32[]{:S(2)}) async-start(f32[8,2,512]{2,1,0:T(2,128)} %broadcast_in_dim.24), calls=%async_computation | async-start | bytes 65536 | tf_op jit(solution)/shard_map/all_to_all | solution.py:34
  74.8 7.4 %all-to-all-done = f32[8,2,512]{2,1,0:T(2,128)S(1)} async-done(((f32[8,2,512]{2,1,0:T(2,128)}), f32[8,2,512]{2,1,0:T(2,128)S(1)}, u32[]{:S(2)}, u32[]{:S(2)}) %all-to-all-start) | async-done | bytes 32800 | tf_op jit(solution)/shard_map/all_to_all | solution.py:34
  83.5 2.7 %collective-permute-start.9 = (bf16[257,1408]{1,0:T(8,128)(2,1)}, bf16[257,1408]{1,0:T(8,128)(2,1)}, u32[]{:S(2)}, u32[]{:S(2)}) collective-permute-start(bf16[257,1408]{1,0:T(8,128)(2,1)} %collective-permute-done.8.refs_3_), channel_id=1, source_target_pairs={{0,6},{1,7},{2,0},{3,1},{4,2},{5,3},{6,4},{7,5},{8,14},{9,15},{10,... | collective-permute-start | bytes 2171144 | tf_op jit(solution)/shard_map/ppermute | solution.py:434
  87.7 5.0 %all-to-all-start.1 = ((f32[16,2,1024]{2,1,0:T(2,128)}), f32[16,2,1024]{2,1,0:T(2,128)S(1)}, u32[]{:S(2)}, u32[]{:S(2)}) async-start(f32[16,2,1024]{2,1,0:T(2,128)} %broadcast_in_dim.25), calls=%async_computation.1 | async-start | bytes 262144 | tf_op jit(solution)/shard_map/all_to_all | solution.py:34
  92.9 1.4 all-gather.5.cloned.1.call-done.refs_5_.weights_hbm
  94.2 9.1 %encode.2 = (bf16[1408,1024]{1,0:T(8,128)(2,1)}, bf16[4,1,1408]{2,1,0:T(2,128)(2,1)}, f32[4,256,768]{2,1,0:T(8,128)}, f32[4,1,768]{2,1,0:T(1,128)}, f32[4,1,768]{2,1,0:T(1,128)}) custom-call(bf16[257,1408]{1,0:T(8,128)(2,1)} %bitcast.83, bf16[257,1408]{1,0:T(8,128)(2,1)} %copy-done.19, bf16[257,1408]{1,0:T(8,128)(2,1)} %copy-done.18, ...), custom_call_target="tpu_custom_call" | custom-call | flops 2223243264 | bytes 8947712 | tf_op jit(solution)/shard_map/encode/pallas_call | solution.py:98
  103.7 3.5 %subtract_convert_fusion.left_ref = bf16[512,1024]{1,0:T(8,128)(2,1)} fusion(f32[512,1024]{1,0:T(8,128)} %copy-done.13, s32[1024]{0:T(1024)S(1)} %iota_add_fusion, f32[1024]{0:T(1024)S(1)} %log_add_fusion, f32[512]{0:T(512)S(1)} %log_add_fusion.1, s32[512]{0:T(512)S(1)} %select_n.101), kind=kLoop, calls=%fused_computation.2 | loop fusion | flops 4194304 | bytes 3158016 | tf_op jit(solution)/shard_map/convert_element_type | solution.py:499
  107.1 6.0 %directions.3 = f32[16,64,1024]{2,1,0:T(8,128)} custom-call(bf16[512,1024]{1,0:T(8,128)(2,1)} %subtract_convert_fusion.left_ref, f32[16,64,1]{2,1,0:T(8,128)} %copy-done.4, bf16[512,1024]{1,0:T(8,128)(2,1)} %bitcast.76, bf16[16,64,1024]{2,1,0:T(8,128)(2,1)} %bitcast.70), custom_call_target="tpu_custom_call" | custom-call | flops 1073741824 | bytes 4194304 | tf_op jit(solution)/shard_map/directions/pallas_call | solution.py:310
  116.2 6.7 %all-to-all-start.2 = ((f32[8,8,1024]{2,1,0:T(8,128)}), f32[8,8,1024]{2,1,0:T(8,128)S(1)}, u32[]{:S(2)}, u32[]{:S(2)}) async-start(f32[8,8,1024]{2,1,0:T(8,128)} %broadcast_in_dim.29), calls=%async_computation.2 | async-start | bytes 524288 | tf_op jit(solution)/shard_map/all_to_all | solution.py:34
  122.9 5.5 %directions.2 = bf16[8,64,1024]{2,1,0:T(8,128)(2,1)} custom-call(bf16[512,1024]{1,0:T(8,128)(2,1)} %subtract_convert_fusion.left_ref, f32[8,64,1]{2,1,0:T(8,128)} %copy-done.11, bf16[1024,1024]{1,0:T(8,128)(2,1)} %bitcast.74, bf16[8,64,1024]{2,1,0:T(8,128)(2,1)} %copy-done.3), custom_call_target="tpu_custom_call" | custom-call | flops 1073741824 | bytes 2097152 | tf_op jit(solution)/shard_map/directions/pallas_call | solution.py:310
  128.4 9.2 %encode.3 = (bf16[1408,1024]{1,0:T(8,128)(2,1)}, bf16[4,1,1408]{2,1,0:T(2,128)(2,1)}, f32[4,256,768]{2,1,0:T(8,128)}, f32[4,1,768]{2,1,0:T(1,128)}, f32[4,1,768]{2,1,0:T(1,128)}) custom-call(bf16[257,1408]{1,0:T(8,128)(2,1)} %copy-done.20, bf16[257,1408]{1,0:T(8,128)(2,1)} %collective-permute-done.9.refs_1_, ...), custom_call_target="tpu_custom_call" | custom-call | flops 2223243264 | bytes 8947712 | tf_op jit(solution)/shard_map/encode/pallas_call | solution.py:98
  138.3 5.9 %head.1 = (bf16[16,8,2176]{2,1,0:T(8,128)(2,1)}, f32[8,1,768]{2,1,0:T(1,128)}) custom-call(s32[9]{0:T(128)} %concatenate.10.spots_ref, f32[1]{0:T(128)} %copy.30.temper_ref, f32[8,8,1024]{2,1,0:T(8,128)} %copy-done.17, f32[8,1024]{1,0:T(8,128)} %copy-done.12, f32[1,1408]{1,0:T(1,128)} %div.21.mean_ref, f32[4,1,768]{2,1,0:T(1,128)} %get-tuple-element.122.act_a, ...), custom_call_target="tpu_custom_call" | custom-call | flops 80740352 | bytes 5046272 | tf_op jit(solution)/shard_map/head/pallas_call | solution.py:382
  144.2 4.6 %all-to-all-start.3 = ((bf16[16,8,2176]{2,1,0:T(8,128)(2,1)}), bf16[16,8,2176]{2,1,0:T(8,128)(2,1)S(1)}, u32[]{:S(2)}, u32[]{:S(2)}) async-start(bf16[16,8,2176]{2,1,0:T(8,128)(2,1)} %get-tuple-element.126), calls=%async_computation.3 | async-start | bytes 1114112 | tf_op jit(solution)/shard_map/all_to_all | solution.py:529
  148.9 3.6 %collective-permute-start.14 = (bf16[2,64,1024]{2,1,0:T(8,128)(2,1)S(1)}, bf16[2,64,1024]{2,1,0:T(8,128)(2,1)S(1)}, u32[]{:S(2)}, u32[]{:S(2)}) collective-permute-start(bf16[2,64,1024]{2,1,0:T(8,128)(2,1)S(1)} %get-tuple-element.145), channel_id=1, source_target_pairs={{0,4},{1,5},{2,6},{3,7},{4,0},{5,1},{6,2},{7,3},{8,12},{9,13},{10,... | collective-permute-start | bytes 786440 | tf_op jit(solution)/shard_map/ppermute | solution.py:434
  153.1 2.7 %collective-permute-start.12 = (bf16[2,64,1024]{2,1,0:T(8,128)(2,1)S(1)}, bf16[2,64,1024]{2,1,0:T(8,128)(2,1)S(1)}, u32[]{:S(2)}, u32[]{:S(2)}) collective-permute-start(bf16[2,64,1024]{2,1,0:T(8,128)(2,1)S(1)} %get-tuple-element.147), channel_id=1, source_target_pairs={{0,6},{1,7},{2,0},{3,1},{4,2},{5,3},{6,4},{7,5},{8,14},{9,15},{10,... | collective-permute-start | bytes 786440 | tf_op jit(solution)/shard_map/ppermute | solution.py:434
  155.7 11.5 %weigh.1 = (f32[8,88,768]{2,1,0:T(8,128)}, bf16[8,88,768]{2,1,0:T(8,128)(2,1)}) custom-call(s32[1]{0:T(128)} %bitcast.1.core_ref, s32[8]{0:T(128)} %stack.78.order_ref, bf16[1408,1024]{1,0:T(8,128)(2,1)} %get-tuple-element.97.refs_0_, bf16[4,1,1408]{2,1,0:T(2,128)(2,1)} %get-tuple-element.98.refs_1_, f32[4,256,768]{2,1,0:T(8,128)} %get-tuple-element.99.refs_2_, ...), custom_call_target="tpu_custom_call" | custom-call | flops 4429185024 | bytes 12058624 | tf_op jit(solution)/shard_map/weigh/pallas_call | solution.py:178
  168.3 0.9 fusion.3
  169.2 1.3 convert_add_fusion
  171.1 1.3 add_convert_fusion
  172.4 5.7 %all-to-all-start.4 = ((bf16[8,88,768]{2,1,0:T(8,128)(2,1)}), bf16[8,88,768]{2,1,0:T(8,128)(2,1)S(1)}, u32[]{:S(2)}, u32[]{:S(2)}) async-start(bf16[8,88,768]{2,1,0:T(8,128)(2,1)} %add_convert_fusion), calls=%async_computation.4 | async-start | bytes 2162688 | tf_op jit(solution)/shard_map/all_to_all | solution.py:552
  178.5 3.7 %collective-permute-start.16 = (bf16[64,1024]{1,0:T(8,128)(2,1)S(1)}, bf16[64,1024]{1,0:T(8,128)(2,1)S(1)}, u32[]{:S(2)}, u32[]{:S(2)}) collective-permute-start(bf16[64,1024]{1,0:T(8,128)(2,1)S(1)} %fusion.5), channel_id=1, source_target_pairs={{0,65},{1,64},{2,67},{3,66},{4,69},{5,68},{6,71},{7,70},{8,73},{9,... | collective-permute-start | bytes 393224 | tf_op jit(solution)/shard_map/ppermute | solution.py:428
  182.2 1.5 collective-permute-done.18
  183.7 3.6 %collective-permute-start.19 = (f32[128,88]{1,0:T(8,128)S(1)}, f32[128,88]{1,0:T(8,128)S(1)}, u32[]{:S(2)}, u32[]{:S(2)}) collective-permute-start(f32[128,88]{1,0:T(8,128)S(1)} %pad_maximum_fusion.2), channel_id=1, source_target_pairs={{0,1},{1,0},{2,3},{3,2},{4,5},{5,4},{6,7},{7,6},{8,9},{9,8},{10,11... | collective-permute-start | bytes 135176 | tf_op jit(solution)/shard_map/ppermute | solution.py:548
  188.1 7.7 %collective-permute-done.19 = f32[128,88]{1,0:T(8,128)S(1)} collective-permute-done((f32[128,88]{1,0:T(8,128)S(1)}, f32[128,88]{1,0:T(8,128)S(1)}, u32[]{:S(2)}, u32[]{:S(2)}) %collective-permute-start.19) | collective-permute-done | bytes 45088 | tf_op jit(solution)/shard_map/ppermute | solution.py:548
  195.9 1.0 fusion
  197.7 1.7 broadcast_multiply_fusion
  (128 shorter events, 17.5 us)
Async XLA Ops:
  7.2 32.4 %copy-start.15 = (bf16[1,257,1408]{2,1,0:T(8,128)(2,1)S(1)}, bf16[1,257,1408]{2,1,0:T(8,128)(2,1)}, u32[]{:S(2)}) copy-start(bf16[1,257,1408]{2,1,0:T(8,128)(2,1)} %param.13) | copy-start | bytes 2171140
  7.2 39.8 %all-gather.3.cloned.1.call-start = ((), (), s32[]{:S(2)}) async-start(), calls=%async_computation.6 | async-start | bytes 2228224 | tf_op jit(solution)/shard_map/all_gather | solution.py:439
  7.9 86.3 %all-gather.5.cloned.1.call-start = ((), (), s32[]{:S(2)}) async-start(), calls=%async_computation.7 | async-start | bytes 7659520 | tf_op jit(solution)/shard_map/all_gather | solution.py:440
  9.8 19.8 %collective-permute-start.3 = (bf16[257,1408]{1,0:T(8,128)(2,1)}, bf16[257,1408]{1,0:T(8,128)(2,1)S(1)}, u32[]{:S(2)}, u32[]{:S(2)}) collective-permute-start(bf16[257,1408]{1,0:T(8,128)(2,1)} %bitcast.81), channel_id=1, source_target_pairs={{0,2},{1,3},{2,4},{3,5},{4,6},{5,7},{6,0},{7,1},{8,10},{9,11},{10,... | collective-permute-start | bytes 2171144 | tf_op jit(solution)/shard_map/ppermute | solution.py:434
  11.4 18.3 %collective-permute-start.2 = (bf16[257,1408]{1,0:T(8,128)(2,1)}, bf16[257,1408]{1,0:T(8,128)(2,1)S(1)}, u32[]{:S(2)}, u32[]{:S(2)}) collective-permute-start(bf16[257,1408]{1,0:T(8,128)(2,1)} %bitcast.82), channel_id=1, source_target_pairs={{0,6},{1,7},{2,0},{3,1},{4,2},{5,3},{6,4},{7,5},{8,14},{9,15},{10,... | collective-permute-start | bytes 2171144 | tf_op jit(solution)/shard_map/ppermute | solution.py:434
  13.2 9.0 %collective-permute-start = (bf16[64,1024]{1,0:T(8,128)(2,1)}, bf16[64,1024]{1,0:T(8,128)(2,1)S(1)}, u32[]{:S(2)}, u32[]{:S(2)}) collective-permute-start(bf16[64,1024]{1,0:T(8,128)(2,1)} %param.9), channel_id=1, source_target_pairs={{0,65},{1,64},{2,67},{3,66},{4,69},{5,68},{6,71},{7,70},{8,73},{9,... | collective-permute-start | bytes 393224 | tf_op jit(solution)/shard_map/ppermute | solution.py:428
  17.2 5.0 %collective-permute-start.1 = (s32[512]{0:T(512)}, s32[512]{0:T(512)S(1)}, u32[]{:S(2)}, u32[]{:S(2)}) collective-permute-start(s32[512]{0:T(512)} %param.11), channel_id=1, source_target_pairs={{0,65},{1,64},{2,67},{3,66},{4,69},{5,68},{6,71},{7,70},{8,73},{9,... | collective-permute-start | bytes 6152 | tf_op jit(solution)/shard_map/ppermute | solution.py:428
  29.7 1.0 copy-start.18
  29.7 1.2 copy-start.19
  31.8 11.9 %collective-permute-start.6 = (bf16[2,64,1024]{2,1,0:T(8,128)(2,1)S(1)}, bf16[2,64,1024]{2,1,0:T(8,128)(2,1)S(1)}, u32[]{:S(2)}, u32[]{:S(2)}) collective-permute-start(bf16[2,64,1024]{2,1,0:T(8,128)(2,1)S(1)} %pad_maximum_fusion.1.refs_0_), channel_id=1, source_target_pairs={{0,4},{1,5},{2,6},{3,7},{4,0},{5,1},{6,2},{7,3},{8,12},{9,13},{10,... | collective-permute-start | bytes 786440 | tf_op jit(solution)/shard_map/ppermute | solution.py:434
  34.4 11.8 %collective-permute-start.5 = (bf16[2,64,1024]{2,1,0:T(8,128)(2,1)S(1)}, bf16[2,64,1024]{2,1,0:T(8,128)(2,1)S(1)}, u32[]{:S(2)}, u32[]{:S(2)}) collective-permute-start(bf16[2,64,1024]{2,1,0:T(8,128)(2,1)S(1)} %pad_maximum_fusion.1.refs_0_), channel_id=1, source_target_pairs={{0,2},{1,3},{2,4},{3,5},{4,6},{5,7},{6,0},{7,1},{8,10},{9,11},{10,... | collective-permute-start | bytes 786440 | tf_op jit(solution)/shard_map/ppermute | solution.py:434
  35.5 10.7 %collective-permute-start.4 = (bf16[2,64,1024]{2,1,0:T(8,128)(2,1)S(1)}, bf16[2,64,1024]{2,1,0:T(8,128)(2,1)S(1)}, u32[]{:S(2)}, u32[]{:S(2)}) collective-permute-start(bf16[2,64,1024]{2,1,0:T(8,128)(2,1)S(1)} %pad_maximum_fusion.1.refs_0_), channel_id=1, source_target_pairs={{0,6},{1,7},{2,0},{3,1},{4,2},{5,3},{6,4},{7,5},{8,14},{9,15},{10,... | collective-permute-start | bytes 786440 | tf_op jit(solution)/shard_map/ppermute | solution.py:434
  39.6 35.2 %collective-permute-start.8 = (bf16[257,1408]{1,0:T(8,128)(2,1)S(1)}, bf16[257,1408]{1,0:T(8,128)(2,1)}, u32[]{:S(2)}, u32[]{:S(2)}) collective-permute-start(bf16[257,1408]{1,0:T(8,128)(2,1)S(1)} %bitcast.84), channel_id=1, source_target_pairs={{0,65},{1,64},{2,67},{3,66},{4,69},{5,68},{6,71},{7,70},{8,73},{9,... | collective-permute-start | bytes 2171144 | tf_op jit(solution)/shard_map/ppermute | solution.py:428
  43.7 5.8 %copy-start.5 = (bf16[2,64,1024]{2,1,0:T(8,128)(2,1)}, bf16[2,64,1024]{2,1,0:T(8,128)(2,1)S(1)}, u32[]{:S(2)}) copy-start(bf16[2,64,1024]{2,1,0:T(8,128)(2,1)S(1)} %collective-permute-done.6.refs_3_) | copy-start | bytes 786436
  46.2 3.3 %copy-start.7 = (bf16[2,64,1024]{2,1,0:T(8,128)(2,1)}, bf16[2,64,1024]{2,1,0:T(8,128)(2,1)S(1)}, u32[]{:S(2)}) copy-start(bf16[2,64,1024]{2,1,0:T(8,128)(2,1)S(1)} %collective-permute-done.5.refs_2_) | copy-start | bytes 786436
  46.9 19.8 %collective-permute-start.7 = (bf16[257,1408]{1,0:T(8,128)(2,1)S(1)}, bf16[257,1408]{1,0:T(8,128)(2,1)S(1)}, u32[]{:S(2)}, u32[]{:S(2)}) collective-permute-start(bf16[257,1408]{1,0:T(8,128)(2,1)S(1)} %bitcast.85), channel_id=1, source_target_pairs={{0,4},{1,5},{2,6},{3,7},{4,0},{5,1},{6,2},{7,3},{8,12},{9,13},{10,... | collective-permute-start | bytes 2171144 | tf_op jit(solution)/shard_map/ppermute | solution.py:434
  49.5 1.6 copy-start
  56.2 1.4 copy-start.2
  56.2 1.4 copy-start.3
  56.2 1.5 copy-start.4
  56.2 1.5 copy-start.11
  56.2 1.5 copy-start.12
  56.2 58.8 %copy-start.1 = (bf16[16,64,1024]{2,1,0:T(8,128)(2,1)}, bf16[16,64,1024]{2,1,0:T(8,128)(2,1)S(1)}, u32[]{:S(2)}) copy-start(bf16[16,64,1024]{2,1,0:T(8,128)(2,1)S(1)} %get-tuple-element.81) | copy-start | bytes 6291460
  57.7 1.4 copy-start.13
  57.7 28.6 %copy-start.27 = (f32[1408]{0:T(1024)S(1)}, f32[1408]{0:T(1024)}, u32[]{:S(2)}) copy-start(f32[1408]{0:T(1024)} %param.14) | copy-start | bytes 16900
  57.8 29.2 %copy-start.28 = (s32[512]{0:T(512)S(1)}, s32[512]{0:T(512)}, u32[]{:S(2)}) copy-start(s32[512]{0:T(512)} %param.11) | copy-start | bytes 6148
  68.3 14.0 %all-to-all-start = ((f32[8,2,512]{2,1,0:T(2,128)}), f32[8,2,512]{2,1,0:T(2,128)S(1)}, u32[]{:S(2)}, u32[]{:S(2)}) async-start(f32[8,2,512]{2,1,0:T(2,128)} %broadcast_in_dim.24), calls=%async_computation | async-start | bytes 65536 | tf_op jit(solution)/shard_map/all_to_all | solution.py:34
  82.3 21.1 %collective-permute-start.11 = (bf16[257,1408]{1,0:T(8,128)(2,1)}, bf16[257,1408]{1,0:T(8,128)(2,1)S(1)}, u32[]{:S(2)}, u32[]{:S(2)}) collective-permute-start(bf16[257,1408]{1,0:T(8,128)(2,1)} %copy-done.20), channel_id=1, source_target_pairs={{0,65},{1,64},{2,67},{3,66},{4,69},{5,68},{6,71},{7,70},{8,73},{9,... | collective-permute-start | bytes 2171144 | tf_op jit(solution)/shard_map/ppermute | solution.py:428
  83.0 20.4 %collective-permute-start.10 = (bf16[257,1408]{1,0:T(8,128)(2,1)}, bf16[257,1408]{1,0:T(8,128)(2,1)}, u32[]{:S(2)}, u32[]{:S(2)}) collective-permute-start(bf16[257,1408]{1,0:T(8,128)(2,1)} %collective-permute-done.8.refs_3_), channel_id=1, source_target_pairs={{0,2},{1,3},{2,4},{3,5},{4,6},{5,7},{6,0},{7,1},{8,10},{9,11},{10,... | collective-permute-start | bytes 2171144 | tf_op jit(solution)/shard_map/ppermute | solution.py:434
  83.5 19.8 %collective-permute-start.9 = (bf16[257,1408]{1,0:T(8,128)(2,1)}, bf16[257,1408]{1,0:T(8,128)(2,1)}, u32[]{:S(2)}, u32[]{:S(2)}) collective-permute-start(bf16[257,1408]{1,0:T(8,128)(2,1)} %collective-permute-done.8.refs_3_), channel_id=1, source_target_pairs={{0,6},{1,7},{2,0},{3,1},{4,2},{5,3},{6,4},{7,5},{8,14},{9,15},{10,... | collective-permute-start | bytes 2171144 | tf_op jit(solution)/shard_map/ppermute | solution.py:434
  87.7 15.6 %all-to-all-start.1 = ((f32[16,2,1024]{2,1,0:T(2,128)}), f32[16,2,1024]{2,1,0:T(2,128)S(1)}, u32[]{:S(2)}, u32[]{:S(2)}) async-start(f32[16,2,1024]{2,1,0:T(2,128)} %broadcast_in_dim.25), calls=%async_computation.1 | async-start | bytes 262144 | tf_op jit(solution)/shard_map/all_to_all | solution.py:34
  92.6 104.2 %reduce-scatter.2.cloned.1.call-start = ((), (), s32[]{:S(2)}) async-start(), calls=%async_computation.8 | async-start | bytes 4456448 | tf_op jit(solution)/shard_map/reduce_scatter | solution.py:505
  103.3 9.8 %copy-start.21 = (bf16[257,1408]{1,0:T(8,128)(2,1)}, bf16[257,1408]{1,0:T(8,128)(2,1)S(1)}, u32[]{:S(2)}) copy-start(bf16[257,1408]{1,0:T(8,128)(2,1)S(1)} %collective-permute-done.11.refs_3_) | copy-start | bytes 2171140
  116.2 21.4 %all-to-all-start.2 = ((f32[8,8,1024]{2,1,0:T(8,128)}), f32[8,8,1024]{2,1,0:T(8,128)S(1)}, u32[]{:S(2)}, u32[]{:S(2)}) async-start(f32[8,8,1024]{2,1,0:T(8,128)} %broadcast_in_dim.29), calls=%async_computation.2 | async-start | bytes 524288 | tf_op jit(solution)/shard_map/all_to_all | solution.py:34
  138.3 10.5 %copy-start.14 = (bf16[8,64,1024]{2,1,0:T(8,128)(2,1)S(1)}, bf16[8,64,1024]{2,1,0:T(8,128)(2,1)}, u32[]{:S(2)}) copy-start(bf16[8,64,1024]{2,1,0:T(8,128)(2,1)} %directions.2) | copy-start | bytes 3145732
  144.2 23.1 %all-to-all-start.3 = ((bf16[16,8,2176]{2,1,0:T(8,128)(2,1)}), bf16[16,8,2176]{2,1,0:T(8,128)(2,1)S(1)}, u32[]{:S(2)}, u32[]{:S(2)}) async-start(bf16[16,8,2176]{2,1,0:T(8,128)(2,1)} %get-tuple-element.126), calls=%async_computation.3 | async-start | bytes 1114112 | tf_op jit(solution)/shard_map/all_to_all | solution.py:529
  148.9 18.3 %collective-permute-start.14 = (bf16[2,64,1024]{2,1,0:T(8,128)(2,1)S(1)}, bf16[2,64,1024]{2,1,0:T(8,128)(2,1)S(1)}, u32[]{:S(2)}, u32[]{:S(2)}) collective-permute-start(bf16[2,64,1024]{2,1,0:T(8,128)(2,1)S(1)} %get-tuple-element.145), channel_id=1, source_target_pairs={{0,4},{1,5},{2,6},{3,7},{4,0},{5,1},{6,2},{7,3},{8,12},{9,13},{10,... | collective-permute-start | bytes 786440 | tf_op jit(solution)/shard_map/ppermute | solution.py:434
  152.5 14.8 %collective-permute-start.13 = (bf16[2,64,1024]{2,1,0:T(8,128)(2,1)S(1)}, bf16[2,64,1024]{2,1,0:T(8,128)(2,1)S(1)}, u32[]{:S(2)}, u32[]{:S(2)}) collective-permute-start(bf16[2,64,1024]{2,1,0:T(8,128)(2,1)S(1)} %get-tuple-element.146), channel_id=1, source_target_pairs={{0,2},{1,3},{2,4},{3,5},{4,6},{5,7},{6,0},{7,1},{8,10},{9,11},{10,... | collective-permute-start | bytes 786440 | tf_op jit(solution)/shard_map/ppermute | solution.py:434
  153.1 14.2 %collective-permute-start.12 = (bf16[2,64,1024]{2,1,0:T(8,128)(2,1)S(1)}, bf16[2,64,1024]{2,1,0:T(8,128)(2,1)S(1)}, u32[]{:S(2)}, u32[]{:S(2)}) collective-permute-start(bf16[2,64,1024]{2,1,0:T(8,128)(2,1)S(1)} %get-tuple-element.147), channel_id=1, source_target_pairs={{0,6},{1,7},{2,0},{3,1},{4,2},{5,3},{6,4},{7,5},{8,14},{9,15},{10,... | collective-permute-start | bytes 786440 | tf_op jit(solution)/shard_map/ppermute | solution.py:434
  155.7 12.4 %copy-start.23 = (bf16[64,1024]{1,0:T(8,128)(2,1)S(1)}, bf16[64,1024]{1,0:T(8,128)(2,1)}, u32[]{:S(2)}) copy-start(bf16[64,1024]{1,0:T(8,128)(2,1)} %param.9) | copy-start | bytes 393220
  167.2 1.1 copy-start.24
  168.1 3.0 %collective-permute-start.15 = (bf16[8,88,768]{2,1,0:T(8,128)(2,1)}, bf16[8,88,768]{2,1,0:T(8,128)(2,1)S(1)}, u32[]{:S(2)}, u32[]{:S(2)}) collective-permute-start(bf16[8,88,768]{2,1,0:T(8,128)(2,1)} %get-tuple-element.128), channel_id=1, source_target_pairs={{0,8},{8,0},{16,24},{24,16},{32,40},{40,32},{48,56},{56,48},{64,72... | collective-permute-start | bytes 3244040 | tf_op jit(solution)/shard_map/ppermute | solution.py:531
  168.1 3.0 %copy-start.16 = (f32[8,88,768]{2,1,0:T(8,128)S(1)}, f32[8,88,768]{2,1,0:T(8,128)}, u32[]{:S(2)}) copy-start(f32[8,88,768]{2,1,0:T(8,128)} %get-tuple-element.134) | copy-start | bytes 6488068
  171.1 7.0 %collective-permute-start.17 = (f32[128,88]{1,0:T(8,128)S(1)}, f32[128,88]{1,0:T(8,128)S(1)}, u32[]{:S(2)}, u32[]{:S(2)}) collective-permute-start(f32[128,88]{1,0:T(8,128)S(1)} %convert_add_fusion.1), channel_id=1, source_target_pairs={{0,2},{1,3},{2,0},{3,1},{4,6},{5,7},{6,4},{7,5},{8,10},{9,11},{10,... | collective-permute-start | bytes 135176 | tf_op jit(solution)/shard_map/ppermute | solution.py:545
  172.4 24.4 %all-to-all-start.4 = ((bf16[8,88,768]{2,1,0:T(8,128)(2,1)}), bf16[8,88,768]{2,1,0:T(8,128)(2,1)S(1)}, u32[]{:S(2)}, u32[]{:S(2)}) async-start(bf16[8,88,768]{2,1,0:T(8,128)(2,1)} %add_convert_fusion), calls=%async_computation.4 | async-start | bytes 2162688 | tf_op jit(solution)/shard_map/all_to_all | solution.py:552
  178.1 5.6 %collective-permute-start.18 = (f32[128,88]{1,0:T(8,128)S(1)}, f32[128,88]{1,0:T(8,128)S(1)}, u32[]{:S(2)}, u32[]{:S(2)}) collective-permute-start(f32[128,88]{1,0:T(8,128)S(1)} %add.198), channel_id=1, source_target_pairs={{0,6},{1,7},{2,4},{3,5},{4,2},{5,3},{6,0},{7,1},{8,14},{9,15},{10,... | collective-permute-start | bytes 135176 | tf_op jit(solution)/shard_map/ppermute | solution.py:545
  178.5 8.8 %collective-permute-start.16 = (bf16[64,1024]{1,0:T(8,128)(2,1)S(1)}, bf16[64,1024]{1,0:T(8,128)(2,1)S(1)}, u32[]{:S(2)}, u32[]{:S(2)}) collective-permute-start(bf16[64,1024]{1,0:T(8,128)(2,1)S(1)} %fusion.5), channel_id=1, source_target_pairs={{0,65},{1,64},{2,67},{3,66},{4,69},{5,68},{6,71},{7,70},{8,73},{9,... | collective-permute-start | bytes 393224 | tf_op jit(solution)/shard_map/ppermute | solution.py:428
  183.7 12.2 %collective-permute-start.19 = (f32[128,88]{1,0:T(8,128)S(1)}, f32[128,88]{1,0:T(8,128)S(1)}, u32[]{:S(2)}, u32[]{:S(2)}) collective-permute-start(f32[128,88]{1,0:T(8,128)S(1)} %pad_maximum_fusion.2), channel_id=1, source_target_pairs={{0,1},{1,0},{2,3},{3,2},{4,5},{5,4},{6,7},{7,6},{8,9},{9,8},{10,11... | collective-permute-start | bytes 135176 | tf_op jit(solution)/shard_map/ppermute | solution.py:548
  (9 other events, 7.7 us)
Sparse Core Ops, SparseCore 0:
  9.7 36.0 all-gather.2
  47.5 46.6 all-gather.4
  113.3 69.7 reduce-scatter.1

commit v4 on v3

--- a/solution.py
+++ b/solution.py
@@ -81,7 +81,7 @@
     half = 0.5 * (1.0 + lax.erf(pre * root_half))
     act_ref[0] = jnp.sum(pre * half, axis=0, keepdims=True) * (1.0 / seq)
     slope = half + pre * jnp.exp(-0.5 * pre * pre) * inv_root_two_pi
-    slope_ref[0] = slope[: seq - 1]
+    slope_ref[0] = slope[: seq - 1].astype(bf16)
     slope_last_ref[0] = slope[seq - 1 :]
 
 
@@ -113,7 +113,7 @@
         out_shape=[
             jax.ShapeDtypeStruct((width, images * (seq - 1)), bf16),
             jax.ShapeDtypeStruct((images, 1, width), bf16),
-            jax.ShapeDtypeStruct((images, seq - 1, hidden), f32),
+            jax.ShapeDtypeStruct((images, seq - 1, hidden), bf16),
             jax.ShapeDtypeStruct((images, 1, hidden), f32),
             jax.ShapeDtypeStruct((images, 1, hidden), f32),
         ],
@@ -141,7 +141,7 @@
         for k, (_, last_ref, slope_ref, slope_last_ref) in enumerate(sets):
             for i in range(images):
                 row = grad_ref[order_ref[k * images + i]]
-                pre_grad[k, pl.ds(i * tokens, tokens), :] = (slope_ref[i] * row).astype(bf16)
+                pre_grad[k, pl.ds(i * tokens, tokens), :] = (slope_ref[i].astype(f32) * row).astype(bf16)
                 pre_last[pl.ds(k * images + i, 1), :] = slope_last_ref[i] * row
                 last_rows[pl.ds(k * images + i, 1), :] = last_ref[i].astype(f32)
         last_term[...] = contract_rows(last_rows[...].astype(bf16), pre_last[...].astype(bf16))
@@ -261,7 +261,7 @@
             pltpu.VMEM((texts, rows, width), bf16),
             pltpu.SemaphoreType.DMA((2, len(ring_img))),
         ],
-        compiler_params=pltpu.CompilerParams(vmem_limit_bytes=24 * 2**20),
+        compiler_params=pltpu.CompilerParams(vmem_limit_bytes=60 * 2**20),
         cost_estimate=pl.CostEstimate(
             flops=4 * (images + texts) * rows * width,
             bytes_accessed=6 * (images + texts) * rows * width,
@@ -474,8 +474,8 @@
     row_mass = jnp.sum(jnp.exp(logits - row_top[:, None]), axis=1)
     col_top = jnp.max(logits, axis=0)
     col_mass = jnp.sum(jnp.exp(logits - col_top[None, :]), axis=0)
-    row_top, row_mass, facing, order, spots, own_mean = lax.optimization_barrier(
-        (row_top, row_mass, facing, order, spots, own_mean)
+    row_top, row_mass, order, spots, own_mean = lax.optimization_barrier(
+        (row_top, row_mass, order, spots, own_mean)
     )
     row_stats = share_rows(jnp.stack((row_top, row_mass)))
     row_stats, other_tok, facing = lax.optimization_barrier((row_stats, other_tok, facing))
@@ -489,9 +489,7 @@
         peak = jnp.max(stats[:, 0], axis=0)
         return peak + jnp.log(jnp.sum(stats[:, 1] * jnp.exp(stats[:, 0] - peak), axis=0))
 
-    row_stats, col_stats, far, far_facing, first = lax.optimization_barrier(
-        (row_stats, col_stats, far, far_facing, first)
-    )
+    row_stats, col_stats, far = lax.optimization_barrier((row_stats, col_stats, far))
     row_lse = lse(row_stats)
     col_lse = lse(col_stats)
     dlogit = (
@@ -506,7 +504,9 @@
     second = encode([[facing], [far[0]], [far[1]], [far_facing]], gain, weights, hidden)
     cached_all = share_rows(cached_part)
     img_part = directions(False, dlogit, txt_low, raw_img, img_inv, bf16)
-    cached_all, second, img_part = lax.optimization_barrier((cached_all, second, img_part))
+    cached_all, first, second, img_part = lax.optimization_barrier(
+        (cached_all, first, second, img_part)
+    )
     img_pairs = img_part.reshape(ring, 2, own_rows, emb)
 
     def to_place(hop):

time: 208 us -> 202 us (0.971)
  local copies, waits for them, and re-layouts: 17 us -> 9.16 us
    unnamed x58 -> x36, local copies, waits for them, and re-layouts: 11.2 us -> 2.72 us
    all_to_all x3, waiting for transfers between devices: 7.43 us -> 12.9 us  [share(): lax.all_to_all(copies, axis, 0, 0, axis_index_groups=groups, tiled=True)]
    ppermute x11, waiting for transfers between devices: 16.9 us -> 13.3 us  [along(): lax.ppermute(piece, 'col', [(i, (i - 2 * hop) % cols) for i in range(cols)])]
    pallas_call x1, Pallas kernels: 2.22 us -> 5.15 us  [gather_units(): pl.pallas_call(unit_kernel, in_specs=[pl.BlockSpec(memory_space=pltpu.SME...]
  transfers between devices with their start and end apart: 28 -> 28, of which waited for: 9 -> 9; matrix products, arithmetic and copies ran while one was open for 8% -> 11% of each run, Pallas kernels for 21% -> 26%
where the time goes in v4:
time: 202 us; the launch traced here: 201 us
  starting transfers between devices  66.9 us (33%)
  Pallas kernels  51.4 us (25%)
  waiting for transfers between devices  41.1 us (20%)
  between operations  14.8 us (7%)
  other arithmetic  12.1 us (6%)
  local copies, waits for them, and re-layouts  9.16 us (5%)
  matrix products  5.57 us (3%)
    ppermute x11, starting transfers between devices, along(): lax.ppermute(piece, 'col', [(i, (i - 2 * hop) % cols) for i in range(cols)])  21.6 us
    pallas_call x2, Pallas kernels, encode(): pl.pallas_call(functools.partial(encode_kernel, cuts), grid=(images,), in...  18.1 us
    all_to_all x3, starting transfers between devices, share(): lax.all_to_all(copies, axis, 0, 0, axis_index_groups=groups, tiled=True)  17 us
    ppermute x11, waiting for transfers between devices, along(): lax.ppermute(piece, 'col', [(i, (i - 2 * hop) % cols) for i in range(cols)])  13.3 us
    all_to_all x3, waiting for transfers between devices, share(): lax.all_to_all(copies, axis, 0, 0, axis_index_groups=groups, tiled=True)  12.9 us
    ppermute x5, starting transfers between devices, across(): return lax.ppermute(piece, both, list(enumerate(twin)))  12.8 us
    pallas_call x2, Pallas kernels, directions(): pl.pallas_call(functools.partial(direction_kernel, turn), in_specs=[vmem]...  11.5 us
    pallas_call x1, Pallas kernels, weigh(): pl.pallas_call(weigh_kernel, grid=(steps,), in_specs=[pl.BlockSpec(memory...  10.8 us
  transfers between devices with their start and end apart: 28, of which 9 were waited for; matrix products, arithmetic and copies ran while one was open for 11% of the time, Pallas kernels for 26%

profile of v4, /device:TPU:8, one launch (start us, length us, event | category | flops | bytes accessed | tf_op | source)
XLA Modules:
  0.0 201.0 jit_solution(9652696506107609204)
XLA Ops:
  8.0 1.9 pad_maximum_fusion
  9.9 1.6 collective-permute-start.3
  11.5 1.7 collective-permute-start.2
  13.2 4.0 %collective-permute-start = (bf16[64,1024]{1,0:T(8,128)(2,1)}, bf16[64,1024]{1,0:T(8,128)(2,1)S(1)}, u32[]{:S(2)}, u32[]{:S(2)}) collective-permute-start(bf16[64,1024]{1,0:T(8,128)(2,1)} %param.9), channel_id=1, source_target_pairs={{0,65},{1,64},{2,67},{3,66},{4,69},{5,68},{6,71},{7,70},{8,73},{9,... | collective-permute-start | bytes 393224 | tf_op jit(solution)/shard_map/ppermute | solution.py:428
  17.3 5.0 %collective-permute-done.1 = s32[512]{0:T(512)S(1)} collective-permute-done((s32[512]{0:T(512)}, s32[512]{0:T(512)S(1)}, u32[]{:S(2)}, u32[]{:S(2)}) %collective-permute-start.1) | collective-permute-done | bytes 2080 | tf_op jit(solution)/shard_map/ppermute | solution.py:428
  22.2 7.5 %collective-permute-done.3.refs_2_ = bf16[257,1408]{1,0:T(8,128)(2,1)S(1)} collective-permute-done((bf16[257,1408]{1,0:T(8,128)(2,1)}, bf16[257,1408]{1,0:T(8,128)(2,1)S(1)}, u32[]{:S(2)}, u32[]{:S(2)}) %collective-permute-start.3) | collective-permute-done | bytes 723744 | tf_op jit(solution)/shard_map/ppermute | solution.py:434
  29.8 0.9 copy-done.6
  30.9 0.9 pad_maximum_fusion.1.refs_0_
  31.8 2.6 %collective-permute-start.6 = (bf16[2,64,1024]{2,1,0:T(8,128)(2,1)S(1)}, bf16[2,64,1024]{2,1,0:T(8,128)(2,1)S(1)}, u32[]{:S(2)}, u32[]{:S(2)}) collective-permute-start(bf16[2,64,1024]{2,1,0:T(8,128)(2,1)S(1)} %pad_maximum_fusion.1.refs_0_), channel_id=1, source_target_pairs={{0,4},{1,5},{2,6},{3,7},{4,0},{5,1},{6,2},{7,3},{8,12},{9,13},{10,... | collective-permute-start | bytes 786440 | tf_op jit(solution)/shard_map/ppermute | solution.py:434
  34.4 1.1 collective-permute-start.5
  35.5 2.2 %collective-permute-start.4 = (bf16[2,64,1024]{2,1,0:T(8,128)(2,1)S(1)}, bf16[2,64,1024]{2,1,0:T(8,128)(2,1)S(1)}, u32[]{:S(2)}, u32[]{:S(2)}) collective-permute-start(bf16[2,64,1024]{2,1,0:T(8,128)(2,1)S(1)} %pad_maximum_fusion.1.refs_0_), channel_id=1, source_target_pairs={{0,6},{1,7},{2,0},{3,1},{4,2},{5,3},{6,4},{7,5},{8,14},{9,15},{10,... | collective-permute-start | bytes 786440 | tf_op jit(solution)/shard_map/ppermute | solution.py:434
  40.2 4.0 %collective-permute-start.7 = (bf16[257,1408]{1,0:T(8,128)(2,1)S(1)}, bf16[257,1408]{1,0:T(8,128)(2,1)}, u32[]{:S(2)}, u32[]{:S(2)}) collective-permute-start(bf16[257,1408]{1,0:T(8,128)(2,1)S(1)} %bitcast.82), channel_id=1, source_target_pairs={{0,65},{1,64},{2,67},{3,66},{4,69},{5,68},{6,71},{7,70},{8,73},{9,... | collective-permute-start | bytes 2171144 | tf_op jit(solution)/shard_map/ppermute | solution.py:428
  44.2 2.0 collective-permute-done.5.refs_2_
  46.2 2.4 %collective-permute-start.8 = (bf16[257,1408]{1,0:T(8,128)(2,1)S(1)}, bf16[257,1408]{1,0:T(8,128)(2,1)}, u32[]{:S(2)}, u32[]{:S(2)}) collective-permute-start(bf16[257,1408]{1,0:T(8,128)(2,1)S(1)} %bitcast.83), channel_id=1, source_target_pairs={{0,4},{1,5},{2,6},{3,7},{4,0},{5,1},{6,2},{7,3},{8,12},{9,13},{10,... | collective-permute-start | bytes 2171144 | tf_op jit(solution)/shard_map/ppermute | solution.py:434
  49.4 5.2 %gather_units.1 = (bf16[8,64,1024]{2,1,0:T(8,128)(2,1)}, bf16[8,64,1024]{2,1,0:T(8,128)(2,1)}, bf16[16,64,1024]{2,1,0:T(8,128)(2,1)}, f32[8,64,1]{2,1,0:T(8,128)...) custom-call(s32[9]{0:T(128)} %stack.74.where_ref, bf16[2,64,1024]{2,1,0:T(8,128)(2,1)} %copy-done.5, ...), custom_call_target="tpu_custom_call" | custom-call | flops 6291456 | bytes 9437184 | tf_op jit(solution)/shard_map/gather_units/pallas_call | solution.py:245
  54.6 3.3 %fusion.13 = (f32[1024]{0:T(1024)S(1)}, f32[512]{0:T(512)S(1)}, f32[512,1024]{1,0:T(8,128)S(1)}) fusion(bf16[512,1024]{1,0:T(8,128)(2,1)} %bitcast.88, bf16[1024,1024]{1,0:T(8,128)(2,1)} %bitcast.74, f32[]{:T(128)} %bitcast.68), kind=kOutput, calls=%fused_computation.50 | convolution fusion | flops 1075313152 | bytes 5249028 | tf_op jit(solution)/shard_map/dot_general | solution.py:28
  59.3 5.9 %all-to-all-start = ((f32[8,2,512]{2,1,0:T(2,128)}), f32[8,2,512]{2,1,0:T(2,128)S(1)}, u32[]{:S(2)}, u32[]{:S(2)}) async-start(f32[8,2,512]{2,1,0:T(2,128)} %broadcast_in_dim.24), calls=%async_computation | async-start | bytes 65536 | tf_op jit(solution)/shard_map/all_to_all | solution.py:34
  65.2 7.4 %all-to-all-done = f32[8,2,512]{2,1,0:T(2,128)S(1)} async-done(((f32[8,2,512]{2,1,0:T(2,128)}), f32[8,2,512]{2,1,0:T(2,128)S(1)}, u32[]{:S(2)}, u32[]{:S(2)}) %all-to-all-start) | async-done | bytes 32800 | tf_op jit(solution)/shard_map/all_to_all | solution.py:34
  73.2 2.7 %collective-permute-start.9 = (bf16[257,1408]{1,0:T(8,128)(2,1)}, bf16[257,1408]{1,0:T(8,128)(2,1)}, u32[]{:S(2)}, u32[]{:S(2)}) collective-permute-start(bf16[257,1408]{1,0:T(8,128)(2,1)} %collective-permute-done.7.refs_3_), channel_id=1, source_target_pairs={{0,6},{1,7},{2,0},{3,1},{4,2},{5,3},{6,4},{7,5},{8,14},{9,15},{10,... | collective-permute-start | bytes 2171144 | tf_op jit(solution)/shard_map/ppermute | solution.py:434
  76.6 4.9 %all-to-all-start.1 = ((f32[16,2,1024]{2,1,0:T(2,128)}), f32[16,2,1024]{2,1,0:T(2,128)S(1)}, u32[]{:S(2)}, u32[]{:S(2)}) async-start(f32[16,2,1024]{2,1,0:T(2,128)} %broadcast_in_dim.25), calls=%async_computation.1 | async-start | bytes 262144 | tf_op jit(solution)/shard_map/all_to_all | solution.py:34
  81.7 5.5 %all-to-all-done.1 = f32[16,2,1024]{2,1,0:T(2,128)S(1)} async-done(((f32[16,2,1024]{2,1,0:T(2,128)}), f32[16,2,1024]{2,1,0:T(2,128)S(1)}, u32[]{:S(2)}, u32[]{:S(2)}) %all-to-all-start.1) | async-done | bytes 131104 | tf_op jit(solution)/shard_map/all_to_all | solution.py:34
  87.2 3.8 %collective-permute-done.10.refs_2_ = bf16[257,1408]{1,0:T(8,128)(2,1)} collective-permute-done((bf16[257,1408]{1,0:T(8,128)(2,1)}, bf16[257,1408]{1,0:T(8,128)(2,1)}, u32[]{:S(2)}, u32[]{:S(2)}) %collective-permute-start.10) | collective-permute-done | bytes 723744 | tf_op jit(solution)/shard_map/ppermute | solution.py:434
  91.4 1.9 subtract_convert_fusion.left_ref
  93.3 6.0 %directions.3 = f32[16,64,1024]{2,1,0:T(8,128)} custom-call(bf16[512,1024]{1,0:T(8,128)(2,1)} %subtract_convert_fusion.left_ref, f32[16,64,1]{2,1,0:T(8,128)} %get-tuple-element.132.inv_ref, bf16[512,1024]{1,0:T(8,128)(2,1)} %bitcast.89, bf16[16,64,1024]{2,1,0:T(8,128)(2,1)} %bitcast.73), custom_call_target="tpu_custom_call" | custom-call | flops 1073741824 | bytes 4194304 | tf_op jit(solution)/shard_map/directions/pallas_call | solution.py:310
  99.4 1.0 collective-permute-start.11
  101.1 0.9 slice.62
  103.2 6.1 %all-to-all-start.2 = ((f32[8,8,1024]{2,1,0:T(8,128)}), f32[8,8,1024]{2,1,0:T(8,128)S(1)}, u32[]{:S(2)}, u32[]{:S(2)}) async-start(f32[8,8,1024]{2,1,0:T(8,128)} %broadcast_in_dim.28), calls=%async_computation.2 | async-start | bytes 524288 | tf_op jit(solution)/shard_map/all_to_all | solution.py:34
  109.3 5.4 %directions.2 = bf16[8,64,1024]{2,1,0:T(8,128)(2,1)} custom-call(bf16[512,1024]{1,0:T(8,128)(2,1)} %subtract_convert_fusion.left_ref, f32[8,64,1]{2,1,0:T(8,128)} %get-tuple-element.104.inv_ref, bf16[1024,1024]{1,0:T(8,128)(2,1)} %bitcast.75, bf16[8,64,1024]{2,1,0:T(8,128)(2,1)} %get-tuple-element.105.raw_hbm), custom_call_target="tpu_custom_call" | custom-call | flops 1073741824 | bytes 2097152 | tf_op jit(solution)/shard_map/directions/pallas_call | solution.py:310
  114.8 9.0 %encode.2 = (bf16[1408,1024]{1,0:T(8,128)(2,1)}, bf16[4,1,1408]{2,1,0:T(2,128)(2,1)}, bf16[4,256,768]{2,1,0:T(8,128)(2,1)}, f32[4,1,768]{2,1,0:T(1,128)}, f32[4,1,768]{2,1,0:T(1,128)}) custom-call(bf16[257,1408]{1,0:T(8,128)(2,1)} %bitcast.81, bf16[257,1408]{1,0:T(8,128)(2,1)} %copy-done.7, bf16[257,1408]{1,0:T(8,128)(2,1)} %copy-done.6, ...), custom_call_target="tpu_custom_call" | custom-call | flops 2223243264 | bytes 8947712 | tf_op jit(solution)/shard_map/encode/pallas_call | solution.py:98
  123.8 9.0 %encode.3 = (bf16[1408,1024]{1,0:T(8,128)(2,1)}, bf16[4,1,1408]{2,1,0:T(2,128)(2,1)}, bf16[4,256,768]{2,1,0:T(8,128)(2,1)}, f32[4,1,768]{2,1,0:T(1,128)}, f32[4,1,768]{2,1,0:T(1,128)}) custom-call(bf16[257,1408]{1,0:T(8,128)(2,1)} %collective-permute-done.8.refs_0_, bf16[257,1408]{1,0:T(8,128)(2,1)} %collective-permute-done.9.refs_1_, ...), custom_call_target="tpu_custom_call" | custom-call | flops 2223243264 | bytes 8947712 | tf_op jit(solution)/shard_map/encode/pallas_call | solution.py:98
  133.6 5.9 %head.1 = (bf16[16,8,2176]{2,1,0:T(8,128)(2,1)}, f32[8,1,768]{2,1,0:T(1,128)}) custom-call(s32[9]{0:T(128)} %concatenate.10.spots_ref, f32[1]{0:T(128)} %copy.30.temper_ref, f32[8,8,1024]{2,1,0:T(8,128)} %copy-done.4, f32[8,1024]{1,0:T(8,128)} %get-tuple-element.116.raw_ref, f32[1,1408]{1,0:T(1,128)} %div.21.mean_ref, ...), custom_call_target="tpu_custom_call" | custom-call | flops 80740352 | bytes 5046272 | tf_op jit(solution)/shard_map/head/pallas_call | solution.py:382
  139.5 5.0 %all-to-all-start.3 = ((bf16[16,8,2176]{2,1,0:T(8,128)(2,1)}), bf16[16,8,2176]{2,1,0:T(8,128)(2,1)S(1)}, u32[]{:S(2)}, u32[]{:S(2)}) async-start(bf16[16,8,2176]{2,1,0:T(8,128)(2,1)} %get-tuple-element.122), calls=%async_computation.3 | async-start | bytes 1114112 | tf_op jit(solution)/shard_map/all_to_all | solution.py:529
  144.5 3.6 %collective-permute-start.14 = (bf16[2,64,1024]{2,1,0:T(8,128)(2,1)S(1)}, bf16[2,64,1024]{2,1,0:T(8,128)(2,1)S(1)}, u32[]{:S(2)}, u32[]{:S(2)}) collective-permute-start(bf16[2,64,1024]{2,1,0:T(8,128)(2,1)S(1)} %get-tuple-element.141), channel_id=1, source_target_pairs={{0,4},{1,5},{2,6},{3,7},{4,0},{5,1},{6,2},{7,3},{8,12},{9,13},{10,... | collective-permute-start | bytes 786440 | tf_op jit(solution)/shard_map/ppermute | solution.py:434
  148.7 2.7 %collective-permute-start.12 = (bf16[2,64,1024]{2,1,0:T(8,128)(2,1)S(1)}, bf16[2,64,1024]{2,1,0:T(8,128)(2,1)S(1)}, u32[]{:S(2)}, u32[]{:S(2)}) collective-permute-start(bf16[2,64,1024]{2,1,0:T(8,128)(2,1)S(1)} %get-tuple-element.143), channel_id=1, source_target_pairs={{0,6},{1,7},{2,0},{3,1},{4,2},{5,3},{6,4},{7,5},{8,14},{9,15},{10,... | collective-permute-start | bytes 786440 | tf_op jit(solution)/shard_map/ppermute | solution.py:434
  151.3 10.8 %weigh.1 = (f32[8,88,768]{2,1,0:T(8,128)}, bf16[8,88,768]{2,1,0:T(8,128)(2,1)}) custom-call(s32[1]{0:T(128)} %bitcast.1.core_ref, s32[8]{0:T(128)} %stack.78.order_ref, bf16[1408,1024]{1,0:T(8,128)(2,1)} %get-tuple-element.106.refs_0_, bf16[4,1,1408]{2,1,0:T(2,128)(2,1)} %get-tuple-element.107.refs_1_, bf16[4,256,768]{2,1,0:T(8,128)(2,1)} %get-tuple-element.108.refs_2_, ...), custom_call_target="tpu_custom_call" | custom-call | flops 4429185024 | bytes 12058624 | tf_op jit(solution)/shard_map/weigh/pallas_call | solution.py:178
  163.3 0.9 fusion.3
  164.2 1.3 convert_add_fusion
  166.0 1.3 add_convert_fusion
  167.3 5.7 %all-to-all-start.4 = ((bf16[8,88,768]{2,1,0:T(8,128)(2,1)}), bf16[8,88,768]{2,1,0:T(8,128)(2,1)S(1)}, u32[]{:S(2)}, u32[]{:S(2)}) async-start(bf16[8,88,768]{2,1,0:T(8,128)(2,1)} %add_convert_fusion), calls=%async_computation.4 | async-start | bytes 2162688 | tf_op jit(solution)/shard_map/all_to_all | solution.py:552
  173.1 1.0 collective-permute-start.18
  174.1 3.7 %collective-permute-start.16 = (bf16[64,1024]{1,0:T(8,128)(2,1)S(1)}, bf16[64,1024]{1,0:T(8,128)(2,1)S(1)}, u32[]{:S(2)}, u32[]{:S(2)}) collective-permute-start(bf16[64,1024]{1,0:T(8,128)(2,1)S(1)} %fusion.5), channel_id=1, source_target_pairs={{0,65},{1,64},{2,67},{3,66},{4,69},{5,68},{6,71},{7,70},{8,73},{9,... | collective-permute-start | bytes 393224 | tf_op jit(solution)/shard_map/ppermute | solution.py:428
  177.8 0.8 collective-permute-done.18
  178.7 3.7 %collective-permute-start.19 = (f32[128,88]{1,0:T(8,128)S(1)}, f32[128,88]{1,0:T(8,128)S(1)}, u32[]{:S(2)}, u32[]{:S(2)}) collective-permute-start(f32[128,88]{1,0:T(8,128)S(1)} %pad_maximum_fusion.2), channel_id=1, source_target_pairs={{0,1},{1,0},{2,3},{3,2},{4,5},{5,4},{6,7},{7,6},{8,9},{9,8},{10,11... | collective-permute-start | bytes 135176 | tf_op jit(solution)/shard_map/ppermute | solution.py:548
  182.4 0.8 fusion.2
  183.1 7.7 %collective-permute-done.19 = f32[128,88]{1,0:T(8,128)S(1)} collective-permute-done((f32[128,88]{1,0:T(8,128)S(1)}, f32[128,88]{1,0:T(8,128)S(1)}, u32[]{:S(2)}, u32[]{:S(2)}) %collective-permute-start.19) | collective-permute-done | bytes 45088 | tf_op jit(solution)/shard_map/ppermute | solution.py:548
  190.9 1.0 fusion
  191.9 0.8 convert_reduce_fusion
  192.7 1.7 broadcast_multiply_fusion
  (106 shorter events, 11.7 us)
Async XLA Ops:
  7.2 33.0 %copy-start.2 = (bf16[1,257,1408]{2,1,0:T(8,128)(2,1)S(1)}, bf16[1,257,1408]{2,1,0:T(8,128)(2,1)}, u32[]{:S(2)}) copy-start(bf16[1,257,1408]{2,1,0:T(8,128)(2,1)} %param.13) | copy-start | bytes 2171140
  7.2 39.1 %all-gather.3.cloned.1.call-start = ((), (), s32[]{:S(2)}) async-start(), calls=%async_computation.6 | async-start | bytes 2228224 | tf_op jit(solution)/shard_map/all_gather | solution.py:439
  7.9 106.8 %all-gather.5.cloned.1.call-start = ((), (), s32[]{:S(2)}) async-start(), calls=%async_computation.7 | async-start | bytes 7659520 | tf_op jit(solution)/shard_map/all_gather | solution.py:440
  9.9 19.8 %collective-permute-start.3 = (bf16[257,1408]{1,0:T(8,128)(2,1)}, bf16[257,1408]{1,0:T(8,128)(2,1)S(1)}, u32[]{:S(2)}, u32[]{:S(2)}) collective-permute-start(bf16[257,1408]{1,0:T(8,128)(2,1)} %bitcast.79), channel_id=1, source_target_pairs={{0,2},{1,3},{2,4},{3,5},{4,6},{5,7},{6,0},{7,1},{8,10},{9,11},{10,... | collective-permute-start | bytes 2171144 | tf_op jit(solution)/shard_map/ppermute | solution.py:434
  11.5 18.3 %collective-permute-start.2 = (bf16[257,1408]{1,0:T(8,128)(2,1)}, bf16[257,1408]{1,0:T(8,128)(2,1)S(1)}, u32[]{:S(2)}, u32[]{:S(2)}) collective-permute-start(bf16[257,1408]{1,0:T(8,128)(2,1)} %bitcast.80), channel_id=1, source_target_pairs={{0,6},{1,7},{2,0},{3,1},{4,2},{5,3},{6,4},{7,5},{8,14},{9,15},{10,... | collective-permute-start | bytes 2171144 | tf_op jit(solution)/shard_map/ppermute | solution.py:434
  13.2 9.0 %collective-permute-start = (bf16[64,1024]{1,0:T(8,128)(2,1)}, bf16[64,1024]{1,0:T(8,128)(2,1)S(1)}, u32[]{:S(2)}, u32[]{:S(2)}) collective-permute-start(bf16[64,1024]{1,0:T(8,128)(2,1)} %param.9), channel_id=1, source_target_pairs={{0,65},{1,64},{2,67},{3,66},{4,69},{5,68},{6,71},{7,70},{8,73},{9,... | collective-permute-start | bytes 393224 | tf_op jit(solution)/shard_map/ppermute | solution.py:428
  17.2 5.0 %collective-permute-start.1 = (s32[512]{0:T(512)}, s32[512]{0:T(512)S(1)}, u32[]{:S(2)}, u32[]{:S(2)}) collective-permute-start(s32[512]{0:T(512)} %param.11), channel_id=1, source_target_pairs={{0,65},{1,64},{2,67},{3,66},{4,69},{5,68},{6,71},{7,70},{8,73},{9,... | collective-permute-start | bytes 6152 | tf_op jit(solution)/shard_map/ppermute | solution.py:428
  29.7 0.9 copy-start.6
  29.8 1.1 copy-start.7
  31.8 17.6 %copy-start.5 = (bf16[2,64,1024]{2,1,0:T(8,128)(2,1)}, bf16[2,64,1024]{2,1,0:T(8,128)(2,1)S(1)}, u32[]{:S(2)}) copy-start(bf16[2,64,1024]{2,1,0:T(8,128)(2,1)S(1)} %pad_maximum_fusion.1.refs_0_) | copy-start | bytes 786436
  31.8 12.4 %collective-permute-start.6 = (bf16[2,64,1024]{2,1,0:T(8,128)(2,1)S(1)}, bf16[2,64,1024]{2,1,0:T(8,128)(2,1)S(1)}, u32[]{:S(2)}, u32[]{:S(2)}) collective-permute-start(bf16[2,64,1024]{2,1,0:T(8,128)(2,1)S(1)} %pad_maximum_fusion.1.refs_0_), channel_id=1, source_target_pairs={{0,4},{1,5},{2,6},{3,7},{4,0},{5,1},{6,2},{7,3},{8,12},{9,13},{10,... | collective-permute-start | bytes 786440 | tf_op jit(solution)/shard_map/ppermute | solution.py:434
  34.4 11.8 %collective-permute-start.5 = (bf16[2,64,1024]{2,1,0:T(8,128)(2,1)S(1)}, bf16[2,64,1024]{2,1,0:T(8,128)(2,1)S(1)}, u32[]{:S(2)}, u32[]{:S(2)}) collective-permute-start(bf16[2,64,1024]{2,1,0:T(8,128)(2,1)S(1)} %pad_maximum_fusion.1.refs_0_), channel_id=1, source_target_pairs={{0,2},{1,3},{2,4},{3,5},{4,6},{5,7},{6,0},{7,1},{8,10},{9,11},{10,... | collective-permute-start | bytes 786440 | tf_op jit(solution)/shard_map/ppermute | solution.py:434
  35.5 10.7 %collective-permute-start.4 = (bf16[2,64,1024]{2,1,0:T(8,128)(2,1)S(1)}, bf16[2,64,1024]{2,1,0:T(8,128)(2,1)S(1)}, u32[]{:S(2)}, u32[]{:S(2)}) collective-permute-start(bf16[2,64,1024]{2,1,0:T(8,128)(2,1)S(1)} %pad_maximum_fusion.1.refs_0_), channel_id=1, source_target_pairs={{0,6},{1,7},{2,0},{3,1},{4,2},{5,3},{6,4},{7,5},{8,14},{9,15},{10,... | collective-permute-start | bytes 786440 | tf_op jit(solution)/shard_map/ppermute | solution.py:434
  40.2 25.0 %collective-permute-start.7 = (bf16[257,1408]{1,0:T(8,128)(2,1)S(1)}, bf16[257,1408]{1,0:T(8,128)(2,1)}, u32[]{:S(2)}, u32[]{:S(2)}) collective-permute-start(bf16[257,1408]{1,0:T(8,128)(2,1)S(1)} %bitcast.82), channel_id=1, source_target_pairs={{0,65},{1,64},{2,67},{3,66},{4,69},{5,68},{6,71},{7,70},{8,73},{9,... | collective-permute-start | bytes 2171144 | tf_op jit(solution)/shard_map/ppermute | solution.py:428
  44.2 5.2 %copy-start.13 = (bf16[2,64,1024]{2,1,0:T(8,128)(2,1)}, bf16[2,64,1024]{2,1,0:T(8,128)(2,1)S(1)}, u32[]{:S(2)}) copy-start(bf16[2,64,1024]{2,1,0:T(8,128)(2,1)S(1)} %collective-permute-done.6.refs_3_) | copy-start | bytes 786436
  46.2 3.2 %copy-start.14 = (bf16[2,64,1024]{2,1,0:T(8,128)(2,1)}, bf16[2,64,1024]{2,1,0:T(8,128)(2,1)S(1)}, u32[]{:S(2)}) copy-start(bf16[2,64,1024]{2,1,0:T(8,128)(2,1)S(1)} %collective-permute-done.5.refs_2_) | copy-start | bytes 786436
  46.2 3.2 %copy-start.15 = (bf16[2,64,1024]{2,1,0:T(8,128)(2,1)}, bf16[2,64,1024]{2,1,0:T(8,128)(2,1)S(1)}, u32[]{:S(2)}) copy-start(bf16[2,64,1024]{2,1,0:T(8,128)(2,1)S(1)} %collective-permute-done.4.refs_1_) | copy-start | bytes 786436
  46.2 26.4 %collective-permute-start.8 = (bf16[257,1408]{1,0:T(8,128)(2,1)S(1)}, bf16[257,1408]{1,0:T(8,128)(2,1)}, u32[]{:S(2)}, u32[]{:S(2)}) collective-permute-start(bf16[257,1408]{1,0:T(8,128)(2,1)S(1)} %bitcast.83), channel_id=1, source_target_pairs={{0,4},{1,5},{2,6},{3,7},{4,0},{5,1},{6,2},{7,3},{8,12},{9,13},{10,... | collective-permute-start | bytes 2171144 | tf_op jit(solution)/shard_map/ppermute | solution.py:434
  57.9 23.9 %copy-start.17 = (s32[512]{0:T(512)S(1)}, s32[512]{0:T(512)}, u32[]{:S(2)}) copy-start(s32[512]{0:T(512)} %param.11) | copy-start | bytes 6148
  59.3 13.3 %all-to-all-start = ((f32[8,2,512]{2,1,0:T(2,128)}), f32[8,2,512]{2,1,0:T(2,128)S(1)}, u32[]{:S(2)}, u32[]{:S(2)}) async-start(f32[8,2,512]{2,1,0:T(2,128)} %broadcast_in_dim.24), calls=%async_computation | async-start | bytes 65536 | tf_op jit(solution)/shard_map/all_to_all | solution.py:34
  72.6 18.4 %collective-permute-start.10 = (bf16[257,1408]{1,0:T(8,128)(2,1)}, bf16[257,1408]{1,0:T(8,128)(2,1)}, u32[]{:S(2)}, u32[]{:S(2)}) collective-permute-start(bf16[257,1408]{1,0:T(8,128)(2,1)} %collective-permute-done.7.refs_3_), channel_id=1, source_target_pairs={{0,2},{1,3},{2,4},{3,5},{4,6},{5,7},{6,0},{7,1},{8,10},{9,11},{10,... | collective-permute-start | bytes 2171144 | tf_op jit(solution)/shard_map/ppermute | solution.py:434
  73.2 17.9 %collective-permute-start.9 = (bf16[257,1408]{1,0:T(8,128)(2,1)}, bf16[257,1408]{1,0:T(8,128)(2,1)}, u32[]{:S(2)}, u32[]{:S(2)}) collective-permute-start(bf16[257,1408]{1,0:T(8,128)(2,1)} %collective-permute-done.7.refs_3_), channel_id=1, source_target_pairs={{0,6},{1,7},{2,0},{3,1},{4,2},{5,3},{6,4},{7,5},{8,14},{9,15},{10,... | collective-permute-start | bytes 2171144 | tf_op jit(solution)/shard_map/ppermute | solution.py:434
  76.6 10.7 %all-to-all-start.1 = ((f32[16,2,1024]{2,1,0:T(2,128)}), f32[16,2,1024]{2,1,0:T(2,128)S(1)}, u32[]{:S(2)}, u32[]{:S(2)}) async-start(f32[16,2,1024]{2,1,0:T(2,128)} %broadcast_in_dim.25), calls=%async_computation.1 | async-start | bytes 262144 | tf_op jit(solution)/shard_map/all_to_all | solution.py:34
  81.5 110.3 %reduce-scatter.2.cloned.1.call-start = ((), (), s32[]{:S(2)}) async-start(), calls=%async_computation.8 | async-start | bytes 4456448 | tf_op jit(solution)/shard_map/reduce_scatter | solution.py:503
  99.3 1.1 copy-start.16
  99.3 1.7 copy-start.8
  99.3 2.7 %copy-start = (bf16[16,64,1024]{2,1,0:T(8,128)(2,1)S(1)}, bf16[16,64,1024]{2,1,0:T(8,128)(2,1)}, u32[]{:S(2)}) copy-start(bf16[16,64,1024]{2,1,0:T(8,128)(2,1)} %get-tuple-element.79) | copy-start | bytes 6291460
  99.4 24.4 %collective-permute-start.11 = (bf16[257,1408]{1,0:T(8,128)(2,1)}, bf16[257,1408]{1,0:T(8,128)(2,1)}, u32[]{:S(2)}, u32[]{:S(2)}) collective-permute-start(bf16[257,1408]{1,0:T(8,128)(2,1)} %collective-permute-done.8.refs_0_), channel_id=1, source_target_pairs={{0,65},{1,64},{2,67},{3,66},{4,69},{5,68},{6,71},{7,70},{8,73},{9,... | collective-permute-start | bytes 2171144 | tf_op jit(solution)/shard_map/ppermute | solution.py:428
  103.2 29.7 %all-to-all-start.2 = ((f32[8,8,1024]{2,1,0:T(8,128)}), f32[8,8,1024]{2,1,0:T(8,128)S(1)}, u32[]{:S(2)}, u32[]{:S(2)}) async-start(f32[8,8,1024]{2,1,0:T(8,128)} %broadcast_in_dim.28), calls=%async_computation.2 | async-start | bytes 524288 | tf_op jit(solution)/shard_map/all_to_all | solution.py:34
  132.9 0.7 copy-start.4
  133.6 10.9 %copy-start.1 = (bf16[8,64,1024]{2,1,0:T(8,128)(2,1)S(1)}, bf16[8,64,1024]{2,1,0:T(8,128)(2,1)}, u32[]{:S(2)}) copy-start(bf16[8,64,1024]{2,1,0:T(8,128)(2,1)} %directions.2) | copy-start | bytes 3145732
  139.5 22.8 %all-to-all-start.3 = ((bf16[16,8,2176]{2,1,0:T(8,128)(2,1)}), bf16[16,8,2176]{2,1,0:T(8,128)(2,1)S(1)}, u32[]{:S(2)}, u32[]{:S(2)}) async-start(bf16[16,8,2176]{2,1,0:T(8,128)(2,1)} %get-tuple-element.122), calls=%async_computation.3 | async-start | bytes 1114112 | tf_op jit(solution)/shard_map/all_to_all | solution.py:529
  144.5 17.7 %collective-permute-start.14 = (bf16[2,64,1024]{2,1,0:T(8,128)(2,1)S(1)}, bf16[2,64,1024]{2,1,0:T(8,128)(2,1)S(1)}, u32[]{:S(2)}, u32[]{:S(2)}) collective-permute-start(bf16[2,64,1024]{2,1,0:T(8,128)(2,1)S(1)} %get-tuple-element.141), channel_id=1, source_target_pairs={{0,4},{1,5},{2,6},{3,7},{4,0},{5,1},{6,2},{7,3},{8,12},{9,13},{10,... | collective-permute-start | bytes 786440 | tf_op jit(solution)/shard_map/ppermute | solution.py:434
  148.1 14.1 %collective-permute-start.13 = (bf16[2,64,1024]{2,1,0:T(8,128)(2,1)S(1)}, bf16[2,64,1024]{2,1,0:T(8,128)(2,1)S(1)}, u32[]{:S(2)}, u32[]{:S(2)}) collective-permute-start(bf16[2,64,1024]{2,1,0:T(8,128)(2,1)S(1)} %get-tuple-element.142), channel_id=1, source_target_pairs={{0,2},{1,3},{2,4},{3,5},{4,6},{5,7},{6,0},{7,1},{8,10},{9,11},{10,... | collective-permute-start | bytes 786440 | tf_op jit(solution)/shard_map/ppermute | solution.py:434
  148.7 13.5 %collective-permute-start.12 = (bf16[2,64,1024]{2,1,0:T(8,128)(2,1)S(1)}, bf16[2,64,1024]{2,1,0:T(8,128)(2,1)S(1)}, u32[]{:S(2)}, u32[]{:S(2)}) collective-permute-start(bf16[2,64,1024]{2,1,0:T(8,128)(2,1)S(1)} %get-tuple-element.143), channel_id=1, source_target_pairs={{0,6},{1,7},{2,0},{3,1},{4,2},{5,3},{6,4},{7,5},{8,14},{9,15},{10,... | collective-permute-start | bytes 786440 | tf_op jit(solution)/shard_map/ppermute | solution.py:434
  151.3 11.7 %copy-start.9 = (bf16[64,1024]{1,0:T(8,128)(2,1)S(1)}, bf16[64,1024]{1,0:T(8,128)(2,1)}, u32[]{:S(2)}) copy-start(bf16[64,1024]{1,0:T(8,128)(2,1)} %param.9) | copy-start | bytes 393220
  162.2 1.1 copy-start.10
  162.2 0.8 copy-start.11
  162.2 0.8 copy-start.12
  163.1 2.9 %collective-permute-start.15 = (bf16[8,88,768]{2,1,0:T(8,128)(2,1)}, bf16[8,88,768]{2,1,0:T(8,128)(2,1)S(1)}, u32[]{:S(2)}, u32[]{:S(2)}) collective-permute-start(bf16[8,88,768]{2,1,0:T(8,128)(2,1)} %get-tuple-element.124), channel_id=1, source_target_pairs={{0,8},{8,0},{16,24},{24,16},{32,40},{40,32},{48,56},{56,48},{64,72... | collective-permute-start | bytes 3244040 | tf_op jit(solution)/shard_map/ppermute | solution.py:531
  163.1 2.9 %copy-start.3 = (f32[8,88,768]{2,1,0:T(8,128)S(1)}, f32[8,88,768]{2,1,0:T(8,128)}, u32[]{:S(2)}) copy-start(f32[8,88,768]{2,1,0:T(8,128)} %get-tuple-element.130) | copy-start | bytes 6488068
  166.0 7.1 %collective-permute-start.17 = (f32[128,88]{1,0:T(8,128)S(1)}, f32[128,88]{1,0:T(8,128)S(1)}, u32[]{:S(2)}, u32[]{:S(2)}) collective-permute-start(f32[128,88]{1,0:T(8,128)S(1)} %convert_add_fusion.1), channel_id=1, source_target_pairs={{0,2},{1,3},{2,0},{3,1},{4,6},{5,7},{6,4},{7,5},{8,10},{9,11},{10,... | collective-permute-start | bytes 135176 | tf_op jit(solution)/shard_map/ppermute | solution.py:545
  167.3 24.5 %all-to-all-start.4 = ((bf16[8,88,768]{2,1,0:T(8,128)(2,1)}), bf16[8,88,768]{2,1,0:T(8,128)(2,1)S(1)}, u32[]{:S(2)}, u32[]{:S(2)}) async-start(bf16[8,88,768]{2,1,0:T(8,128)(2,1)} %add_convert_fusion), calls=%async_computation.4 | async-start | bytes 2162688 | tf_op jit(solution)/shard_map/all_to_all | solution.py:552
  173.1 5.6 %collective-permute-start.18 = (f32[128,88]{1,0:T(8,128)S(1)}, f32[128,88]{1,0:T(8,128)S(1)}, u32[]{:S(2)}, u32[]{:S(2)}) collective-permute-start(f32[128,88]{1,0:T(8,128)S(1)} %add.198), channel_id=1, source_target_pairs={{0,6},{1,7},{2,4},{3,5},{4,2},{5,3},{6,0},{7,1},{8,14},{9,15},{10,... | collective-permute-start | bytes 135176 | tf_op jit(solution)/shard_map/ppermute | solution.py:545
  174.1 8.2 %collective-permute-start.16 = (bf16[64,1024]{1,0:T(8,128)(2,1)S(1)}, bf16[64,1024]{1,0:T(8,128)(2,1)S(1)}, u32[]{:S(2)}, u32[]{:S(2)}) collective-permute-start(bf16[64,1024]{1,0:T(8,128)(2,1)S(1)} %fusion.5), channel_id=1, source_target_pairs={{0,65},{1,64},{2,67},{3,66},{4,69},{5,68},{6,71},{7,70},{8,73},{9,... | collective-permute-start | bytes 393224 | tf_op jit(solution)/shard_map/ppermute | solution.py:428
  178.7 12.2 %collective-permute-start.19 = (f32[128,88]{1,0:T(8,128)S(1)}, f32[128,88]{1,0:T(8,128)S(1)}, u32[]{:S(2)}, u32[]{:S(2)}) collective-permute-start(f32[128,88]{1,0:T(8,128)S(1)} %pad_maximum_fusion.2), channel_id=1, source_target_pairs={{0,1},{1,0},{2,3},{3,2},{4,5},{5,4},{6,7},{7,6},{8,9},{9,8},{10,11... | collective-permute-start | bytes 135176 | tf_op jit(solution)/shard_map/ppermute | solution.py:548
Sparse Core Ops, SparseCore 0:
  9.7 36.0 all-gather.2
  47.5 48.0 all-gather.4
  99.5 66.7 reduce-scatter.1

commit v5 on v4

--- a/solution.py
+++ b/solution.py
@@ -271,60 +271,83 @@
     )(where, *ring_img, raw_txt)
 
 
-def direction_kernel(turn, left_ref, inv_ref, low_hbm, raw_hbm, out_hbm, low, raw, out, *rest):
-    in_sems, out_sems = rest[-2:]
-    blocks, rows, _ = raw.shape
-    part = blocks // 4
+def direction_kernel(
+    dlogit_ref, inv_img, inv_txt, low_img_hbm, low_txt_hbm, raw_img_hbm, raw_txt_hbm,
+    img_hbm, txt_hbm, low_img, low_txt, raw_img, raw_txt, img_out, txt_out, turned, in_sems, out_sems,
+):
+    groups, rows, _ = raw_img.shape
+    many = raw_txt.shape[0]
     loads = [
-        pltpu.make_async_copy(low_hbm, low, in_sems.at[0]),
-        pltpu.make_async_copy(raw_hbm, raw, in_sems.at[1]),
+        pltpu.make_async_copy(source, target, in_sems.at[k])
+        for k, (source, target) in enumerate(
+            (
+                (low_txt_hbm, low_txt),
+                (raw_img_hbm, raw_img),
+                (low_img_hbm, low_img),
+                (raw_txt_hbm, raw_txt),
+            )
+        )
     ]
     for load in loads:
         load.start()
-    left = left_ref
-    if turn:
-        left = rest[0]
-        left[...] = left_ref[...].T
-    for load in loads:
-        load.wait()
+    turned[...] = dlogit_ref[...].T
     stores = []
-    for k in range(4):
-        total = jnp.dot(
-            left[pl.ds(k * part * rows, part * rows), :], low[...], preferred_element_type=f32
-        )
-        for m in range(part):
-            unit = raw[k * part + m].astype(f32) * inv_ref[k * part + m]
-            piece = project(total[m * rows : (m + 1) * rows], unit)
-            out[k * part + m] = piece.astype(out.dtype)
-        piece = pl.ds(k * part, part)
-        stores.append(pltpu.make_async_copy(out.at[piece], out_hbm.at[piece], out_sems.at[k]))
-        stores[-1].start()
+
+    def run(left, right, raw, inv, out, hbm, count):
+        for k in range(4):
+            part = count // 4
+            total = jnp.dot(
+                left[pl.ds(k * part * rows, part * rows), :], right[...], preferred_element_type=f32
+            )
+            for m in range(part):
+                unit = raw[k * part + m].astype(f32) * inv[k * part + m]
+                piece = project(total[m * rows : (m + 1) * rows], unit)
+                out[k * part + m] = piece.astype(out.dtype)
+            piece = pl.ds(k * part, part)
+            store = pltpu.make_async_copy(out.at[piece], hbm.at[piece], out_sems.at[len(stores)])
+            store.start()
+            stores.append(store)
+
+    loads[0].wait()
+    loads[1].wait()
+    run(dlogit_ref, low_txt, raw_img, inv_img, img_out, img_hbm, groups)
+    loads[2].wait()
+    loads[3].wait()
+    run(turned, low_img, raw_txt, inv_txt, txt_out, txt_hbm, many)
     for store in stores:
         store.wait()
 
 
-def directions(turn, dlogit, low, raw, inv, kind):
+def directions(dlogit, low_img, low_txt, raw_img, raw_txt, inv_img, inv_txt):
+    rows, cols = dlogit.shape
+    width = low_img.shape[1]
     vmem = pl.BlockSpec(memory_space=pltpu.VMEM)
     hbm = pl.BlockSpec(memory_space=pltpu.HBM)
-    turned = [pltpu.VMEM(dlogit.shape[::-1], bf16)] if turn else []
     return pl.pallas_call(
-        functools.partial(direction_kernel, turn),
-        in_specs=[vmem] * 2 + [hbm] * 2,
-        out_specs=hbm,
-        out_shape=jax.ShapeDtypeStruct(raw.shape, kind),
+        direction_kernel,
+        in_specs=[vmem] * 3 + [hbm] * 4,
+        out_specs=[hbm] * 2,
+        out_shape=[
+            jax.ShapeDtypeStruct(raw_img.shape, bf16),
+            jax.ShapeDtypeStruct(raw_txt.shape, f32),
+        ],
         scratch_shapes=[
-            pltpu.VMEM(low.shape, bf16),
-            pltpu.VMEM(raw.shape, bf16),
-            pltpu.VMEM(raw.shape, kind),
-        ]
-        + turned
-        + [pltpu.SemaphoreType.DMA((2,)), pltpu.SemaphoreType.DMA((4,))],
+            pltpu.VMEM(low_img.shape, bf16),
+            pltpu.VMEM(low_txt.shape, bf16),
+            pltpu.VMEM(raw_img.shape, bf16),
+            pltpu.VMEM(raw_txt.shape, bf16),
+            pltpu.VMEM(raw_img.shape, bf16),
+            pltpu.VMEM(raw_txt.shape, f32),
+            pltpu.VMEM((cols, rows), bf16),
+            pltpu.SemaphoreType.DMA((4,)),
+            pltpu.SemaphoreType.DMA((8,)),
+        ],
         compiler_params=pltpu.CompilerParams(vmem_limit_bytes=60 * 2**20),
         cost_estimate=pl.CostEstimate(
-            flops=2 * dlogit.size * low.shape[1], bytes_accessed=4 * raw.size, transcendentals=0
+            flops=4 * rows * cols * width, bytes_accessed=10 * cols * width, transcendentals=0
         ),
         name="directions",
-    )(dlogit, inv, low, raw)
+    )(dlogit, inv_img, inv_txt, low_img, low_txt, raw_img, raw_txt)
 
 
 def project(partial, unit):
@@ -499,11 +522,10 @@
     cached_part = jnp.dot(
         dlogit.reshape(cols, own_rows, txt_count)[:, 0], txt_low, preferred_element_type=f32
     )
-    txt_part = directions(True, dlogit, img_low, raw_txt, txt_inv, f32)
+    img_part, txt_part = directions(dlogit, img_low, txt_low, raw_img, raw_txt, img_inv, txt_inv)
     txt_sum = lax.psum_scatter(txt_part.reshape(-1, emb), "dp", scatter_dimension=0, tiled=True)
     second = encode([[facing], [far[0]], [far[1]], [far_facing]], gain, weights, hidden)
     cached_all = share_rows(cached_part)
-    img_part = directions(False, dlogit, txt_low, raw_img, img_inv, bf16)
     cached_all, first, second, img_part = lax.optimization_barrier(
         (cached_all, first, second, img_part)
     )

time: 202 us -> 198 us (0.980)
  Pallas kernels: 51.4 us -> 47.6 us
    pallas_call x2 -> x1, Pallas kernels: 11.5 us -> 7.61 us  [directions(): pl.pallas_call(direction_kernel, in_specs=[vmem] * 3 + [hbm] * 4, out_spe...]
  transfers between devices with their start and end apart: 28 -> 28, of which waited for: 9 -> 10; matrix products, arithmetic and copies ran while one was open for 11% -> 11% of each run, Pallas kernels for 26% -> 24%
where the time goes in v5:
time: 198 us; the launch traced here: 197 us
  starting transfers between devices  65.6 us (33%)
  Pallas kernels  47.6 us (24%)
  waiting for transfers between devices  42.2 us (21%)
  between operations  14.8 us (7%)
  other arithmetic  12.1 us (6%)
  local copies, waits for them, and re-layouts  9.08 us (5%)
  matrix products  5.57 us (3%)
    ppermute x11, starting transfers between devices, along(): lax.ppermute(piece, 'col', [(i, (i - 2 * hop) % cols) for i in range(cols)])  20.5 us
    pallas_call x2, Pallas kernels, encode(): pl.pallas_call(functools.partial(encode_kernel, cuts), grid=(images,), in...  18 us
    all_to_all x3, starting transfers between devices, share(): lax.all_to_all(copies, axis, 0, 0, axis_index_groups=groups, tiled=True)  16.9 us
    ppermute x11, waiting for transfers between devices, along(): lax.ppermute(piece, 'col', [(i, (i - 2 * hop) % cols) for i in range(cols)])  13.4 us
    all_to_all x3, waiting for transfers between devices, share(): lax.all_to_all(copies, axis, 0, 0, axis_index_groups=groups, tiled=True)  12.7 us
    ppermute x5, starting transfers between devices, across(): return lax.ppermute(piece, both, list(enumerate(twin)))  12 us
    pallas_call x1, Pallas kernels, weigh(): pl.pallas_call(weigh_kernel, grid=(steps,), in_specs=[pl.BlockSpec(memory...  10.9 us
    ppermute x1, waiting for transfers between devices, on_device(): pool_all += lax.ppermute(turned, 'col', [(c, c ^ 1) for c in range(cols)])  7.74 us
  transfers between devices with their start and end apart: 28, of which 10 were waited for; matrix products, arithmetic and copies ran while one was open for 11% of the time, Pallas kernels for 24%

profile of v5, /device:TPU:8, one launch (start us, length us, event | category | flops | bytes accessed | tf_op | source)
XLA Modules:
  0.0 196.9 jit_solution(9616657260039976855)
XLA Ops:
  8.0 1.9 pad_maximum_fusion
  9.9 1.6 collective-permute-start.3
  11.5 1.7 collective-permute-start.2
  13.2 4.0 %collective-permute-start = (bf16[64,1024]{1,0:T(8,128)(2,1)}, bf16[64,1024]{1,0:T(8,128)(2,1)S(1)}, u32[]{:S(2)}, u32[]{:S(2)}) collective-permute-start(bf16[64,1024]{1,0:T(8,128)(2,1)} %param.9), channel_id=1, source_target_pairs={{0,65},{1,64},{2,67},{3,66},{4,69},{5,68},{6,71},{7,70},{8,73},{9,... | collective-permute-start | bytes 393224 | tf_op jit(solution)/shard_map/ppermute | solution.py:451
  17.3 5.0 %collective-permute-done.1 = s32[512]{0:T(512)S(1)} collective-permute-done((s32[512]{0:T(512)}, s32[512]{0:T(512)S(1)}, u32[]{:S(2)}, u32[]{:S(2)}) %collective-permute-start.1) | collective-permute-done | bytes 2080 | tf_op jit(solution)/shard_map/ppermute | solution.py:451
  22.2 7.5 %collective-permute-done.3.refs_2_ = bf16[257,1408]{1,0:T(8,128)(2,1)S(1)} collective-permute-done((bf16[257,1408]{1,0:T(8,128)(2,1)}, bf16[257,1408]{1,0:T(8,128)(2,1)S(1)}, u32[]{:S(2)}, u32[]{:S(2)}) %collective-permute-start.3) | collective-permute-done | bytes 723744 | tf_op jit(solution)/shard_map/ppermute | solution.py:457
  29.7 0.9 copy-done.6
  30.9 0.9 pad_maximum_fusion.1.refs_0_
  31.8 2.6 %collective-permute-start.6 = (bf16[2,64,1024]{2,1,0:T(8,128)(2,1)S(1)}, bf16[2,64,1024]{2,1,0:T(8,128)(2,1)S(1)}, u32[]{:S(2)}, u32[]{:S(2)}) collective-permute-start(bf16[2,64,1024]{2,1,0:T(8,128)(2,1)S(1)} %pad_maximum_fusion.1.refs_0_), channel_id=1, source_target_pairs={{0,4},{1,5},{2,6},{3,7},{4,0},{5,1},{6,2},{7,3},{8,12},{9,13},{10,... | collective-permute-start | bytes 786440 | tf_op jit(solution)/shard_map/ppermute | solution.py:457
  34.4 1.1 collective-permute-start.5
  35.5 2.2 %collective-permute-start.4 = (bf16[2,64,1024]{2,1,0:T(8,128)(2,1)S(1)}, bf16[2,64,1024]{2,1,0:T(8,128)(2,1)S(1)}, u32[]{:S(2)}, u32[]{:S(2)}) collective-permute-start(bf16[2,64,1024]{2,1,0:T(8,128)(2,1)S(1)} %pad_maximum_fusion.1.refs_0_), channel_id=1, source_target_pairs={{0,6},{1,7},{2,0},{3,1},{4,2},{5,3},{6,4},{7,5},{8,14},{9,15},{10,... | collective-permute-start | bytes 786440 | tf_op jit(solution)/shard_map/ppermute | solution.py:457
  40.1 4.0 %collective-permute-start.7 = (bf16[257,1408]{1,0:T(8,128)(2,1)S(1)}, bf16[257,1408]{1,0:T(8,128)(2,1)}, u32[]{:S(2)}, u32[]{:S(2)}) collective-permute-start(bf16[257,1408]{1,0:T(8,128)(2,1)S(1)} %bitcast.80), channel_id=1, source_target_pairs={{0,65},{1,64},{2,67},{3,66},{4,69},{5,68},{6,71},{7,70},{8,73},{9,... | collective-permute-start | bytes 2171144 | tf_op jit(solution)/shard_map/ppermute | solution.py:451
  44.1 2.0 %collective-permute-done.5.refs_2_ = bf16[2,64,1024]{2,1,0:T(8,128)(2,1)S(1)} collective-permute-done((bf16[2,64,1024]{2,1,0:T(8,128)(2,1)S(1)}, bf16[2,64,1024]{2,1,0:T(8,128)(2,1)S(1)}, u32[]{:S(2)}, u32[]{:S(2)}) %collective-permute-start.5) | collective-permute-done | bytes 262176 | tf_op jit(solution)/shard_map/ppermute | solution.py:457
  46.2 2.5 %collective-permute-start.8 = (bf16[257,1408]{1,0:T(8,128)(2,1)S(1)}, bf16[257,1408]{1,0:T(8,128)(2,1)}, u32[]{:S(2)}, u32[]{:S(2)}) collective-permute-start(bf16[257,1408]{1,0:T(8,128)(2,1)S(1)} %bitcast.81), channel_id=1, source_target_pairs={{0,4},{1,5},{2,6},{3,7},{4,0},{5,1},{6,2},{7,3},{8,12},{9,13},{10,... | collective-permute-start | bytes 2171144 | tf_op jit(solution)/shard_map/ppermute | solution.py:457
  49.4 5.2 %gather_units.1 = (bf16[8,64,1024]{2,1,0:T(8,128)(2,1)}, bf16[8,64,1024]{2,1,0:T(8,128)(2,1)}, bf16[16,64,1024]{2,1,0:T(8,128)(2,1)}, f32[8,64,1]{2,1,0:T(8,128)...) custom-call(s32[9]{0:T(128)} %stack.74.where_ref, bf16[2,64,1024]{2,1,0:T(8,128)(2,1)} %copy-done.5, ...), custom_call_target="tpu_custom_call" | custom-call | flops 6291456 | bytes 9437184 | tf_op jit(solution)/shard_map/gather_units/pallas_call | solution.py:245
  54.6 3.3 %fusion.13 = (f32[1024]{0:T(1024)S(1)}, f32[512]{0:T(512)S(1)}, f32[512,1024]{1,0:T(8,128)S(1)}) fusion(bf16[512,1024]{1,0:T(8,128)(2,1)} %bitcast.88, bf16[1024,1024]{1,0:T(8,128)(2,1)} %bitcast.72, f32[]{:T(128)} %bitcast.68), kind=kOutput, calls=%fused_computation.50 | convolution fusion | flops 1075313152 | bytes 5249028 | tf_op jit(solution)/shard_map/dot_general | solution.py:28
  59.3 5.9 %all-to-all-start = ((f32[8,2,512]{2,1,0:T(2,128)}), f32[8,2,512]{2,1,0:T(2,128)S(1)}, u32[]{:S(2)}, u32[]{:S(2)}) async-start(f32[8,2,512]{2,1,0:T(2,128)} %broadcast_in_dim.24), calls=%async_computation | async-start | bytes 65536 | tf_op jit(solution)/shard_map/all_to_all | solution.py:34
  65.2 7.4 %all-to-all-done = f32[8,2,512]{2,1,0:T(2,128)S(1)} async-done(((f32[8,2,512]{2,1,0:T(2,128)}), f32[8,2,512]{2,1,0:T(2,128)S(1)}, u32[]{:S(2)}, u32[]{:S(2)}) %all-to-all-start) | async-done | bytes 32800 | tf_op jit(solution)/shard_map/all_to_all | solution.py:34
  73.2 2.7 %collective-permute-start.9 = (bf16[257,1408]{1,0:T(8,128)(2,1)}, bf16[257,1408]{1,0:T(8,128)(2,1)}, u32[]{:S(2)}, u32[]{:S(2)}) collective-permute-start(bf16[257,1408]{1,0:T(8,128)(2,1)} %collective-permute-done.7.refs_3_), channel_id=1, source_target_pairs={{0,6},{1,7},{2,0},{3,1},{4,2},{5,3},{6,4},{7,5},{8,14},{9,15},{10,... | collective-permute-start | bytes 2171144 | tf_op jit(solution)/shard_map/ppermute | solution.py:457
  76.6 4.9 %all-to-all-start.1 = ((f32[16,2,1024]{2,1,0:T(2,128)}), f32[16,2,1024]{2,1,0:T(2,128)S(1)}, u32[]{:S(2)}, u32[]{:S(2)}) async-start(f32[16,2,1024]{2,1,0:T(2,128)} %broadcast_in_dim.25), calls=%async_computation.1 | async-start | bytes 262144 | tf_op jit(solution)/shard_map/all_to_all | solution.py:34
  81.9 5.3 %all-to-all-done.1 = f32[16,2,1024]{2,1,0:T(2,128)S(1)} async-done(((f32[16,2,1024]{2,1,0:T(2,128)}), f32[16,2,1024]{2,1,0:T(2,128)S(1)}, u32[]{:S(2)}, u32[]{:S(2)}) %all-to-all-start.1) | async-done | bytes 131104 | tf_op jit(solution)/shard_map/all_to_all | solution.py:34
  87.2 3.9 %collective-permute-done.10.refs_2_ = bf16[257,1408]{1,0:T(8,128)(2,1)} collective-permute-done((bf16[257,1408]{1,0:T(8,128)(2,1)}, bf16[257,1408]{1,0:T(8,128)(2,1)}, u32[]{:S(2)}, u32[]{:S(2)}) %collective-permute-start.10) | collective-permute-done | bytes 723744 | tf_op jit(solution)/shard_map/ppermute | solution.py:457
  91.4 1.9 subtract_convert_fusion.dlogit_ref
  93.3 7.6 %directions.1 = (bf16[8,64,1024]{2,1,0:T(8,128)(2,1)}, f32[16,64,1024]{2,1,0:T(8,128)}) custom-call(bf16[512,1024]{1,0:T(8,128)(2,1)} %subtract_convert_fusion.dlogit_ref, f32[8,64,1]{2,1,0:T(8,128)} %get-tuple-element.106.inv_img, f32[16,64,1]{2,1,0:T(8,128)} %get-tuple-element.107.inv_txt, bf16[512,1024]{1,0:T(8,128)(2,1)} %bitcast.89, ...), custom_call_target="tpu_custom_call" | custom-call | flops 2147483648 | bytes 10485760 | tf_op jit(solution)/shard_map/directions/pallas_call | solution.py:326
  101.0 0.8 collective-permute-start.11
  102.5 0.9 slice.62
  104.6 6.1 %all-to-all-start.2 = ((f32[8,8,1024]{2,1,0:T(8,128)}), f32[8,8,1024]{2,1,0:T(8,128)S(1)}, u32[]{:S(2)}, u32[]{:S(2)}) async-start(f32[8,8,1024]{2,1,0:T(8,128)} %broadcast_in_dim.28), calls=%async_computation.2 | async-start | bytes 524288 | tf_op jit(solution)/shard_map/all_to_all | solution.py:34
  110.7 9.1 %encode.2 = (bf16[1408,1024]{1,0:T(8,128)(2,1)}, bf16[4,1,1408]{2,1,0:T(2,128)(2,1)}, bf16[4,256,768]{2,1,0:T(8,128)(2,1)}, f32[4,1,768]{2,1,0:T(1,128)}, f32[4,1,768]{2,1,0:T(1,128)}) custom-call(bf16[257,1408]{1,0:T(8,128)(2,1)} %bitcast.79, bf16[257,1408]{1,0:T(8,128)(2,1)} %copy-done.7, bf16[257,1408]{1,0:T(8,128)(2,1)} %copy-done.6, ...), custom_call_target="tpu_custom_call" | custom-call | flops 2223243264 | bytes 8947712 | tf_op jit(solution)/shard_map/encode/pallas_call | solution.py:98
  119.8 1.3 collective-permute-done.11.refs_3_
  121.0 9.0 %encode.3 = (bf16[1408,1024]{1,0:T(8,128)(2,1)}, bf16[4,1,1408]{2,1,0:T(2,128)(2,1)}, bf16[4,256,768]{2,1,0:T(8,128)(2,1)}, f32[4,1,768]{2,1,0:T(1,128)}, f32[4,1,768]{2,1,0:T(1,128)}) custom-call(bf16[257,1408]{1,0:T(8,128)(2,1)} %collective-permute-done.8.refs_0_, bf16[257,1408]{1,0:T(8,128)(2,1)} %collective-permute-done.9.refs_1_, ...), custom_call_target="tpu_custom_call" | custom-call | flops 2223243264 | bytes 8947712 | tf_op jit(solution)/shard_map/encode/pallas_call | solution.py:98
  130.7 5.9 %head.1 = (bf16[16,8,2176]{2,1,0:T(8,128)(2,1)}, f32[8,1,768]{2,1,0:T(1,128)}) custom-call(s32[9]{0:T(128)} %concatenate.10.spots_ref, f32[1]{0:T(128)} %copy.30.temper_ref, f32[8,8,1024]{2,1,0:T(8,128)} %copy-done.3, f32[8,1024]{1,0:T(8,128)} %get-tuple-element.120.raw_ref, f32[1,1408]{1,0:T(1,128)} %div.21.mean_ref, ...), custom_call_target="tpu_custom_call" | custom-call | flops 80740352 | bytes 5046272 | tf_op jit(solution)/shard_map/head/pallas_call | solution.py:405
  136.6 5.0 %all-to-all-start.3 = ((bf16[16,8,2176]{2,1,0:T(8,128)(2,1)}), bf16[16,8,2176]{2,1,0:T(8,128)(2,1)S(1)}, u32[]{:S(2)}, u32[]{:S(2)}) async-start(bf16[16,8,2176]{2,1,0:T(8,128)(2,1)} %get-tuple-element.126), calls=%async_computation.3 | async-start | bytes 1114112 | tf_op jit(solution)/shard_map/all_to_all | solution.py:551
  141.7 2.4 %collective-permute-start.14 = (bf16[2,64,1024]{2,1,0:T(8,128)(2,1)S(1)}, bf16[2,64,1024]{2,1,0:T(8,128)(2,1)S(1)}, u32[]{:S(2)}, u32[]{:S(2)}) collective-permute-start(bf16[2,64,1024]{2,1,0:T(8,128)(2,1)S(1)} %get-tuple-element.145), channel_id=1, source_target_pairs={{0,4},{1,5},{2,6},{3,7},{4,0},{5,1},{6,2},{7,3},{8,12},{9,13},{10,... | collective-permute-start | bytes 786440 | tf_op jit(solution)/shard_map/ppermute | solution.py:457
  144.1 1.2 collective-permute-start.13
  145.3 2.0 %collective-permute-start.12 = (bf16[2,64,1024]{2,1,0:T(8,128)(2,1)S(1)}, bf16[2,64,1024]{2,1,0:T(8,128)(2,1)S(1)}, u32[]{:S(2)}, u32[]{:S(2)}) collective-permute-start(bf16[2,64,1024]{2,1,0:T(8,128)(2,1)S(1)} %get-tuple-element.147), channel_id=1, source_target_pairs={{0,6},{1,7},{2,0},{3,1},{4,2},{5,3},{6,4},{7,5},{8,14},{9,15},{10,... | collective-permute-start | bytes 786440 | tf_op jit(solution)/shard_map/ppermute | solution.py:457
  147.3 10.9 %weigh.1 = (f32[8,88,768]{2,1,0:T(8,128)}, bf16[8,88,768]{2,1,0:T(8,128)(2,1)}) custom-call(s32[1]{0:T(128)} %bitcast.1.core_ref, s32[8]{0:T(128)} %stack.78.order_ref, bf16[1408,1024]{1,0:T(8,128)(2,1)} %get-tuple-element.110.refs_0_, bf16[4,1,1408]{2,1,0:T(2,128)(2,1)} %get-tuple-element.111.refs_1_, bf16[4,256,768]{2,1,0:T(8,128)(2,1)} %get-tuple-element.112.refs_2_, ...), custom_call_target="tpu_custom_call" | custom-call | flops 4429185024 | bytes 12058624 | tf_op jit(solution)/shard_map/weigh/pallas_call | solution.py:178
  159.2 0.9 fusion.3
  160.2 1.3 convert_add_fusion
  162.0 1.3 add_convert_fusion
  163.3 5.7 %all-to-all-start.4 = ((bf16[8,88,768]{2,1,0:T(8,128)(2,1)}), bf16[8,88,768]{2,1,0:T(8,128)(2,1)S(1)}, u32[]{:S(2)}, u32[]{:S(2)}) async-start(bf16[8,88,768]{2,1,0:T(8,128)(2,1)} %add_convert_fusion), calls=%async_computation.4 | async-start | bytes 2162688 | tf_op jit(solution)/shard_map/all_to_all | solution.py:574
  169.0 1.7 collective-permute-start.18
  170.7 3.0 %collective-permute-start.16 = (bf16[64,1024]{1,0:T(8,128)(2,1)S(1)}, bf16[64,1024]{1,0:T(8,128)(2,1)S(1)}, u32[]{:S(2)}, u32[]{:S(2)}) collective-permute-start(bf16[64,1024]{1,0:T(8,128)(2,1)S(1)} %fusion.5), channel_id=1, source_target_pairs={{0,65},{1,64},{2,67},{3,66},{4,69},{5,68},{6,71},{7,70},{8,73},{9,... | collective-permute-start | bytes 393224 | tf_op jit(solution)/shard_map/ppermute | solution.py:451
  173.8 0.8 collective-permute-done.18
  174.6 3.7 %collective-permute-start.19 = (f32[128,88]{1,0:T(8,128)S(1)}, f32[128,88]{1,0:T(8,128)S(1)}, u32[]{:S(2)}, u32[]{:S(2)}) collective-permute-start(f32[128,88]{1,0:T(8,128)S(1)} %pad_maximum_fusion.2), channel_id=1, source_target_pairs={{0,1},{1,0},{2,3},{3,2},{4,5},{5,4},{6,7},{7,6},{8,9},{9,8},{10,11... | collective-permute-start | bytes 135176 | tf_op jit(solution)/shard_map/ppermute | solution.py:570
  179.1 7.7 %collective-permute-done.19 = f32[128,88]{1,0:T(8,128)S(1)} collective-permute-done((f32[128,88]{1,0:T(8,128)S(1)}, f32[128,88]{1,0:T(8,128)S(1)}, u32[]{:S(2)}, u32[]{:S(2)}) %collective-permute-start.19) | collective-permute-done | bytes 45088 | tf_op jit(solution)/shard_map/ppermute | solution.py:570
  186.8 1.0 fusion
  187.8 0.8 convert_reduce_fusion
  188.6 1.7 broadcast_multiply_fusion
  (105 shorter events, 12.0 us)
Async XLA Ops:
  7.2 32.9 %copy-start.1 = (bf16[1,257,1408]{2,1,0:T(8,128)(2,1)S(1)}, bf16[1,257,1408]{2,1,0:T(8,128)(2,1)}, u32[]{:S(2)}) copy-start(bf16[1,257,1408]{2,1,0:T(8,128)(2,1)} %param.13) | copy-start | bytes 2171140
  7.2 39.0 %all-gather.3.cloned.1.call-start = ((), (), s32[]{:S(2)}) async-start(), calls=%async_computation.6 | async-start | bytes 2228224 | tf_op jit(solution)/shard_map/all_gather | solution.py:462
  7.9 102.8 %all-gather.5.cloned.1.call-start = ((), (), s32[]{:S(2)}) async-start(), calls=%async_computation.7 | async-start | bytes 7659520 | tf_op jit(solution)/shard_map/all_gather | solution.py:463
  9.9 19.8 %collective-permute-start.3 = (bf16[257,1408]{1,0:T(8,128)(2,1)}, bf16[257,1408]{1,0:T(8,128)(2,1)S(1)}, u32[]{:S(2)}, u32[]{:S(2)}) collective-permute-start(bf16[257,1408]{1,0:T(8,128)(2,1)} %bitcast.77), channel_id=1, source_target_pairs={{0,2},{1,3},{2,4},{3,5},{4,6},{5,7},{6,0},{7,1},{8,10},{9,11},{10,... | collective-permute-start | bytes 2171144 | tf_op jit(solution)/shard_map/ppermute | solution.py:457
  11.5 18.3 %collective-permute-start.2 = (bf16[257,1408]{1,0:T(8,128)(2,1)}, bf16[257,1408]{1,0:T(8,128)(2,1)S(1)}, u32[]{:S(2)}, u32[]{:S(2)}) collective-permute-start(bf16[257,1408]{1,0:T(8,128)(2,1)} %bitcast.78), channel_id=1, source_target_pairs={{0,6},{1,7},{2,0},{3,1},{4,2},{5,3},{6,4},{7,5},{8,14},{9,15},{10,... | collective-permute-start | bytes 2171144 | tf_op jit(solution)/shard_map/ppermute | solution.py:457
  13.2 9.0 %collective-permute-start = (bf16[64,1024]{1,0:T(8,128)(2,1)}, bf16[64,1024]{1,0:T(8,128)(2,1)S(1)}, u32[]{:S(2)}, u32[]{:S(2)}) collective-permute-start(bf16[64,1024]{1,0:T(8,128)(2,1)} %param.9), channel_id=1, source_target_pairs={{0,65},{1,64},{2,67},{3,66},{4,69},{5,68},{6,71},{7,70},{8,73},{9,... | collective-permute-start | bytes 393224 | tf_op jit(solution)/shard_map/ppermute | solution.py:451
  17.2 5.0 %collective-permute-start.1 = (s32[512]{0:T(512)}, s32[512]{0:T(512)S(1)}, u32[]{:S(2)}, u32[]{:S(2)}) collective-permute-start(s32[512]{0:T(512)} %param.11), channel_id=1, source_target_pairs={{0,65},{1,64},{2,67},{3,66},{4,69},{5,68},{6,71},{7,70},{8,73},{9,... | collective-permute-start | bytes 6152 | tf_op jit(solution)/shard_map/ppermute | solution.py:451
  29.7 0.9 copy-start.6
  29.7 1.1 copy-start.7
  31.8 17.6 %copy-start.5 = (bf16[2,64,1024]{2,1,0:T(8,128)(2,1)}, bf16[2,64,1024]{2,1,0:T(8,128)(2,1)S(1)}, u32[]{:S(2)}) copy-start(bf16[2,64,1024]{2,1,0:T(8,128)(2,1)S(1)} %pad_maximum_fusion.1.refs_0_) | copy-start | bytes 786436
  31.8 12.3 %collective-permute-start.6 = (bf16[2,64,1024]{2,1,0:T(8,128)(2,1)S(1)}, bf16[2,64,1024]{2,1,0:T(8,128)(2,1)S(1)}, u32[]{:S(2)}, u32[]{:S(2)}) collective-permute-start(bf16[2,64,1024]{2,1,0:T(8,128)(2,1)S(1)} %pad_maximum_fusion.1.refs_0_), channel_id=1, source_target_pairs={{0,4},{1,5},{2,6},{3,7},{4,0},{5,1},{6,2},{7,3},{8,12},{9,13},{10,... | collective-permute-start | bytes 786440 | tf_op jit(solution)/shard_map/ppermute | solution.py:457
  34.4 11.8 %collective-permute-start.5 = (bf16[2,64,1024]{2,1,0:T(8,128)(2,1)S(1)}, bf16[2,64,1024]{2,1,0:T(8,128)(2,1)S(1)}, u32[]{:S(2)}, u32[]{:S(2)}) collective-permute-start(bf16[2,64,1024]{2,1,0:T(8,128)(2,1)S(1)} %pad_maximum_fusion.1.refs_0_), channel_id=1, source_target_pairs={{0,2},{1,3},{2,4},{3,5},{4,6},{5,7},{6,0},{7,1},{8,10},{9,11},{10,... | collective-permute-start | bytes 786440 | tf_op jit(solution)/shard_map/ppermute | solution.py:457
  35.5 10.7 %collective-permute-start.4 = (bf16[2,64,1024]{2,1,0:T(8,128)(2,1)S(1)}, bf16[2,64,1024]{2,1,0:T(8,128)(2,1)S(1)}, u32[]{:S(2)}, u32[]{:S(2)}) collective-permute-start(bf16[2,64,1024]{2,1,0:T(8,128)(2,1)S(1)} %pad_maximum_fusion.1.refs_0_), channel_id=1, source_target_pairs={{0,6},{1,7},{2,0},{3,1},{4,2},{5,3},{6,4},{7,5},{8,14},{9,15},{10,... | collective-permute-start | bytes 786440 | tf_op jit(solution)/shard_map/ppermute | solution.py:457
  40.1 25.1 %collective-permute-start.7 = (bf16[257,1408]{1,0:T(8,128)(2,1)S(1)}, bf16[257,1408]{1,0:T(8,128)(2,1)}, u32[]{:S(2)}, u32[]{:S(2)}) collective-permute-start(bf16[257,1408]{1,0:T(8,128)(2,1)S(1)} %bitcast.80), channel_id=1, source_target_pairs={{0,65},{1,64},{2,67},{3,66},{4,69},{5,68},{6,71},{7,70},{8,73},{9,... | collective-permute-start | bytes 2171144 | tf_op jit(solution)/shard_map/ppermute | solution.py:451
  44.1 5.3 %copy-start.13 = (bf16[2,64,1024]{2,1,0:T(8,128)(2,1)}, bf16[2,64,1024]{2,1,0:T(8,128)(2,1)S(1)}, u32[]{:S(2)}) copy-start(bf16[2,64,1024]{2,1,0:T(8,128)(2,1)S(1)} %collective-permute-done.6.refs_3_) | copy-start | bytes 786436
  46.2 3.2 %copy-start.14 = (bf16[2,64,1024]{2,1,0:T(8,128)(2,1)}, bf16[2,64,1024]{2,1,0:T(8,128)(2,1)S(1)}, u32[]{:S(2)}) copy-start(bf16[2,64,1024]{2,1,0:T(8,128)(2,1)S(1)} %collective-permute-done.5.refs_2_) | copy-start | bytes 786436
  46.2 3.2 %copy-start.15 = (bf16[2,64,1024]{2,1,0:T(8,128)(2,1)}, bf16[2,64,1024]{2,1,0:T(8,128)(2,1)S(1)}, u32[]{:S(2)}) copy-start(bf16[2,64,1024]{2,1,0:T(8,128)(2,1)S(1)} %collective-permute-done.4.refs_1_) | copy-start | bytes 786436
  46.2 26.4 %collective-permute-start.8 = (bf16[257,1408]{1,0:T(8,128)(2,1)S(1)}, bf16[257,1408]{1,0:T(8,128)(2,1)}, u32[]{:S(2)}, u32[]{:S(2)}) collective-permute-start(bf16[257,1408]{1,0:T(8,128)(2,1)S(1)} %bitcast.81), channel_id=1, source_target_pairs={{0,4},{1,5},{2,6},{3,7},{4,0},{5,1},{6,2},{7,3},{8,12},{9,13},{10,... | collective-permute-start | bytes 2171144 | tf_op jit(solution)/shard_map/ppermute | solution.py:457
  57.9 24.0 %copy-start.17 = (s32[512]{0:T(512)S(1)}, s32[512]{0:T(512)}, u32[]{:S(2)}) copy-start(s32[512]{0:T(512)} %param.11) | copy-start | bytes 6148
  59.3 13.3 %all-to-all-start = ((f32[8,2,512]{2,1,0:T(2,128)}), f32[8,2,512]{2,1,0:T(2,128)S(1)}, u32[]{:S(2)}, u32[]{:S(2)}) async-start(f32[8,2,512]{2,1,0:T(2,128)} %broadcast_in_dim.24), calls=%async_computation | async-start | bytes 65536 | tf_op jit(solution)/shard_map/all_to_all | solution.py:34
  72.6 18.5 %collective-permute-start.10 = (bf16[257,1408]{1,0:T(8,128)(2,1)}, bf16[257,1408]{1,0:T(8,128)(2,1)}, u32[]{:S(2)}, u32[]{:S(2)}) collective-permute-start(bf16[257,1408]{1,0:T(8,128)(2,1)} %collective-permute-done.7.refs_3_), channel_id=1, source_target_pairs={{0,2},{1,3},{2,4},{3,5},{4,6},{5,7},{6,0},{7,1},{8,10},{9,11},{10,... | collective-permute-start | bytes 2171144 | tf_op jit(solution)/shard_map/ppermute | solution.py:457
  73.2 17.9 %collective-permute-start.9 = (bf16[257,1408]{1,0:T(8,128)(2,1)}, bf16[257,1408]{1,0:T(8,128)(2,1)}, u32[]{:S(2)}, u32[]{:S(2)}) collective-permute-start(bf16[257,1408]{1,0:T(8,128)(2,1)} %collective-permute-done.7.refs_3_), channel_id=1, source_target_pairs={{0,6},{1,7},{2,0},{3,1},{4,2},{5,3},{6,4},{7,5},{8,14},{9,15},{10,... | collective-permute-start | bytes 2171144 | tf_op jit(solution)/shard_map/ppermute | solution.py:457
  76.6 10.7 %all-to-all-start.1 = ((f32[16,2,1024]{2,1,0:T(2,128)}), f32[16,2,1024]{2,1,0:T(2,128)S(1)}, u32[]{:S(2)}, u32[]{:S(2)}) async-start(f32[16,2,1024]{2,1,0:T(2,128)} %broadcast_in_dim.25), calls=%async_computation.1 | async-start | bytes 262144 | tf_op jit(solution)/shard_map/all_to_all | solution.py:34
  81.5 106.3 %reduce-scatter.2.cloned.1.call-start = ((), (), s32[]{:S(2)}) async-start(), calls=%async_computation.8 | async-start | bytes 4456448 | tf_op jit(solution)/shard_map/reduce_scatter | solution.py:526
  100.9 0.9 copy-start.16
  100.9 1.5 copy-start.8
  100.9 2.5 %copy-start = (bf16[16,64,1024]{2,1,0:T(8,128)(2,1)S(1)}, bf16[16,64,1024]{2,1,0:T(8,128)(2,1)}, u32[]{:S(2)}) copy-start(bf16[16,64,1024]{2,1,0:T(8,128)(2,1)} %get-tuple-element.81) | copy-start | bytes 6291460
  101.0 20.1 %collective-permute-start.11 = (bf16[257,1408]{1,0:T(8,128)(2,1)}, bf16[257,1408]{1,0:T(8,128)(2,1)}, u32[]{:S(2)}, u32[]{:S(2)}) collective-permute-start(bf16[257,1408]{1,0:T(8,128)(2,1)} %collective-permute-done.8.refs_0_), channel_id=1, source_target_pairs={{0,65},{1,64},{2,67},{3,66},{4,69},{5,68},{6,71},{7,70},{8,73},{9,... | collective-permute-start | bytes 2171144 | tf_op jit(solution)/shard_map/ppermute | solution.py:451
  104.6 25.4 %all-to-all-start.2 = ((f32[8,8,1024]{2,1,0:T(8,128)}), f32[8,8,1024]{2,1,0:T(8,128)S(1)}, u32[]{:S(2)}, u32[]{:S(2)}) async-start(f32[8,8,1024]{2,1,0:T(8,128)} %broadcast_in_dim.28), calls=%async_computation.2 | async-start | bytes 524288 | tf_op jit(solution)/shard_map/all_to_all | solution.py:34
  130.0 0.7 copy-start.3
  130.7 10.9 %copy-start.4 = (bf16[8,64,1024]{2,1,0:T(8,128)(2,1)S(1)}, bf16[8,64,1024]{2,1,0:T(8,128)(2,1)}, u32[]{:S(2)}) copy-start(bf16[8,64,1024]{2,1,0:T(8,128)(2,1)} %get-tuple-element.127) | copy-start | bytes 3145732
  136.6 21.6 %all-to-all-start.3 = ((bf16[16,8,2176]{2,1,0:T(8,128)(2,1)}), bf16[16,8,2176]{2,1,0:T(8,128)(2,1)S(1)}, u32[]{:S(2)}, u32[]{:S(2)}) async-start(bf16[16,8,2176]{2,1,0:T(8,128)(2,1)} %get-tuple-element.126), calls=%async_computation.3 | async-start | bytes 1114112 | tf_op jit(solution)/shard_map/all_to_all | solution.py:551
  141.7 16.5 %collective-permute-start.14 = (bf16[2,64,1024]{2,1,0:T(8,128)(2,1)S(1)}, bf16[2,64,1024]{2,1,0:T(8,128)(2,1)S(1)}, u32[]{:S(2)}, u32[]{:S(2)}) collective-permute-start(bf16[2,64,1024]{2,1,0:T(8,128)(2,1)S(1)} %get-tuple-element.145), channel_id=1, source_target_pairs={{0,4},{1,5},{2,6},{3,7},{4,0},{5,1},{6,2},{7,3},{8,12},{9,13},{10,... | collective-permute-start | bytes 786440 | tf_op jit(solution)/shard_map/ppermute | solution.py:457
  144.1 14.1 %collective-permute-start.13 = (bf16[2,64,1024]{2,1,0:T(8,128)(2,1)S(1)}, bf16[2,64,1024]{2,1,0:T(8,128)(2,1)S(1)}, u32[]{:S(2)}, u32[]{:S(2)}) collective-permute-start(bf16[2,64,1024]{2,1,0:T(8,128)(2,1)S(1)} %get-tuple-element.146), channel_id=1, source_target_pairs={{0,2},{1,3},{2,4},{3,5},{4,6},{5,7},{6,0},{7,1},{8,10},{9,11},{10,... | collective-permute-start | bytes 786440 | tf_op jit(solution)/shard_map/ppermute | solution.py:457
  145.3 12.9 %collective-permute-start.12 = (bf16[2,64,1024]{2,1,0:T(8,128)(2,1)S(1)}, bf16[2,64,1024]{2,1,0:T(8,128)(2,1)S(1)}, u32[]{:S(2)}, u32[]{:S(2)}) collective-permute-start(bf16[2,64,1024]{2,1,0:T(8,128)(2,1)S(1)} %get-tuple-element.147), channel_id=1, source_target_pairs={{0,6},{1,7},{2,0},{3,1},{4,2},{5,3},{6,4},{7,5},{8,14},{9,15},{10,... | collective-permute-start | bytes 786440 | tf_op jit(solution)/shard_map/ppermute | solution.py:457
  147.3 11.8 %copy-start.9 = (bf16[64,1024]{1,0:T(8,128)(2,1)S(1)}, bf16[64,1024]{1,0:T(8,128)(2,1)}, u32[]{:S(2)}) copy-start(bf16[64,1024]{1,0:T(8,128)(2,1)} %param.9) | copy-start | bytes 393220
  158.2 1.1 copy-start.10
  158.2 0.8 copy-start.11
  158.2 0.8 copy-start.12
  159.1 2.9 %collective-permute-start.15 = (bf16[8,88,768]{2,1,0:T(8,128)(2,1)}, bf16[8,88,768]{2,1,0:T(8,128)(2,1)S(1)}, u32[]{:S(2)}, u32[]{:S(2)}) collective-permute-start(bf16[8,88,768]{2,1,0:T(8,128)(2,1)} %get-tuple-element.128), channel_id=1, source_target_pairs={{0,8},{8,0},{16,24},{24,16},{32,40},{40,32},{48,56},{56,48},{64,72... | collective-permute-start | bytes 3244040 | tf_op jit(solution)/shard_map/ppermute | solution.py:553
  159.1 2.9 %copy-start.2 = (f32[8,88,768]{2,1,0:T(8,128)S(1)}, f32[8,88,768]{2,1,0:T(8,128)}, u32[]{:S(2)}) copy-start(f32[8,88,768]{2,1,0:T(8,128)} %get-tuple-element.134) | copy-start | bytes 6488068
  162.0 7.0 %collective-permute-start.17 = (f32[128,88]{1,0:T(8,128)S(1)}, f32[128,88]{1,0:T(8,128)S(1)}, u32[]{:S(2)}, u32[]{:S(2)}) collective-permute-start(f32[128,88]{1,0:T(8,128)S(1)} %convert_add_fusion.1), channel_id=1, source_target_pairs={{0,2},{1,3},{2,0},{3,1},{4,6},{5,7},{6,4},{7,5},{8,10},{9,11},{10,... | collective-permute-start | bytes 135176 | tf_op jit(solution)/shard_map/ppermute | solution.py:567
  163.3 24.5 %all-to-all-start.4 = ((bf16[8,88,768]{2,1,0:T(8,128)(2,1)}), bf16[8,88,768]{2,1,0:T(8,128)(2,1)S(1)}, u32[]{:S(2)}, u32[]{:S(2)}) async-start(bf16[8,88,768]{2,1,0:T(8,128)(2,1)} %add_convert_fusion), calls=%async_computation.4 | async-start | bytes 2162688 | tf_op jit(solution)/shard_map/all_to_all | solution.py:574
  169.0 5.6 %collective-permute-start.18 = (f32[128,88]{1,0:T(8,128)S(1)}, f32[128,88]{1,0:T(8,128)S(1)}, u32[]{:S(2)}, u32[]{:S(2)}) collective-permute-start(f32[128,88]{1,0:T(8,128)S(1)} %add.198), channel_id=1, source_target_pairs={{0,6},{1,7},{2,4},{3,5},{4,2},{5,3},{6,0},{7,1},{8,14},{9,15},{10,... | collective-permute-start | bytes 135176 | tf_op jit(solution)/shard_map/ppermute | solution.py:567
  170.7 7.6 %collective-permute-start.16 = (bf16[64,1024]{1,0:T(8,128)(2,1)S(1)}, bf16[64,1024]{1,0:T(8,128)(2,1)S(1)}, u32[]{:S(2)}, u32[]{:S(2)}) collective-permute-start(bf16[64,1024]{1,0:T(8,128)(2,1)S(1)} %fusion.5), channel_id=1, source_target_pairs={{0,65},{1,64},{2,67},{3,66},{4,69},{5,68},{6,71},{7,70},{8,73},{9,... | collective-permute-start | bytes 393224 | tf_op jit(solution)/shard_map/ppermute | solution.py:451
  174.6 12.2 %collective-permute-start.19 = (f32[128,88]{1,0:T(8,128)S(1)}, f32[128,88]{1,0:T(8,128)S(1)}, u32[]{:S(2)}, u32[]{:S(2)}) collective-permute-start(f32[128,88]{1,0:T(8,128)S(1)} %pad_maximum_fusion.2), channel_id=1, source_target_pairs={{0,1},{1,0},{2,3},{3,2},{4,5},{5,4},{6,7},{7,6},{8,9},{9,8},{10,11... | collective-permute-start | bytes 135176 | tf_op jit(solution)/shard_map/ppermute | solution.py:570
Sparse Core Ops, SparseCore 0:
  9.7 36.0 all-gather.2
  47.5 48.0 all-gather.4
  101.1 66.0 reduce-scatter.1
